TPU v7x, 32 devices: a whole 2x2x4 slice. The times are simulated.
32 devices in a mesh: row: 4 (over y, x), col: 8 (over z, core).
Axes of the slice: x: 2, y: 2, z: 4, core: 2. Of those that a mesh axis runs over, the one named last changes fastest.
Arguments:
- inputs: bfloat16 [4, 64, 64, 1280], P(None, 'row', 'col'), may hold values from -6 to 6
- cotangent: bfloat16 [4, 64, 64, 1280], P(None, 'row', 'col'), may hold values from -6 to 6
- w_in: bfloat16 [1474560], P(('row', 'col')), may hold values from -0.0546875 to 0.0546875
- w_out: bfloat16 [1474560], P(('row', 'col')), may hold values from -0.1875 to 0.1875
Outputs:
- input_grad: bfloat16 [4, 64, 64, 1280], P(None, 'row', 'col')
All inputs are finite; a program needn't handle non-finite values.
Results may differ from a plain program's by a relative error of at most 0.0032.
Values may be sent and summed in bfloat16 or wider, within the bound.
No kernel may reach another device: no remote copies, remote signals or barrier semaphores. Data moves between devices by JAX's collectives and lax.ppermute only.
A program may use at most 64 MiB of HBM per device.

v0:
```python
import jax
import jax.numpy as jnp
from jax import lax
from jax.sharding import PartitionSpec as P

C = 1280
MID = 128


def padded_2(block, sides, width):
    for axis, dim in sides:
        count = lax.axis_size(axis)
        forward = [(i, i + 1) for i in range(count - 1)]
        backward = [(target, source) for source, target in forward]
        low = lax.ppermute(
            lax.slice_in_dim(block, block.shape[dim] - width, None, axis=dim), axis, forward
        )
        high = lax.ppermute(lax.slice_in_dim(block, 0, width, axis=dim), axis, backward)
        block = jnp.concatenate([low, block, high], axis=dim)
    return block


def convolve(padded, kernel):
    return lax.conv_general_dilated(
        padded,
        kernel,
        (1, 1),
        "VALID",
        dimension_numbers=("NHWC", "HWIO", "NHWC"),
        preferred_element_type=jnp.float32,
    )


def shards(inputs, cotangent, w_in, w_out):
    part_in, part_out = (
        lax.all_gather(w_in, "col", axis=0, tiled=True),
        lax.all_gather(w_out, "col", axis=0, tiled=True),
    )
    full_in, full_out = (
        lax.all_gather(part_in, "row", axis=0, tiled=True),
        lax.all_gather(part_out, "row", axis=0, tiled=True),
    )
    ker_in = full_in.reshape(3, 3, C, MID)
    pad_input = padded_2(inputs, (("row", 1), ("col", 2)), 1)
    pre = convolve(pad_input, ker_in)
    out_back = full_out.reshape(3, 3, MID, C)[::-1, ::-1].transpose(0, 1, 3, 2)
    pad_cotangent = padded_2(cotangent, (("row", 1), ("col", 2)), 1)
    back_mid = convolve(pad_cotangent, out_back)
    sigmoid_pre = jax.nn.sigmoid(pre)
    grad_mid = (back_mid * (sigmoid_pre * (1.0 + pre * (1.0 - sigmoid_pre)))).astype(jnp.bfloat16)
    pad_grad = padded_2(grad_mid, (("row", 1), ("col", 2)), 1)
    in_back = ker_in[::-1, ::-1].transpose(0, 1, 3, 2)
    result = cotangent.astype(jnp.float32) + convolve(pad_grad, in_back)
    return result.astype(jnp.bfloat16)


def solution(mesh):
    return jax.shard_map(
        shards,
        mesh=mesh,
        in_specs=(
            P(None, "row", "col", None),
            P(None, "row", "col", None),
            P(("row", "col")),
            P(("row", "col")),
        ),
        out_specs=P(None, "row", "col", None),
        check_vma=False,
    )
```

profile of v0, /device:TPU:3, one launch (start us, length us, event | category | flops | bytes accessed | tf_op | source)
XLA Modules:
  0.0 158.2 jit_solution(6843183894573307823)
XLA Ops:
  6.5 17.6 %all_gather.14 = bf16[368640]{0:T(1024)(128)(2,1)} all-gather(bf16[46080]{0:T(1024)(128)(2,1)} %param.6), channel_id=1, replica_groups=mesh['row'=4,'col'=8] {'col'}, dimensions={0}, use_global_device_ids=true | all-gather | bytes 829440 | tf_op jit(solution)/shard_map/all_gather | solution.py:36
  24.2 16.7 %all_gather.12 = bf16[368640]{0:T(1024)(128)(2,1)} all-gather(bf16[46080]{0:T(1024)(128)(2,1)} %param.7), channel_id=1, replica_groups=mesh['row'=4,'col'=8] {'col'}, dimensions={0}, use_global_device_ids=true | all-gather | bytes 829440 | tf_op jit(solution)/shard_map/all_gather | solution.py:37
  41.0 3.1 %collective-permute-start.4 = (bf16[4,1,8,1280]{3,0,2,1:T(4,128)(2,1)S(1)}, bf16[4,1,8,1280]{3,0,2,1:T(4,128)(2,1)S(1)}, u32[]{:S(2)}, u32[]{:S(2)}) collective-permute-start(bf16[4,1,8,1280]{3,0,2,1:T(4,128)(2,1)S(1)} %copy.35), channel_id=1, source_target_pairs={{0,8},{8,16},{16,24},{1,9},{9,17},{17,25},{2,10},{10,18},{18,26},{... | collective-permute-start | bytes 245768 | tf_op jit(solution)/shard_map/ppermute | solution.py:15
  44.2 2.2 %collective-permute-start.5 = (bf16[4,1,8,1280]{3,0,2,1:T(4,128)(2,1)S(1)}, bf16[4,1,8,1280]{3,0,2,1:T(4,128)(2,1)S(1)}, u32[]{:S(2)}, u32[]{:S(2)}) collective-permute-start(bf16[4,1,8,1280]{3,0,2,1:T(4,128)(2,1)S(1)} %copy.36), channel_id=1, source_target_pairs={{8,0},{16,8},{24,16},{9,1},{17,9},{25,17},{10,2},{18,10},{26,18},{... | collective-permute-start | bytes 245768 | tf_op jit(solution)/shard_map/ppermute | solution.py:18
  46.4 4.0 %collective-permute-start = (bf16[4,1,8,1280]{3,0,2,1:T(4,128)(2,1)S(1)}, bf16[4,1,8,1280]{3,0,2,1:T(4,128)(2,1)S(1)}, u32[]{:S(2)}, u32[]{:S(2)}) collective-permute-start(bf16[4,1,8,1280]{3,0,2,1:T(4,128)(2,1)S(1)} %copy.33), channel_id=1, source_target_pairs={{0,8},{8,16},{16,24},{1,9},{9,17},{17,25},{2,10},{10,18},{18,26},{... | collective-permute-start | bytes 245768 | tf_op jit(solution)/shard_map/ppermute | solution.py:15
  50.5 1.9 %collective-permute-start.1 = (bf16[4,1,8,1280]{3,0,2,1:T(4,128)(2,1)S(1)}, bf16[4,1,8,1280]{3,0,2,1:T(4,128)(2,1)S(1)}, u32[]{:S(2)}, u32[]{:S(2)}) collective-permute-start(bf16[4,1,8,1280]{3,0,2,1:T(4,128)(2,1)S(1)} %copy.34), channel_id=1, source_target_pairs={{8,0},{16,8},{24,16},{9,1},{17,9},{25,17},{10,2},{18,10},{26,18},{... | collective-permute-start | bytes 245768 | tf_op jit(solution)/shard_map/ppermute | solution.py:18
  52.4 1.1 constant_dynamic-update-slice_fusion.4
  54.0 1.1 constant_dynamic-update-slice_fusion.1
  55.2 5.2 %collective-permute-start.6 = (bf16[4,18,1,1280]{3,0,2,1:T(4,128)(2,1)S(1)}, bf16[4,18,1,1280]{3,0,2,1:T(4,128)(2,1)S(1)}, u32[]{:S(2)}, u32[]{:S(2)}) collective-permute-start(bf16[4,18,1,1280]{3,0,2,1:T(4,128)(2,1)S(1)} %get-tuple-element.5), channel_id=1, source_target_pairs={{0,1},{1,2},{2,3},{3,4},{4,5},{5,6},{6,7},{8,9},{9,10},{10,11},{11... | collective-permute-start | bytes 552968 | tf_op jit(solution)/shard_map/ppermute | solution.py:15
  60.4 1.9 %collective-permute-start.7 = (bf16[4,18,1,1280]{3,0,2,1:T(4,128)(2,1)S(1)}, bf16[4,18,1,1280]{3,0,2,1:T(4,128)(2,1)}, u32[]{:S(2)}, u32[]{:S(2)}) collective-permute-start(bf16[4,18,1,1280]{3,0,2,1:T(4,128)(2,1)S(1)} %get-tuple-element.6), channel_id=1, source_target_pairs={{1,0},{2,1},{3,2},{4,3},{5,4},{6,5},{7,6},{9,8},{10,9},{11,10},{12... | collective-permute-start | bytes 552968 | tf_op jit(solution)/shard_map/ppermute | solution.py:18
  62.6 3.6 %collective-permute-start.2 = (bf16[4,18,1,1280]{3,0,2,1:T(4,128)(2,1)S(1)}, bf16[4,18,1,1280]{3,0,2,1:T(4,128)(2,1)S(1)}, u32[]{:S(2)}, u32[]{:S(2)}) collective-permute-start(bf16[4,18,1,1280]{3,0,2,1:T(4,128)(2,1)S(1)} %get-tuple-element.7), channel_id=1, source_target_pairs={{0,1},{1,2},{2,3},{3,4},{4,5},{5,6},{6,7},{8,9},{9,10},{10,11},{11... | collective-permute-start | bytes 552968 | tf_op jit(solution)/shard_map/ppermute | solution.py:15
  66.2 2.1 %collective-permute-start.3 = (bf16[4,18,1,1280]{3,0,2,1:T(4,128)(2,1)S(1)}, bf16[4,18,1,1280]{3,0,2,1:T(4,128)(2,1)}, u32[]{:S(2)}, u32[]{:S(2)}) collective-permute-start(bf16[4,18,1,1280]{3,0,2,1:T(4,128)(2,1)S(1)} %get-tuple-element.8), channel_id=1, source_target_pairs={{1,0},{2,1},{3,2},{4,3},{5,4},{6,5},{7,6},{9,8},{10,9},{11,10},{12... | collective-permute-start | bytes 552968 | tf_op jit(solution)/shard_map/ppermute | solution.py:18
  69.2 7.9 %fusion.7 = f32[4,16,8,128]{3,0,2,1:T(4,128)} fusion(bf16[3,3,1280,128]{3,2,1,0:T(8,128)(2,1)} %bitcast.4, bf16[4,18,1,1280]{3,0,2,1:T(4,128)(2,1)} %collective-permute-done.7, bf16[4,18,8,1280]{3,0,2,1:T(4,128)(2,1)} %copy-done.2, bf16[4,18,1,1280]{3,0,2,1:T(4,128)(2,1)S(1)} %collective-permute-done.6), kind=kOutput, calls=%fused_computation.8 | convolution fusion | flops 1515479040 | bytes 5054464 | tf_op jit(solution)/shard_map/conv_general_dilated | solution.py:24
  77.1 38.1 %all-gather.3.cloned.1.call-done = bf16[1474560]{0:T(1024)(128)(2,1)} async-done(((bf16[368640]{0:T(1024)(128)(2,1)}), bf16[1474560]{0:T(1024)(128)(2,1)}) %all-gather.3.cloned.1.call-update) | async-done | bytes 2949136 | tf_op jit(solution)/shard_map/all_gather | solution.py:41
  115.2 6.6 %reshape.6 = bf16[3,3,128,1280]{3,2,1,0:T(8,128)(2,1)} reshape(bf16[1474560]{0:T(1024)(128)(2,1)} %all-gather.3.cloned.1.call-done) | data formatting | bytes 5898240 | tf_op jit(solution)/shard_map/reshape | solution.py:46
  121.8 6.9 %fusion.16 = bf16[4,16,8,128]{3,0,2,1:T(4,128)(2,1)S(1)} fusion(bf16[3,3,128,1280]{3,2,1,0:T(8,128)(2,1)} %reshape.6, bf16[4,18,1,1280]{3,0,2,1:T(4,128)(2,1)} %collective-permute-done.3, bf16[4,18,8,1280]{3,0,2,1:T(4,128)(2,1)S(1)} %constant_dynamic-update-slice_fusion, bf16[4,18,1,1280]{3,0,2,1:T(4,128)(2,1)S(1)} %collective-permute-done.2, ...), kind=kOutput, calls=%fused_computation.15 | convolution fusion | flops 1516068864 | bytes 5185536 | tf_op jit(solution)/shard_map/conv_general_dilated | solution.py:24
  128.7 3.1 %collective-permute-start.8 = (bf16[4,1,8,128]{3,0,2,1:T(4,128)(2,1)S(1)}, bf16[4,1,8,128]{3,0,2,1:T(4,128)(2,1)S(1)}, u32[]{:S(2)}, u32[]{:S(2)}) collective-permute-start(bf16[4,1,8,128]{3,0,2,1:T(4,128)(2,1)S(1)} %get-tuple-element.15), channel_id=1, source_target_pairs={{0,8},{8,16},{16,24},{1,9},{9,17},{17,25},{2,10},{10,18},{18,26},{... | collective-permute-start | bytes 24584 | tf_op jit(solution)/shard_map/ppermute | solution.py:15
  131.8 2.2 %collective-permute-start.9 = (bf16[4,1,8,128]{3,0,2,1:T(4,128)(2,1)S(1)}, bf16[4,1,8,128]{3,0,2,1:T(4,128)(2,1)S(1)}, u32[]{:S(2)}, u32[]{:S(2)}) collective-permute-start(bf16[4,1,8,128]{3,0,2,1:T(4,128)(2,1)S(1)} %get-tuple-element.16), channel_id=1, source_target_pairs={{8,0},{16,8},{24,16},{9,1},{17,9},{25,17},{10,2},{18,10},{26,18},{... | collective-permute-start | bytes 24584 | tf_op jit(solution)/shard_map/ppermute | solution.py:18
  134.0 3.1 %collective-permute-done.9 = bf16[4,1,8,128]{3,0,2,1:T(4,128)(2,1)S(1)} collective-permute-done((bf16[4,1,8,128]{3,0,2,1:T(4,128)(2,1)S(1)}, bf16[4,1,8,128]{3,0,2,1:T(4,128)(2,1)S(1)}, u32[]{:S(2)}, u32[]{:S(2)}) %collective-permute-start.9) | collective-permute-done | bytes 8224 | tf_op jit(solution)/shard_map/ppermute | solution.py:18
  137.1 5.1 %collective-permute-start.10 = (bf16[4,18,1,128]{3,0,2,1:T(4,128)(2,1)S(1)}, bf16[4,18,1,128]{3,0,2,1:T(4,128)(2,1)S(1)}, u32[]{:S(2)}, u32[]{:S(2)}) collective-permute-start(bf16[4,18,1,128]{3,0,2,1:T(4,128)(2,1)S(1)} %get-tuple-element.13), channel_id=1, source_target_pairs={{0,1},{1,2},{2,3},{3,4},{4,5},{5,6},{6,7},{8,9},{9,10},{10,11},{11... | collective-permute-start | bytes 55304 | tf_op jit(solution)/shard_map/ppermute | solution.py:15
  142.3 1.9 %collective-permute-start.11 = (bf16[4,18,1,128]{3,0,2,1:T(4,128)(2,1)S(1)}, bf16[4,18,1,128]{3,0,2,1:T(4,128)(2,1)S(1)}, u32[]{:S(2)}, u32[]{:S(2)}) collective-permute-start(bf16[4,18,1,128]{3,0,2,1:T(4,128)(2,1)S(1)} %get-tuple-element.14), channel_id=1, source_target_pairs={{1,0},{2,1},{3,2},{4,3},{5,4},{6,5},{7,6},{9,8},{10,9},{11,10},{12... | collective-permute-start | bytes 55304 | tf_op jit(solution)/shard_map/ppermute | solution.py:18
  144.2 3.1 %collective-permute-done.11 = bf16[4,18,1,128]{3,0,2,1:T(4,128)(2,1)S(1)} collective-permute-done((bf16[4,18,1,128]{3,0,2,1:T(4,128)(2,1)S(1)}, bf16[4,18,1,128]{3,0,2,1:T(4,128)(2,1)S(1)}, u32[]{:S(2)}, u32[]{:S(2)}) %collective-permute-start.11) | collective-permute-done | bytes 18464 | tf_op jit(solution)/shard_map/ppermute | solution.py:18
  147.3 2.5 %fusion.19 = f32[4,16,8,1280]{3,0,2,1:T(4,128)S(1)} fusion(bf16[3,3,1280,128]{3,2,1,0:T(8,128)(2,1)S(1)} %bitcast.5, bf16[4,18,1,128]{3,0,2,1:T(4,128)(2,1)S(1)} %collective-permute-done.11, bf16[4,1,8,128]{3,0,2,1:T(4,128)(2,1)S(1)} %collective-permute-done.9, bf16[4,16,8,128]{3,0,2,1:T(4,128)(2,1)S(1)} %fusion.16, ...), kind=kOutput, calls=%fused_computation.16 | convolution fusion | flops 1510871040 | bytes 5754880 | tf_op jit(solution)/shard_map/conv_general_dilated | solution.py:24
  149.9 1.5 fusion
  (37 shorter events, 1.9 us)
Async XLA Ops:
  6.5 34.4 %copy-start.1 = (bf16[4,16,8,1280]{3,2,1,0:T(8,128)(2,1)S(1)}, bf16[4,16,8,1280]{3,2,1,0:T(8,128)(2,1)}, u32[]{:S(2)}) copy-start(bf16[4,16,8,1280]{3,2,1,0:T(8,128)(2,1)} %param.4) | copy-start | bytes 3932164
  6.5 39.8 %copy-start = (bf16[4,16,8,1280]{3,2,1,0:T(8,128)(2,1)S(1)}, bf16[4,16,8,1280]{3,2,1,0:T(8,128)(2,1)}, u32[]{:S(2)}) copy-start(bf16[4,16,8,1280]{3,2,1,0:T(8,128)(2,1)} %param.5) | copy-start | bytes 3932164
  6.5 62.7 %all-gather.5.cloned.1.call-start = ((), (), s32[]{:S(2)}) async-start(), calls=%async_computation.1 | async-start | bytes 3686400 | tf_op jit(solution)/shard_map/all_gather | solution.py:40
  24.2 91.0 %all-gather.3.cloned.1.call-start = ((), (), s32[]{:S(2)}) async-start(), calls=%async_computation | async-start | bytes 3686400 | tf_op jit(solution)/shard_map/all_gather | solution.py:41
  41.0 11.4 %collective-permute-start.4 = (bf16[4,1,8,1280]{3,0,2,1:T(4,128)(2,1)S(1)}, bf16[4,1,8,1280]{3,0,2,1:T(4,128)(2,1)S(1)}, u32[]{:S(2)}, u32[]{:S(2)}) collective-permute-start(bf16[4,1,8,1280]{3,0,2,1:T(4,128)(2,1)S(1)} %copy.35), channel_id=1, source_target_pairs={{0,8},{8,16},{16,24},{1,9},{9,17},{17,25},{2,10},{10,18},{18,26},{... | collective-permute-start | bytes 245768 | tf_op jit(solution)/shard_map/ppermute | solution.py:15
  44.2 9.7 %collective-permute-start.5 = (bf16[4,1,8,1280]{3,0,2,1:T(4,128)(2,1)S(1)}, bf16[4,1,8,1280]{3,0,2,1:T(4,128)(2,1)S(1)}, u32[]{:S(2)}, u32[]{:S(2)}) collective-permute-start(bf16[4,1,8,1280]{3,0,2,1:T(4,128)(2,1)S(1)} %copy.36), channel_id=1, source_target_pairs={{8,0},{16,8},{24,16},{9,1},{17,9},{25,17},{10,2},{18,10},{26,18},{... | collective-permute-start | bytes 245768 | tf_op jit(solution)/shard_map/ppermute | solution.py:18
  46.4 7.5 %collective-permute-start = (bf16[4,1,8,1280]{3,0,2,1:T(4,128)(2,1)S(1)}, bf16[4,1,8,1280]{3,0,2,1:T(4,128)(2,1)S(1)}, u32[]{:S(2)}, u32[]{:S(2)}) collective-permute-start(bf16[4,1,8,1280]{3,0,2,1:T(4,128)(2,1)S(1)} %copy.33), channel_id=1, source_target_pairs={{0,8},{8,16},{16,24},{1,9},{9,17},{17,25},{2,10},{10,18},{18,26},{... | collective-permute-start | bytes 245768 | tf_op jit(solution)/shard_map/ppermute | solution.py:15
  50.5 11.9 %collective-permute-start.1 = (bf16[4,1,8,1280]{3,0,2,1:T(4,128)(2,1)S(1)}, bf16[4,1,8,1280]{3,0,2,1:T(4,128)(2,1)S(1)}, u32[]{:S(2)}, u32[]{:S(2)}) collective-permute-start(bf16[4,1,8,1280]{3,0,2,1:T(4,128)(2,1)S(1)} %copy.34), channel_id=1, source_target_pairs={{8,0},{16,8},{24,16},{9,1},{17,9},{25,17},{10,2},{18,10},{26,18},{... | collective-permute-start | bytes 245768 | tf_op jit(solution)/shard_map/ppermute | solution.py:18
  54.0 8.6 %copy-start.2 = (bf16[4,18,8,1280]{3,0,2,1:T(4,128)(2,1)}, bf16[4,18,8,1280]{3,0,2,1:T(4,128)(2,1)S(1)}, u32[]{:S(2)}) copy-start(bf16[4,18,8,1280]{3,0,2,1:T(4,128)(2,1)S(1)} %constant_dynamic-update-slice_fusion.3) | copy-start | bytes 4423684
  55.2 13.1 %collective-permute-start.6 = (bf16[4,18,1,1280]{3,0,2,1:T(4,128)(2,1)S(1)}, bf16[4,18,1,1280]{3,0,2,1:T(4,128)(2,1)S(1)}, u32[]{:S(2)}, u32[]{:S(2)}) collective-permute-start(bf16[4,18,1,1280]{3,0,2,1:T(4,128)(2,1)S(1)} %get-tuple-element.5), channel_id=1, source_target_pairs={{0,1},{1,2},{2,3},{3,4},{4,5},{5,6},{6,7},{8,9},{9,10},{10,11},{11... | collective-permute-start | bytes 552968 | tf_op jit(solution)/shard_map/ppermute | solution.py:15
  60.4 7.9 %collective-permute-start.7 = (bf16[4,18,1,1280]{3,0,2,1:T(4,128)(2,1)S(1)}, bf16[4,18,1,1280]{3,0,2,1:T(4,128)(2,1)}, u32[]{:S(2)}, u32[]{:S(2)}) collective-permute-start(bf16[4,18,1,1280]{3,0,2,1:T(4,128)(2,1)S(1)} %get-tuple-element.6), channel_id=1, source_target_pairs={{1,0},{2,1},{3,2},{4,3},{5,4},{6,5},{7,6},{9,8},{10,9},{11,10},{12... | collective-permute-start | bytes 552968 | tf_op jit(solution)/shard_map/ppermute | solution.py:18
  62.6 59.2 %collective-permute-start.2 = (bf16[4,18,1,1280]{3,0,2,1:T(4,128)(2,1)S(1)}, bf16[4,18,1,1280]{3,0,2,1:T(4,128)(2,1)S(1)}, u32[]{:S(2)}, u32[]{:S(2)}) collective-permute-start(bf16[4,18,1,1280]{3,0,2,1:T(4,128)(2,1)S(1)} %get-tuple-element.7), channel_id=1, source_target_pairs={{0,1},{1,2},{2,3},{3,4},{4,5},{5,6},{6,7},{8,9},{9,10},{10,11},{11... | collective-permute-start | bytes 552968 | tf_op jit(solution)/shard_map/ppermute | solution.py:15
  66.2 55.6 %collective-permute-start.3 = (bf16[4,18,1,1280]{3,0,2,1:T(4,128)(2,1)S(1)}, bf16[4,18,1,1280]{3,0,2,1:T(4,128)(2,1)}, u32[]{:S(2)}, u32[]{:S(2)}) collective-permute-start(bf16[4,18,1,1280]{3,0,2,1:T(4,128)(2,1)S(1)} %get-tuple-element.8), channel_id=1, source_target_pairs={{1,0},{2,1},{3,2},{4,3},{5,4},{6,5},{7,6},{9,8},{10,9},{11,10},{12... | collective-permute-start | bytes 552968 | tf_op jit(solution)/shard_map/ppermute | solution.py:18
  121.8 25.6 %copy-start.3 = (bf16[1474560]{0:T(1024)(128)(2,1)S(1)}, bf16[1474560]{0:T(1024)(128)(2,1)}, u32[]{:S(2)}) copy-start(bf16[1474560]{0:T(1024)(128)(2,1)} %all-gather.5.cloned.1.call-done) | copy-start | bytes 8847364
  128.7 5.3 %collective-permute-start.8 = (bf16[4,1,8,128]{3,0,2,1:T(4,128)(2,1)S(1)}, bf16[4,1,8,128]{3,0,2,1:T(4,128)(2,1)S(1)}, u32[]{:S(2)}, u32[]{:S(2)}) collective-permute-start(bf16[4,1,8,128]{3,0,2,1:T(4,128)(2,1)S(1)} %get-tuple-element.15), channel_id=1, source_target_pairs={{0,8},{8,16},{16,24},{1,9},{9,17},{17,25},{2,10},{10,18},{18,26},{... | collective-permute-start | bytes 24584 | tf_op jit(solution)/shard_map/ppermute | solution.py:15
  131.8 5.3 %collective-permute-start.9 = (bf16[4,1,8,128]{3,0,2,1:T(4,128)(2,1)S(1)}, bf16[4,1,8,128]{3,0,2,1:T(4,128)(2,1)S(1)}, u32[]{:S(2)}, u32[]{:S(2)}) collective-permute-start(bf16[4,1,8,128]{3,0,2,1:T(4,128)(2,1)S(1)} %get-tuple-element.16), channel_id=1, source_target_pairs={{8,0},{16,8},{24,16},{9,1},{17,9},{25,17},{10,2},{18,10},{26,18},{... | collective-permute-start | bytes 24584 | tf_op jit(solution)/shard_map/ppermute | solution.py:18
  137.1 7.0 %collective-permute-start.10 = (bf16[4,18,1,128]{3,0,2,1:T(4,128)(2,1)S(1)}, bf16[4,18,1,128]{3,0,2,1:T(4,128)(2,1)S(1)}, u32[]{:S(2)}, u32[]{:S(2)}) collective-permute-start(bf16[4,18,1,128]{3,0,2,1:T(4,128)(2,1)S(1)} %get-tuple-element.13), channel_id=1, source_target_pairs={{0,1},{1,2},{2,3},{3,4},{4,5},{5,6},{6,7},{8,9},{9,10},{10,11},{11... | collective-permute-start | bytes 55304 | tf_op jit(solution)/shard_map/ppermute | solution.py:15
  142.3 5.1 %collective-permute-start.11 = (bf16[4,18,1,128]{3,0,2,1:T(4,128)(2,1)S(1)}, bf16[4,18,1,128]{3,0,2,1:T(4,128)(2,1)S(1)}, u32[]{:S(2)}, u32[]{:S(2)}) collective-permute-start(bf16[4,18,1,128]{3,0,2,1:T(4,128)(2,1)S(1)} %get-tuple-element.14), channel_id=1, source_target_pairs={{1,0},{2,1},{3,2},{4,3},{5,4},{6,5},{7,6},{9,8},{10,9},{11,10},{12... | collective-permute-start | bytes 55304 | tf_op jit(solution)/shard_map/ppermute | solution.py:18
Sparse Core Ops, SparseCore 0:
  24.3 44.9 all-gather.4
  71.1 44.0 all-gather.2
where the time goes:
time: 159 us; the launch traced here: 158 us
  waiting for transfers between devices  45.5 us (29%)
  starting transfers between devices  36.4 us (23%)
  blocking collectives  34.3 us (22%)
  matrix products  17.3 us (11%)
  between operations  13.7 us (9%)
  local copies, waits for them, and re-layouts  9.43 us (6%)
    all_gather x1, waiting for transfers between devices, shards(): lax.all_gather(part_out, 'row', axis=0, tiled=True)  38.1 us
    ppermute x6, starting transfers between devices, padded_2(): lax.ppermute(lax.slice_in_dim(block, block.shape[dim] - width, None, axis...  24.2 us
    all_gather x1, blocking collectives, shards(): lax.all_gather(w_in, 'col', axis=0, tiled=True)  17.6 us
    conv_general_dilated x3, matrix products, convolve(): lax.conv_general_dilated(padded, kernel, (1, 1), 'VALID', dimension_numbe...  17.3 us
    all_gather x1, blocking collectives, shards(): lax.all_gather(w_out, 'col', axis=0, tiled=True)  16.7 us
    ppermute x6, starting transfers between devices, padded_2(): lax.ppermute(lax.slice_in_dim(block, 0, width, axis=dim), axis, backward)  12.2 us
    reshape x1, local copies, waits for them, and re-layouts, shards(): out_back = full_out.reshape(3, 3, MID, C)[::-1, ::-1].transpose(0, 1, 3, 2)  6.59 us
    ppermute x6, waiting for transfers between devices, padded_2(): lax.ppermute(lax.slice_in_dim(block, 0, width, axis=dim), axis, backward)  6.23 us
  transfers between devices with their start and end apart: 14, of which 5 were waited for; matrix products, arithmetic and copies ran while one was open for 11% of the time, Pallas kernels for 0%

commit v1 on v0

v1 whole, which is shorter than its diff:
```python
import jax
import jax.numpy as jnp
from jax import lax
from jax.experimental import pallas as pl
from jax.experimental.pallas import tpu as pltpu
from jax.sharding import PartitionSpec as P

AXES = ("row", "col")
VMEM_LIMIT = 40 * 1024 * 1024
TAPS = 3


def is_power(n):
    return n > 0 and n & (n - 1) == 0


def whole(array):
    return pl.BlockSpec(memory_space=pltpu.VMEM)


def anywhere(array):
    return pl.BlockSpec(memory_space=pl.ANY)


class Geometry:
    def __init__(self, inputs, w_in):
        self.batch, self.high, self.wide, self.chan = inputs.shape
        self.rows, self.cols = lax.axis_size("row"), lax.axis_size("col")
        self.zs = self.cols // 2
        self.shard = w_in.shape[0]
        self.mid = self.shard * self.rows * self.cols // (TAPS * TAPS * self.chan)
        self.pixels = self.batch * self.high * self.wide
        self.ext = self.high + 2
        self.lines = self.batch * self.ext
        self.plane = self.lines * self.wide
        self.unit = 2 * self.shard // self.mid

    def pieces_fit(self):
        return (
            self.cols % 2 == 0
            and is_power(self.zs)
            and is_power(self.rows)
            and self.rows >= 2
            and self.shard % self.chan == 0
            and self.shard % self.mid == 0
            and self.unit % 16 == 0
            and self.chan % self.mid == 0
            and (2 * self.shard // self.chan) % 8 == 0
        )


def device_perm(geo, move):
    pairs = []
    for row in range(geo.rows):
        for col in range(geo.cols):
            r, z, k = move(row, col // 2, col % 2)
            pairs.append((row * geo.cols + col, r * geo.cols + z * 2 + k))
    return pairs


def send(x, perm):
    return lax.ppermute(x, AXES, perm)


def row_bits(geo, core):
    bits = [1 << i for i in range(geo.rows.bit_length() - 1)]
    return bits if core == 0 else bits[::-1]


def row_masks(geo, core):
    masks = [0]
    for bit in row_bits(geo, core):
        masks = masks + [m ^ bit for m in masks]
    return masks


def gather_rows(geo, x):
    parts = [x]
    for step in range(len(row_bits(geo, 0))):
        held = parts[0] if len(parts) == 1 else jnp.concatenate(parts, axis=0)
        perm = device_perm(
            geo, lambda r, z, k: (r ^ row_bits(geo, k)[step], z, k)
        )
        parts = [held, send(held, perm)]
    return parts


def gather_pieces(geo, w_in, w_out, core):
    blocks = geo.chan // geo.mid
    deep = geo.shard // geo.chan
    k1 = w_in.reshape(-1, geo.mid)
    k2 = w_out.reshape(deep, blocks, geo.mid).transpose(1, 0, 2)
    swap = device_perm(geo, lambda r, z, k: (r, z, 1 - k))
    got = send(jnp.where(core == 0, k2.reshape(-1, geo.mid), k1), swap)
    chip1 = jnp.concatenate([k1, got], axis=0)
    chip2 = jnp.concatenate([got.reshape(blocks, deep, geo.mid), k2], axis=1)
    own = jnp.where(core == 0, chip1, chip2.reshape(-1, geo.mid))
    ours = []
    for dz in range(geo.zs):
        here = own if dz == 0 else send(own, device_perm(geo, lambda r, z, k: (r, z ^ dz, k)))
        ours.append(gather_rows(geo, here))
    theirs = [[send(x, swap) for x in parts] for parts in ours]
    flat_ours = [x for parts in ours for x in parts]
    flat_theirs = [x for parts in theirs for x in parts]
    return flat_ours, flat_theirs


def chip_table(geo, core):
    row = lax.axis_index("row")
    z = lax.axis_index("col") // 2
    dz = jnp.arange(geo.zs)[:, None]
    by_core = [
        ((row ^ jnp.array(row_masks(geo, k))[None, :]) * geo.zs + (z ^ dz)).reshape(-1)
        for k in (0, 1)
    ]
    mine = jnp.where(core == 0, by_core[0], by_core[1])
    other = jnp.where(core == 0, by_core[1], by_core[0])
    return jnp.concatenate([jnp.asarray([core]), mine, other]).astype(jnp.int32)


def assemble(geo, table, ours, theirs, k1s, k2st, k2s, sems):
    unit = geo.unit
    core = table[0]
    jobs = []
    count = 0
    for source, group in enumerate((ours, theirs)):
        for ref in group:
            for q in range(ref.shape[0] // unit):
                jobs.append((source, ref.at[pl.ds(q * unit, unit)], count))
                count += 1

    def copies(job):
        source, ref, index = job
        chip = table[1 + index]
        first = pltpu.make_async_copy(
            ref, k1s.at[pl.ds(pl.multiple_of(chip * unit, 16), unit)], sems.at[index]
        )
        second = pltpu.make_async_copy(ref, k2st.at[chip], sems.at[index])
        return first, second, core == source

    for job in jobs:
        first, second, is_first = copies(job)
        pl.when(is_first)(first.start)
        pl.when(jnp.logical_not(is_first))(second.start)
    for job in jobs:
        first, second, is_first = copies(job)
        pl.when(is_first)(first.wait)
        pl.when(jnp.logical_not(is_first))(second.wait)
    blocks = geo.chan // geo.mid
    deep = 2 * geo.shard // geo.chan
    for s in range(geo.rows * geo.zs):
        for b in range(blocks):
            k2s[s * deep : (s + 1) * deep, b * geo.mid : (b + 1) * geo.mid] = k2st[
                s, b * deep : (b + 1) * deep, :
            ]


def partial_convolutions(geo, k1s, k2s, x, cot, ext, up, down, left, right, acc):
    mid, chan = geo.mid, geo.chan
    taps = TAPS * TAPS
    shape = (geo.batch, geo.high, geo.wide, mid)
    lane = lax.broadcasted_iota(jnp.int32, (geo.batch, geo.ext, geo.wide, mid), 2)
    for kind in range(2):
        acc[...] = jnp.zeros_like(acc)
        for t in range(0, taps, 2):
            many = min(2, taps - t)
            if kind == 0:
                rhs = [k1s[(t + n) * chan : (t + n + 1) * chan, :] for n in range(many)]
                rhs = rhs[0] if many == 1 else jnp.concatenate(rhs, axis=1)
                y = jnp.dot(x[...], rhs, preferred_element_type=jnp.float32)
            else:
                rhs = k2s[t * mid : (t + many) * mid, :]
                y = lax.dot_general(
                    cot[...], rhs, (((1,), (1,)), ((), ())), preferred_element_type=jnp.float32
                )
            for n in range(many):
                a, e = divmod(t + n, TAPS)
                if kind == 0:
                    a, e = TAPS - 1 - a, TAPS - 1 - e
                acc[e, :, a : a + geo.high] += y[:, n * mid : (n + 1) * mid].reshape(shape)
        to_left = pltpu.roll(acc[0], geo.wide - 1, 2)
        to_right = pltpu.roll(acc[2], 1, 2)
        zero = jnp.zeros_like(to_left)
        main = (
            acc[1]
            + jnp.where(lane == geo.wide - 1, zero, to_left)
            + jnp.where(lane == 0, zero, to_right)
        )
        side = jnp.where(lane == geo.wide - 1, to_left, zero) + jnp.where(
            lane == 0, to_right, zero
        )
        base = kind * 2 * geo.plane
        ext[pl.ds(base, geo.plane), :] = main.reshape(geo.plane, mid)
        ext[pl.ds(base + geo.plane, geo.plane), :] = side.reshape(geo.plane, mid)
        for place, value in enumerate((main, side)):
            up[kind, place] = value[:, 0:2].astype(jnp.bfloat16)
            down[kind, place] = value[:, geo.high : geo.high + 2].astype(jnp.bfloat16)

        def column(place, j):
            return ext[pl.ds(base + place * geo.plane + j, geo.lines, stride=geo.wide), :]

        left[kind, 0] = column(1, geo.wide - 1)
        left[kind, 1] = column(0, 0)
        right[kind, 0] = column(0, geo.wide - 1)
        right[kind, 1] = column(1, 0)


def first_kernel(geo, pieces, *refs):
    if pieces:
        table, x, cot = refs[:3]
        ours, theirs = refs[3 : 3 + pieces], refs[3 + pieces : 3 + 2 * pieces]
        ext, up, down, left, right, k1s, acc, k2st, k2s, sems = refs[3 + 2 * pieces :]
        assemble(geo, table, ours, theirs, k1s, k2st, k2s, sems)
    else:
        x, cot, k1s, k2s, ext, up, down, left, right, acc = refs
    partial_convolutions(geo, k1s, k2s, x, cot, ext, up, down, left, right, acc)


def first_call(geo, x, cot, pieces=None, kernels=None):
    f32, bf16 = jnp.float32, jnp.bfloat16
    strip = (2, 2, geo.batch, 2, geo.wide, geo.mid)
    edge = (2, 2, geo.lines, geo.mid)
    outs = [
        jax.ShapeDtypeStruct((4 * geo.plane, geo.mid), f32),
        jax.ShapeDtypeStruct(strip, bf16),
        jax.ShapeDtypeStruct(strip, bf16),
        jax.ShapeDtypeStruct(edge, f32),
        jax.ShapeDtypeStruct(edge, f32),
    ]
    scratch = [pltpu.VMEM((TAPS, geo.batch, geo.ext, geo.wide, geo.mid), f32)]
    taps = TAPS * TAPS
    if pieces is not None:
        table, ours, theirs = pieces
        args = [table, x, cot, *ours, *theirs]
        specs = [pl.BlockSpec(memory_space=pltpu.SMEM), whole(x), whole(cot)]
        specs += [anywhere(p) for p in (*ours, *theirs)]
        outs.append(jax.ShapeDtypeStruct((taps * geo.chan, geo.mid), bf16))
        chips = geo.rows * geo.zs
        scratch += [
            pltpu.VMEM((chips, geo.unit, geo.mid), bf16),
            pltpu.VMEM((taps * geo.mid, geo.chan), bf16),
            pltpu.SemaphoreType.DMA((2 * chips,)),
        ]
        count = len(ours)
    else:
        args = [x, cot, *kernels]
        specs = [whole(p) for p in args]
        count = 0
    return pl.pallas_call(
        lambda *refs: first_kernel(geo, count, *refs),
        out_shape=outs,
        in_specs=specs,
        out_specs=[whole(o) for o in outs],
        scratch_shapes=scratch,
        compiler_params=pltpu.CompilerParams(vmem_limit_bytes=VMEM_LIMIT),
        cost_estimate=pl.CostEstimate(
            flops=4 * geo.pixels * taps * geo.chan * geo.mid,
            bytes_accessed=4 * taps * geo.chan * geo.mid + 4 * geo.pixels * geo.chan,
            transcendentals=0,
        ),
    )(*args)


def second_kernel(geo, place, k1_any, ext, above, below, lefts, rights, cot, out, k1s, full, shifted, lhs, sem):
    mid, chan, wide, high = geo.mid, geo.chan, geo.wide, geo.high
    load = pltpu.make_async_copy(k1_any, k1s, sem)
    load.start()
    full[...] = ext[...]
    f32 = jnp.float32
    for kind in range(2):
        for part in range(2):
            base = (kind * 2 + part) * geo.plane
            for b in range(geo.batch):
                top = base + b * geo.ext * wide
                two = (2 * wide, mid)
                full[pl.ds(top, 2 * wide), :] += above[kind, part, b].astype(f32).reshape(two)
                bottom = top + high * wide
                full[pl.ds(bottom, 2 * wide), :] += below[kind, part, b].astype(f32).reshape(two)
        base = kind * 2 * geo.plane

        def add(part, j, value):
            at = pl.ds(base + part * geo.plane + j, geo.lines, stride=wide)
            full[at, :] = full[at, :] + value.astype(f32)

        add(1, wide - 1, lefts[kind, 0])
        add(0, 0, lefts[kind, 1])
        add(0, wide - 1, rights[kind, 0])
        add(1, 0, rights[kind, 1])

    shape = (geo.batch, geo.ext, wide, mid)
    line = lax.broadcasted_iota(jnp.int32, shape, 1)
    lane = lax.broadcasted_iota(jnp.int32, shape, 2)
    row, col = place[0], place[1]
    inside = jnp.logical_and(
        jnp.logical_or(line > 0, row > 0),
        jnp.logical_or(line < geo.ext - 1, row < geo.rows - 1),
    )
    beside = jnp.logical_or(
        jnp.logical_and(lane == wide - 1, col > 0),
        jnp.logical_and(lane == 0, col < geo.cols - 1),
    )
    grads = []
    for part, keep in enumerate((inside, jnp.logical_and(inside, beside))):
        pre = full[pl.ds(part * geo.plane, geo.plane), :].reshape(shape)
        back = full[pl.ds((2 + part) * geo.plane, geo.plane), :].reshape(shape)
        s = jax.nn.sigmoid(pre)
        grad = back * (s * (1.0 + pre * (1.0 - s)))
        grad = jnp.where(keep, grad, jnp.zeros_like(grad))
        grads.append(grad.astype(jnp.bfloat16).astype(f32))
    main, side = grads
    shifted[0] = jnp.where(
        lane == wide - 1, pltpu.roll(side, wide - 1, 2), pltpu.roll(main, wide - 1, 2)
    )
    shifted[1] = main
    shifted[2] = jnp.where(lane == 0, pltpu.roll(side, 1, 2), pltpu.roll(main, 1, 2))
    taps = TAPS * TAPS
    for t in range(taps):
        a, e = divmod(t, TAPS)
        window = shifted[e, :, TAPS - 1 - a : TAPS - 1 - a + high]
        lhs[:, t * mid : (t + 1) * mid] = window.reshape(geo.pixels, mid).astype(jnp.bfloat16)
    load.wait()
    tile = 2 * mid
    for n in range(chan // tile):
        rhs = jnp.concatenate(
            [k1s[t * chan + n * tile : t * chan + (n + 1) * tile, :] for t in range(taps)], axis=1
        )
        y = lax.dot_general(
            lhs[...], rhs, (((1,), (1,)), ((), ())), preferred_element_type=f32
        )
        at = slice(n * tile, (n + 1) * tile)
        out[:, at] = (cot[:, at].astype(f32) + y).astype(jnp.bfloat16)


def second_call(geo, place, k1, ext, above, below, lefts, rights, cot):
    taps = TAPS * TAPS
    out = jax.ShapeDtypeStruct((geo.pixels, geo.chan), jnp.bfloat16)
    args = [place, k1, ext, above, below, lefts, rights, cot]
    specs = [pl.BlockSpec(memory_space=pltpu.SMEM), anywhere(k1)] + [whole(a) for a in args[2:]]
    return pl.pallas_call(
        lambda *refs: second_kernel(geo, *refs),
        out_shape=out,
        in_specs=specs,
        out_specs=whole(out),
        scratch_shapes=[
            pltpu.VMEM((taps * geo.chan, geo.mid), jnp.bfloat16),
            pltpu.VMEM((4 * geo.plane, geo.mid), jnp.float32),
            pltpu.VMEM((TAPS, geo.batch, geo.ext, geo.wide, geo.mid), jnp.float32),
            pltpu.VMEM((geo.pixels, taps * geo.mid), jnp.bfloat16),
            pltpu.SemaphoreType.DMA,
        ],
        compiler_params=pltpu.CompilerParams(vmem_limit_bytes=VMEM_LIMIT),
        cost_estimate=pl.CostEstimate(
            flops=2 * geo.pixels * taps * geo.chan * geo.mid,
            bytes_accessed=2 * taps * geo.chan * geo.mid + 4 * geo.pixels * geo.chan,
            transcendentals=geo.plane * geo.mid * 2,
        ),
    )(*args)


def shift(x, axis, forward):
    count = lax.axis_size(axis)
    pairs = [(i, i + 1) if forward else (i + 1, i) for i in range(count - 1)]
    return lax.ppermute(x, axis, pairs)


def edge_of(strip, parts_and_columns):
    return jnp.stack([strip[:, part, :, :, j] for part, j in parts_and_columns], axis=1)


def shards(inputs, cotangent, w_in, w_out):
    geo = Geometry(inputs, w_in)
    row, col = lax.axis_index("row"), lax.axis_index("col")
    core = col % 2
    x = inputs.reshape(geo.pixels, geo.chan)
    cot = cotangent.reshape(geo.pixels, geo.chan)
    if geo.pieces_fit():
        ours, theirs = gather_pieces(geo, w_in, w_out, core)
        ext, up, down, left, right, k1 = first_call(
            geo, x, cot, pieces=(chip_table(geo, core), ours, theirs)
        )
    else:
        k1 = lax.all_gather(w_in, AXES, axis=0, tiled=True).reshape(-1, geo.mid)
        k2 = lax.all_gather(w_out, AXES, axis=0, tiled=True).reshape(-1, geo.chan)
        ext, up, down, left, right = first_call(geo, x, cot, kernels=(k1, k2))
    above = shift(down, "row", True)
    below = shift(up, "row", False)
    last = geo.wide - 1
    edges = []
    for edge, where in ((left, ((1, last), (0, 0))), (right, ((0, last), (1, 0)))):
        full = edge.reshape(2, 2, geo.batch, geo.ext, geo.mid)
        top = edge_of(above, where).astype(jnp.float32)
        bottom = edge_of(below, where).astype(jnp.float32)
        gap = jnp.zeros((2, 2, geo.batch, geo.ext - 4, geo.mid), jnp.float32)
        full = full + jnp.concatenate([top, gap, bottom], axis=3)
        edges.append(full.astype(jnp.bfloat16).reshape(edge.shape))
    lefts = shift(edges[1], "col", True)
    rights = shift(edges[0], "col", False)
    place = jnp.stack([row, col]).astype(jnp.int32)
    out = second_call(geo, place, k1, ext, above, below, lefts, rights, cot)
    return out.reshape(inputs.shape)


def solution(mesh):
    return jax.shard_map(
        shards,
        mesh=mesh,
        in_specs=(
            P(None, "row", "col", None),
            P(None, "row", "col", None),
            P(("row", "col")),
            P(("row", "col")),
        ),
        out_specs=P(None, "row", "col", None),
        check_vma=False,
    )
```

time: 159 us -> 80.2 us (0.50)
  blocking collectives: 34.3 us -> 0 us
  waiting for transfers between devices: 45.5 us -> 22.8 us
  matrix products: 17.3 us -> 0 us
  Pallas kernels: 0 us -> 14 us
  between operations: 13.7 us -> 0.41 us
  local copies, waits for them, and re-layouts: 9.43 us -> 2.92 us
    all_gather x2 -> x0, waiting for transfers between devices: 38.9 us -> none  [the longest x1 38.1 us: shards(): lax.all_gather(part_out, 'row', axis=0, tiled=True)]
    all_gather x2 -> x0, blocking collectives: 34.3 us -> none  [the longest x1 17.6 us: shards(): lax.all_gather(w_in, 'col', axis=0, tiled=True)]
    conv_general_dilated x3 -> x0, matrix products: 17.3 us -> none  [convolve(): lax.conv_general_dilated(padded, kernel, (1, 1), 'VALID', dimension_numbe...]
    ppermute x12 -> x24, waiting for transfers between devices: 6.54 us -> 22.8 us  [the longest x20 17.2 us: send(): return lax.ppermute(x, AXES, perm)]
    pallas_call x0 -> x2, Pallas kernels: none -> 14 us  [the longest x1 9.57 us: first_call(): pl.pallas_call(lambda *refs: first_kernel(geo, count, *refs), out_shape=o...]
    reshape x1 -> x4, local copies, waits for them, and re-layouts: 6.59 us -> 1.03 us  [the longest x1 0.96 us: gather_pieces(): k2 = w_out.reshape(deep, blocks, geo.mid).transpose(1, 0, 2)]
    ppermute x12 -> x24, starting transfers between devices: 36.4 us -> 37.1 us  [the longest x20 24.6 us: send(): return lax.ppermute(x, AXES, perm)]
  transfers between devices with their start and end apart: 14 -> 24, of which waited for: 5 -> 11; matrix products, arithmetic and copies ran while one was open for 11% -> 1% of each run, Pallas kernels for 0% -> 0%
where the time goes in v1:
time: 80.2 us; the launch traced here: 78.8 us
  starting transfers between devices  37.1 us (46%)
  waiting for transfers between devices  22.8 us (28%)
  Pallas kernels  14 us (17%)
  local copies, waits for them, and re-layouts  2.92 us (4%)
  other arithmetic  1.53 us (2%)
    ppermute x20, starting transfers between devices, send(): return lax.ppermute(x, AXES, perm)  24.6 us
    ppermute x20, waiting for transfers between devices, send(): return lax.ppermute(x, AXES, perm)  17.2 us
    ppermute x4, starting transfers between devices, shift(): return lax.ppermute(x, axis, pairs)  12.5 us
    pallas_call x1, Pallas kernels, first_call(): pl.pallas_call(lambda *refs: first_kernel(geo, count, *refs), out_shape=o...  9.57 us
    ppermute x4, waiting for transfers between devices, shift(): return lax.ppermute(x, axis, pairs)  5.62 us
    pallas_call x1, Pallas kernels, second_call(): pl.pallas_call(lambda *refs: second_kernel(geo, *refs), out_shape=out, in...  4.4 us
  transfers between devices with their start and end apart: 24, of which 11 were waited for; matrix products, arithmetic and copies ran while one was open for 1% of the time, Pallas kernels for 0%

profile of v1, /device:TPU:3, one launch (start us, length us, event | category | flops | bytes accessed | tf_op | source)
XLA Modules:
  0.0 78.8 jit_solution(8619347244285473410)
XLA Ops:
  0.0 1.0 %reshape.56 = bf16[36,10,128]{2,1,0:T(8,128)(2,1)S(1)} reshape(bf16[46080]{0:T(1024)(128)(2,1)} %param.9) | data formatting | bytes 184320 | tf_op jit(solution)/shard_map/reshape | solution.py:92
  2.7 0.9 %collective-permute-done = bf16[360,128]{1,0:T(8,128)(2,1)S(1)} collective-permute-done((bf16[360,128]{1,0:T(8,128)(2,1)S(1)}, bf16[360,128]{1,0:T(8,128)(2,1)S(1)}, u32[]{:S(2)}, u32[]{:S(2)}) %collective-permute-start) | collective-permute-done | bytes 92192 | tf_op jit(solution)/shard_map/ppermute | solution.py:62
  3.9 1.3 %collective-permute-start.1 = (bf16[720,128]{1,0:T(8,128)(2,1)S(1)}, bf16[720,128]{1,0:T(8,128)(2,1)S(1)}, u32[]{:S(2)}, u32[]{:S(2)}) collective-permute-start(bf16[720,128]{1,0:T(8,128)(2,1)S(1)} %maximum_select_fusion), channel_id=1, source_target_pairs={{0,8},{1,17},{2,10},{3,19},{4,12},{5,21},{6,14},{7,23},{8,0},{9,25... | collective-permute-start | bytes 552968 | tf_op jit(solution)/shard_map/ppermute | solution.py:62
  5.2 1.3 %collective-permute-start.3 = (bf16[720,128]{1,0:T(8,128)(2,1)S(1)}, bf16[720,128]{1,0:T(8,128)(2,1)S(1)}, u32[]{:S(2)}, u32[]{:S(2)}) collective-permute-start(bf16[720,128]{1,0:T(8,128)(2,1)S(1)} %maximum_select_fusion), channel_id=1, source_target_pairs={{0,2},{1,3},{2,0},{3,1},{4,6},{5,7},{6,4},{7,5},{8,10},{9,11},{10,... | collective-permute-start | bytes 552968 | tf_op jit(solution)/shard_map/ppermute | solution.py:62
  6.5 2.3 %collective-permute-start.6 = (bf16[720,128]{1,0:T(8,128)(2,1)S(1)}, bf16[720,128]{1,0:T(8,128)(2,1)S(1)}, u32[]{:S(2)}, u32[]{:S(2)}) collective-permute-start(bf16[720,128]{1,0:T(8,128)(2,1)S(1)} %maximum_select_fusion), channel_id=1, source_target_pairs={{0,4},{1,5},{2,6},{3,7},{4,0},{5,1},{6,2},{7,3},{8,12},{9,13},{10,... | collective-permute-start | bytes 552968 | tf_op jit(solution)/shard_map/ppermute | solution.py:62
  9.2 2.3 %collective-permute-start.12 = (bf16[1440,128]{1,0:T(8,128)(2,1)S(1)}, bf16[1440,128]{1,0:T(8,128)(2,1)S(1)}, u32[]{:S(2)}, u32[]{:S(2)}) collective-permute-start(bf16[1440,128]{1,0:T(8,128)(2,1)S(1)} %pad_maximum_fusion.refs_3_), channel_id=1, source_target_pairs={{0,1},{1,0},{2,3},{3,2},{4,5},{5,4},{6,7},{7,6},{8,9},{9,8},{10,11... | collective-permute-start | bytes 1105928 | tf_op jit(solution)/shard_map/ppermute | solution.py:62
  11.5 3.8 %collective-permute-done.3 = bf16[720,128]{1,0:T(8,128)(2,1)S(1)} collective-permute-done((bf16[720,128]{1,0:T(8,128)(2,1)S(1)}, bf16[720,128]{1,0:T(8,128)(2,1)S(1)}, u32[]{:S(2)}, u32[]{:S(2)}) %collective-permute-start.3) | collective-permute-done | bytes 184352 | tf_op jit(solution)/shard_map/ppermute | solution.py:62
  15.3 1.5 %collective-permute-start.7 = (bf16[720,128]{1,0:T(8,128)(2,1)S(1)}, bf16[720,128]{1,0:T(8,128)(2,1)S(1)}, u32[]{:S(2)}, u32[]{:S(2)}) collective-permute-start(bf16[720,128]{1,0:T(8,128)(2,1)S(1)} %collective-permute-done.6), channel_id=1, source_target_pairs={{0,8},{1,17},{2,10},{3,19},{4,12},{5,21},{6,14},{7,23},{8,0},{9,25... | collective-permute-start | bytes 552968 | tf_op jit(solution)/shard_map/ppermute | solution.py:62
  16.8 4.9 %collective-permute-done.9 = bf16[720,128]{1,0:T(8,128)(2,1)S(1)} collective-permute-done((bf16[720,128]{1,0:T(8,128)(2,1)S(1)}, bf16[720,128]{1,0:T(8,128)(2,1)S(1)}, u32[]{:S(2)}, u32[]{:S(2)}) %collective-permute-start.9) | collective-permute-done | bytes 184352 | tf_op jit(solution)/shard_map/ppermute | solution.py:62
  22.0 1.5 %collective-permute-start.8 = (bf16[1440,128]{1,0:T(8,128)(2,1)S(1)}, bf16[1440,128]{1,0:T(8,128)(2,1)}, u32[]{:S(2)}, u32[]{:S(2)}) collective-permute-start(bf16[1440,128]{1,0:T(8,128)(2,1)S(1)} %constant_dynamic-update-slice_fusion.2.refs_7_), channel_id=1, source_target_pairs={{0,16},{1,9},{2,18},{3,11},{4,20},{5,13},{6,22},{7,15},{8,24},{9,1... | collective-permute-start | bytes 1105928 | tf_op jit(solution)/shard_map/ppermute | solution.py:62
  23.5 3.0 %collective-permute-done.10 = bf16[720,128]{1,0:T(8,128)(2,1)S(1)} collective-permute-done((bf16[720,128]{1,0:T(8,128)(2,1)S(1)}, bf16[720,128]{1,0:T(8,128)(2,1)S(1)}, u32[]{:S(2)}, u32[]{:S(2)}) %collective-permute-start.10) | collective-permute-done | bytes 184352 | tf_op jit(solution)/shard_map/ppermute | solution.py:62
  26.6 9.3 %collective-permute-start.14 = (bf16[1440,128]{1,0:T(8,128)(2,1)S(1)}, bf16[1440,128]{1,0:T(8,128)(2,1)}, u32[]{:S(2)}, u32[]{:S(2)}) collective-permute-start(bf16[1440,128]{1,0:T(8,128)(2,1)S(1)} %constant_dynamic-update-slice_fusion.refs_5_), channel_id=1, source_target_pairs={{0,1},{1,0},{2,3},{3,2},{4,5},{5,4},{6,7},{7,6},{8,9},{9,8},{10,11... | collective-permute-start | bytes 1105928 | tf_op jit(solution)/shard_map/ppermute | solution.py:62
  36.6 1.4 %collective-permute-start.13 = (bf16[1440,128]{1,0:T(8,128)(2,1)S(1)}, bf16[1440,128]{1,0:T(8,128)(2,1)}, u32[]{:S(2)}, u32[]{:S(2)}) collective-permute-start(bf16[1440,128]{1,0:T(8,128)(2,1)S(1)} %collective-permute-done.2.refs_4_), channel_id=1, source_target_pairs={{0,1},{1,0},{2,3},{3,2},{4,5},{5,4},{6,7},{7,6},{8,9},{9,8},{10,11... | collective-permute-start | bytes 1105928 | tf_op jit(solution)/shard_map/ppermute | solution.py:62
  38.0 2.6 %collective-permute-done.11.refs_10_ = bf16[1440,128]{1,0:T(8,128)(2,1)} collective-permute-done((bf16[1440,128]{1,0:T(8,128)(2,1)S(1)}, bf16[1440,128]{1,0:T(8,128)(2,1)}, u32[]{:S(2)}, u32[]{:S(2)}) %collective-permute-start.11) | collective-permute-done | bytes 368672 | tf_op jit(solution)/shard_map/ppermute | solution.py:62
  40.5 1.4 %collective-permute-start.15 = (bf16[1440,128]{1,0:T(8,128)(2,1)}, bf16[1440,128]{1,0:T(8,128)(2,1)}, u32[]{:S(2)}, u32[]{:S(2)}) collective-permute-start(bf16[1440,128]{1,0:T(8,128)(2,1)} %collective-permute-done.5.refs_6_), channel_id=1, source_target_pairs={{0,1},{1,0},{2,3},{3,2},{4,5},{5,4},{6,7},{7,6},{8,9},{9,8},{10,11... | collective-permute-start | bytes 1105928 | tf_op jit(solution)/shard_map/ppermute | solution.py:62
  44.6 1.3 %copy-done.1 = bf16[4,16,8,1280]{3,2,1,0:T(8,128)(2,1)S(1)} copy-done((bf16[4,16,8,1280]{3,2,1,0:T(8,128)(2,1)S(1)}, bf16[4,16,8,1280]{3,2,1,0:T(8,128)(2,1)}, u32[]{:S(2)}) %copy-start.1) | copy-done | bytes 1310744
  45.9 9.6 %shard_map.64 = (f32[2304,128]{1,0:T(8,128)S(1)}, bf16[2,2,4,2,8,128]{5,4,3,2,1,0:T(8,128)(2,1)S(1)}, bf16[2,2,4,2,8,128]{5,4,3,2,1,0:T(8,128)(2,1)S(1)}, f32[2,...) custom-call(s32[33]{0:T(128)S(1)} %pad_add_fusion.1.refs_0_, ...), custom_call_target="tpu_custom_call" | custom-call | flops 3019898880 | bytes 8519680 | tf_op jit(solution)/shard_map/pallas_call | solution.py:249
  55.5 3.2 %collective-permute-start.21 = (bf16[2,2,4,2,8,128]{5,4,3,2,1,0:T(8,128)(2,1)S(1)}, bf16[2,2,4,2,8,128]{5,4,3,2,1,0:T(8,128)(2,1)S(1)}, u32[]{:S(2)}, u32[]{:S(2)}) collective-permute-start(bf16[2,2,4,2,8,128]{5,4,3,2,1,0:T(8,128)(2,1)S(1)} %get-tuple-element.14), channel_id=1, source_target_pairs={{8,0},{16,8},{24,16},{9,1},{17,9},{25,17},{10,2},{18,10},{26,18},{... | collective-permute-start | bytes 196616 | tf_op jit(solution)/shard_map/ppermute | solution.py:363
  58.9 2.9 %collective-permute-start.20 = (bf16[2,2,4,2,8,128]{5,4,3,2,1,0:T(8,128)(2,1)S(1)}, bf16[2,2,4,2,8,128]{5,4,3,2,1,0:T(8,128)(2,1)S(1)}, u32[]{:S(2)}, u32[]{:S(2)}) collective-permute-start(bf16[2,2,4,2,8,128]{5,4,3,2,1,0:T(8,128)(2,1)S(1)} %get-tuple-element.13), channel_id=1, source_target_pairs={{0,8},{8,16},{16,24},{1,9},{9,17},{17,25},{2,10},{10,18},{18,26},{... | collective-permute-start | bytes 196616 | tf_op jit(solution)/shard_map/ppermute | solution.py:363
  61.9 2.0 %collective-permute-done.20.refs_3_ = bf16[2,2,4,2,8,128]{5,4,3,2,1,0:T(8,128)(2,1)S(1)} collective-permute-done((bf16[2,2,4,2,8,128]{5,4,3,2,1,0:T(8,128)(2,1)S(1)}, bf16[2,2,4,2,8,128]{5,4,3,2,1,0:T(8,128)(2,1)S(1)}, u32[]{:S(2)}, u32[]{:S(2)}) %collective-permute-start.20) | collective-permute-done | bytes 65568 | tf_op jit(solution)/shard_map/ppermute | solution.py:363
  64.2 4.5 %collective-permute-start.22 = (bf16[2,2,72,128]{3,2,1,0:T(8,128)(2,1)S(1)}, bf16[2,2,72,128]{3,2,1,0:T(8,128)(2,1)S(1)}, u32[]{:S(2)}, u32[]{:S(2)}) collective-permute-start(bf16[2,2,72,128]{3,2,1,0:T(8,128)(2,1)S(1)} %fusion.1), channel_id=1, source_target_pairs={{0,1},{1,2},{2,3},{3,4},{4,5},{5,6},{6,7},{8,9},{9,10},{10,11},{11... | collective-permute-start | bytes 221192 | tf_op jit(solution)/shard_map/ppermute | solution.py:363
  68.7 1.9 %collective-permute-start.23 = (bf16[2,2,72,128]{3,2,1,0:T(8,128)(2,1)S(1)}, bf16[2,2,72,128]{3,2,1,0:T(8,128)(2,1)S(1)}, u32[]{:S(2)}, u32[]{:S(2)}) collective-permute-start(bf16[2,2,72,128]{3,2,1,0:T(8,128)(2,1)S(1)} %fusion), channel_id=1, source_target_pairs={{1,0},{2,1},{3,2},{4,3},{5,4},{6,5},{7,6},{9,8},{10,9},{11,10},{12... | collective-permute-start | bytes 221192 | tf_op jit(solution)/shard_map/ppermute | solution.py:363
  70.7 3.7 %collective-permute-done.23.refs_6_ = bf16[2,2,72,128]{3,2,1,0:T(8,128)(2,1)S(1)} collective-permute-done((bf16[2,2,72,128]{3,2,1,0:T(8,128)(2,1)S(1)}, bf16[2,2,72,128]{3,2,1,0:T(8,128)(2,1)S(1)}, u32[]{:S(2)}, u32[]{:S(2)}) %collective-permute-start.23) | collective-permute-done | bytes 73760 | tf_op jit(solution)/shard_map/ppermute | solution.py:363
  74.4 4.4 %shard_map.65 = bf16[512,1280]{1,0:T(8,128)(2,1)} custom-call(s32[2]{0:T(128)S(1)} %pad_add_fusion.refs_0_, bf16[11520,128]{1,0:T(8,128)(2,1)S(1)} %get-tuple-element.11.refs_1_, f32[2304,128]{1,0:T(8,128)S(1)} %get-tuple-element.12.refs_2_, bf16[2,2,4,2,8,128]{5,4,3,2,1,0:T(8,128)(2,1)S(1)} %collective-permute-done.20.refs_3_, ...), custom_call_target="tpu_custom_call" | custom-call | flops 1509949440 | bytes 5570560 | tf_op jit(solution)/shard_map/pallas_call | solution.py:339
  (80 shorter events, 6.5 us)
Async XLA Ops:
  2.0 1.7 %collective-permute-start = (bf16[360,128]{1,0:T(8,128)(2,1)S(1)}, bf16[360,128]{1,0:T(8,128)(2,1)S(1)}, u32[]{:S(2)}, u32[]{:S(2)}) collective-permute-start(bf16[360,128]{1,0:T(8,128)(2,1)S(1)} %broadcast_select_fusion), channel_id=1, source_target_pairs={{0,1},{1,0},{2,3},{3,2},{4,5},{5,4},{6,7},{7,6},{8,9},{9,8},{10,11... | collective-permute-start | bytes 276488 | tf_op jit(solution)/shard_map/ppermute | solution.py:62
  3.9 4.9 %collective-permute-start.1 = (bf16[720,128]{1,0:T(8,128)(2,1)S(1)}, bf16[720,128]{1,0:T(8,128)(2,1)S(1)}, u32[]{:S(2)}, u32[]{:S(2)}) collective-permute-start(bf16[720,128]{1,0:T(8,128)(2,1)S(1)} %maximum_select_fusion), channel_id=1, source_target_pairs={{0,8},{1,17},{2,10},{3,19},{4,12},{5,21},{6,14},{7,23},{8,0},{9,25... | collective-permute-start | bytes 552968 | tf_op jit(solution)/shard_map/ppermute | solution.py:62
  5.2 10.1 %collective-permute-start.3 = (bf16[720,128]{1,0:T(8,128)(2,1)S(1)}, bf16[720,128]{1,0:T(8,128)(2,1)S(1)}, u32[]{:S(2)}, u32[]{:S(2)}) collective-permute-start(bf16[720,128]{1,0:T(8,128)(2,1)S(1)} %maximum_select_fusion), channel_id=1, source_target_pairs={{0,2},{1,3},{2,0},{3,1},{4,6},{5,7},{6,4},{7,5},{8,10},{9,11},{10,... | collective-permute-start | bytes 552968 | tf_op jit(solution)/shard_map/ppermute | solution.py:62
  6.5 8.8 %collective-permute-start.6 = (bf16[720,128]{1,0:T(8,128)(2,1)S(1)}, bf16[720,128]{1,0:T(8,128)(2,1)S(1)}, u32[]{:S(2)}, u32[]{:S(2)}) collective-permute-start(bf16[720,128]{1,0:T(8,128)(2,1)S(1)} %maximum_select_fusion), channel_id=1, source_target_pairs={{0,4},{1,5},{2,6},{3,7},{4,0},{5,1},{6,2},{7,3},{8,12},{9,13},{10,... | collective-permute-start | bytes 552968 | tf_op jit(solution)/shard_map/ppermute | solution.py:62
  8.8 12.9 %collective-permute-start.9 = (bf16[720,128]{1,0:T(8,128)(2,1)S(1)}, bf16[720,128]{1,0:T(8,128)(2,1)S(1)}, u32[]{:S(2)}, u32[]{:S(2)}) collective-permute-start(bf16[720,128]{1,0:T(8,128)(2,1)S(1)} %maximum_select_fusion), channel_id=1, source_target_pairs={{0,6},{1,7},{2,4},{3,5},{4,2},{5,3},{6,0},{7,1},{8,14},{9,15},{10,... | collective-permute-start | bytes 552968 | tf_op jit(solution)/shard_map/ppermute | solution.py:62
  8.9 17.7 %collective-permute-start.2 = (bf16[1440,128]{1,0:T(8,128)(2,1)S(1)}, bf16[1440,128]{1,0:T(8,128)(2,1)S(1)}, u32[]{:S(2)}, u32[]{:S(2)}) collective-permute-start(bf16[1440,128]{1,0:T(8,128)(2,1)S(1)} %pad_maximum_fusion.refs_3_), channel_id=1, source_target_pairs={{0,16},{1,9},{2,18},{3,11},{4,20},{5,13},{6,22},{7,15},{8,24},{9,1... | collective-permute-start | bytes 1105928 | tf_op jit(solution)/shard_map/ppermute | solution.py:62
  9.2 26.7 %collective-permute-start.12 = (bf16[1440,128]{1,0:T(8,128)(2,1)S(1)}, bf16[1440,128]{1,0:T(8,128)(2,1)S(1)}, u32[]{:S(2)}, u32[]{:S(2)}) collective-permute-start(bf16[1440,128]{1,0:T(8,128)(2,1)S(1)} %pad_maximum_fusion.refs_3_), channel_id=1, source_target_pairs={{0,1},{1,0},{2,3},{3,2},{4,5},{5,4},{6,7},{7,6},{8,9},{9,8},{10,11... | collective-permute-start | bytes 1105928 | tf_op jit(solution)/shard_map/ppermute | solution.py:62
  15.3 6.5 %collective-permute-start.4 = (bf16[720,128]{1,0:T(8,128)(2,1)S(1)}, bf16[720,128]{1,0:T(8,128)(2,1)S(1)}, u32[]{:S(2)}, u32[]{:S(2)}) collective-permute-start(bf16[720,128]{1,0:T(8,128)(2,1)S(1)} %collective-permute-done.3), channel_id=1, source_target_pairs={{0,8},{1,17},{2,10},{3,19},{4,12},{5,21},{6,14},{7,23},{8,0},{9,25... | collective-permute-start | bytes 552968 | tf_op jit(solution)/shard_map/ppermute | solution.py:62
  15.3 6.7 %collective-permute-start.7 = (bf16[720,128]{1,0:T(8,128)(2,1)S(1)}, bf16[720,128]{1,0:T(8,128)(2,1)S(1)}, u32[]{:S(2)}, u32[]{:S(2)}) collective-permute-start(bf16[720,128]{1,0:T(8,128)(2,1)S(1)} %collective-permute-done.6), channel_id=1, source_target_pairs={{0,8},{1,17},{2,10},{3,19},{4,12},{5,21},{6,14},{7,23},{8,0},{9,25... | collective-permute-start | bytes 552968 | tf_op jit(solution)/shard_map/ppermute | solution.py:62
  21.7 4.7 %collective-permute-start.10 = (bf16[720,128]{1,0:T(8,128)(2,1)S(1)}, bf16[720,128]{1,0:T(8,128)(2,1)S(1)}, u32[]{:S(2)}, u32[]{:S(2)}) collective-permute-start(bf16[720,128]{1,0:T(8,128)(2,1)S(1)} %collective-permute-done.9), channel_id=1, source_target_pairs={{0,8},{1,17},{2,10},{3,19},{4,12},{5,21},{6,14},{7,23},{8,0},{9,25... | collective-permute-start | bytes 552968 | tf_op jit(solution)/shard_map/ppermute | solution.py:62
  21.9 14.1 %collective-permute-start.5 = (bf16[1440,128]{1,0:T(8,128)(2,1)S(1)}, bf16[1440,128]{1,0:T(8,128)(2,1)}, u32[]{:S(2)}, u32[]{:S(2)}) collective-permute-start(bf16[1440,128]{1,0:T(8,128)(2,1)S(1)} %constant_dynamic-update-slice_fusion.refs_5_), channel_id=1, source_target_pairs={{0,16},{1,9},{2,18},{3,11},{4,20},{5,13},{6,22},{7,15},{8,24},{9,1... | collective-permute-start | bytes 1105928 | tf_op jit(solution)/shard_map/ppermute | solution.py:62
  22.0 14.6 %collective-permute-start.8 = (bf16[1440,128]{1,0:T(8,128)(2,1)S(1)}, bf16[1440,128]{1,0:T(8,128)(2,1)}, u32[]{:S(2)}, u32[]{:S(2)}) collective-permute-start(bf16[1440,128]{1,0:T(8,128)(2,1)S(1)} %constant_dynamic-update-slice_fusion.2.refs_7_), channel_id=1, source_target_pairs={{0,16},{1,9},{2,18},{3,11},{4,20},{5,13},{6,22},{7,15},{8,24},{9,1... | collective-permute-start | bytes 1105928 | tf_op jit(solution)/shard_map/ppermute | solution.py:62
  26.5 14.0 %collective-permute-start.11 = (bf16[1440,128]{1,0:T(8,128)(2,1)S(1)}, bf16[1440,128]{1,0:T(8,128)(2,1)}, u32[]{:S(2)}, u32[]{:S(2)}) collective-permute-start(bf16[1440,128]{1,0:T(8,128)(2,1)S(1)} %constant_dynamic-update-slice_fusion.4.refs_9_), channel_id=1, source_target_pairs={{0,16},{1,9},{2,18},{3,11},{4,20},{5,13},{6,22},{7,15},{8,24},{9,1... | collective-permute-start | bytes 1105928 | tf_op jit(solution)/shard_map/ppermute | solution.py:62
  26.6 15.3 %collective-permute-start.14 = (bf16[1440,128]{1,0:T(8,128)(2,1)S(1)}, bf16[1440,128]{1,0:T(8,128)(2,1)}, u32[]{:S(2)}, u32[]{:S(2)}) collective-permute-start(bf16[1440,128]{1,0:T(8,128)(2,1)S(1)} %constant_dynamic-update-slice_fusion.refs_5_), channel_id=1, source_target_pairs={{0,1},{1,0},{2,3},{3,2},{4,5},{5,4},{6,7},{7,6},{8,9},{9,8},{10,11... | collective-permute-start | bytes 1105928 | tf_op jit(solution)/shard_map/ppermute | solution.py:62
  35.9 6.0 %collective-permute-start.16 = (bf16[1440,128]{1,0:T(8,128)(2,1)S(1)}, bf16[1440,128]{1,0:T(8,128)(2,1)}, u32[]{:S(2)}, u32[]{:S(2)}) collective-permute-start(bf16[1440,128]{1,0:T(8,128)(2,1)S(1)} %constant_dynamic-update-slice_fusion.2.refs_7_), channel_id=1, source_target_pairs={{0,1},{1,0},{2,3},{3,2},{4,5},{5,4},{6,7},{7,6},{8,9},{9,8},{10,11... | collective-permute-start | bytes 1105928 | tf_op jit(solution)/shard_map/ppermute | solution.py:62
  36.0 6.8 %collective-permute-start.18 = (bf16[1440,128]{1,0:T(8,128)(2,1)S(1)}, bf16[1440,128]{1,0:T(8,128)(2,1)}, u32[]{:S(2)}, u32[]{:S(2)}) collective-permute-start(bf16[1440,128]{1,0:T(8,128)(2,1)S(1)} %constant_dynamic-update-slice_fusion.4.refs_9_), channel_id=1, source_target_pairs={{0,1},{1,0},{2,3},{3,2},{4,5},{5,4},{6,7},{7,6},{8,9},{9,8},{10,11... | collective-permute-start | bytes 1105928 | tf_op jit(solution)/shard_map/ppermute | solution.py:62
  36.6 6.2 %collective-permute-start.13 = (bf16[1440,128]{1,0:T(8,128)(2,1)S(1)}, bf16[1440,128]{1,0:T(8,128)(2,1)}, u32[]{:S(2)}, u32[]{:S(2)}) collective-permute-start(bf16[1440,128]{1,0:T(8,128)(2,1)S(1)} %collective-permute-done.2.refs_4_), channel_id=1, source_target_pairs={{0,1},{1,0},{2,3},{3,2},{4,5},{5,4},{6,7},{7,6},{8,9},{9,8},{10,11... | collective-permute-start | bytes 1105928 | tf_op jit(solution)/shard_map/ppermute | solution.py:62
  40.5 3.0 %collective-permute-start.15 = (bf16[1440,128]{1,0:T(8,128)(2,1)}, bf16[1440,128]{1,0:T(8,128)(2,1)}, u32[]{:S(2)}, u32[]{:S(2)}) collective-permute-start(bf16[1440,128]{1,0:T(8,128)(2,1)} %collective-permute-done.5.refs_6_), channel_id=1, source_target_pairs={{0,1},{1,0},{2,3},{3,2},{4,5},{5,4},{6,7},{7,6},{8,9},{9,8},{10,11... | collective-permute-start | bytes 1105928 | tf_op jit(solution)/shard_map/ppermute | solution.py:62
  41.9 2.2 %collective-permute-start.17 = (bf16[1440,128]{1,0:T(8,128)(2,1)}, bf16[1440,128]{1,0:T(8,128)(2,1)}, u32[]{:S(2)}, u32[]{:S(2)}) collective-permute-start(bf16[1440,128]{1,0:T(8,128)(2,1)} %collective-permute-done.8.refs_8_), channel_id=1, source_target_pairs={{0,1},{1,0},{2,3},{3,2},{4,5},{5,4},{6,7},{7,6},{8,9},{9,8},{10,11... | collective-permute-start | bytes 1105928 | tf_op jit(solution)/shard_map/ppermute | solution.py:62
  41.9 2.7 %collective-permute-start.19 = (bf16[1440,128]{1,0:T(8,128)(2,1)}, bf16[1440,128]{1,0:T(8,128)(2,1)}, u32[]{:S(2)}, u32[]{:S(2)}) collective-permute-start(bf16[1440,128]{1,0:T(8,128)(2,1)} %collective-permute-done.11.refs_10_), channel_id=1, source_target_pairs={{0,1},{1,0},{2,3},{3,2},{4,5},{5,4},{6,7},{7,6},{8,9},{9,8},{10,11... | collective-permute-start | bytes 1105928 | tf_op jit(solution)/shard_map/ppermute | solution.py:62
  55.5 6.3 %collective-permute-start.21 = (bf16[2,2,4,2,8,128]{5,4,3,2,1,0:T(8,128)(2,1)S(1)}, bf16[2,2,4,2,8,128]{5,4,3,2,1,0:T(8,128)(2,1)S(1)}, u32[]{:S(2)}, u32[]{:S(2)}) collective-permute-start(bf16[2,2,4,2,8,128]{5,4,3,2,1,0:T(8,128)(2,1)S(1)} %get-tuple-element.14), channel_id=1, source_target_pairs={{8,0},{16,8},{24,16},{9,1},{17,9},{25,17},{10,2},{18,10},{26,18},{... | collective-permute-start | bytes 196616 | tf_op jit(solution)/shard_map/ppermute | solution.py:363
  58.9 5.0 %collective-permute-start.20 = (bf16[2,2,4,2,8,128]{5,4,3,2,1,0:T(8,128)(2,1)S(1)}, bf16[2,2,4,2,8,128]{5,4,3,2,1,0:T(8,128)(2,1)S(1)}, u32[]{:S(2)}, u32[]{:S(2)}) collective-permute-start(bf16[2,2,4,2,8,128]{5,4,3,2,1,0:T(8,128)(2,1)S(1)} %get-tuple-element.13), channel_id=1, source_target_pairs={{0,8},{8,16},{16,24},{1,9},{9,17},{17,25},{2,10},{10,18},{18,26},{... | collective-permute-start | bytes 196616 | tf_op jit(solution)/shard_map/ppermute | solution.py:363
  64.2 6.5 %collective-permute-start.22 = (bf16[2,2,72,128]{3,2,1,0:T(8,128)(2,1)S(1)}, bf16[2,2,72,128]{3,2,1,0:T(8,128)(2,1)S(1)}, u32[]{:S(2)}, u32[]{:S(2)}) collective-permute-start(bf16[2,2,72,128]{3,2,1,0:T(8,128)(2,1)S(1)} %fusion.1), channel_id=1, source_target_pairs={{0,1},{1,2},{2,3},{3,4},{4,5},{5,6},{6,7},{8,9},{9,10},{10,11},{11... | collective-permute-start | bytes 221192 | tf_op jit(solution)/shard_map/ppermute | solution.py:363
  68.7 5.7 %collective-permute-start.23 = (bf16[2,2,72,128]{3,2,1,0:T(8,128)(2,1)S(1)}, bf16[2,2,72,128]{3,2,1,0:T(8,128)(2,1)S(1)}, u32[]{:S(2)}, u32[]{:S(2)}) collective-permute-start(bf16[2,2,72,128]{3,2,1,0:T(8,128)(2,1)S(1)} %fusion), channel_id=1, source_target_pairs={{1,0},{2,1},{3,2},{4,3},{5,4},{6,5},{7,6},{9,8},{10,9},{11,10},{12... | collective-permute-start | bytes 221192 | tf_op jit(solution)/shard_map/ppermute | solution.py:363
  (4 other events, 73.0 us)

commit v2 on v0

v2 whole, which is shorter than its diff:
```python
import jax
import jax.numpy as jnp
from jax import lax
from jax.experimental import pallas as pl
from jax.experimental.pallas import tpu as pltpu
from jax.sharding import PartitionSpec as P

AXES = ("row", "col")
VMEM_LIMIT = 16 * 1024 * 1024
TAPS = 3


def is_power(n):
    return n > 0 and n & (n - 1) == 0


def whole(array):
    return pl.BlockSpec(memory_space=pltpu.VMEM)


def far(array):
    return pl.BlockSpec(memory_space=pltpu.HBM)


class Geometry:
    def __init__(self, inputs, w_in):
        self.batch, self.high, self.wide, self.chan = inputs.shape
        self.rows, self.cols = lax.axis_size("row"), lax.axis_size("col")
        self.zs = self.cols // 2
        self.shard = w_in.shape[0]
        self.mid = self.shard * self.rows * self.cols // (TAPS * TAPS * self.chan)
        self.pixels = self.batch * self.high * self.wide
        self.ext = self.high + 2
        self.lines = self.batch * self.ext
        self.plane = self.lines * self.wide
        self.deep1 = self.shard // self.mid
        self.deep2 = self.shard // self.chan
        self.blocks = self.chan // self.mid

    def pieces_fit(self):
        return (
            self.cols % 2 == 0
            and is_power(self.zs)
            and is_power(self.rows)
            and self.rows >= 2
            and self.shard % self.chan == 0
            and self.chan % self.mid == 0
            and (2 * self.deep1) % 16 == 0
            and (4 * self.deep2) % 16 == 0
        )


def device_perm(geo, move):
    pairs = []
    for row in range(geo.rows):
        for col in range(geo.cols):
            r, z, k = move(row, col // 2, col % 2)
            pairs.append((row * geo.cols + col, r * geo.cols + z * 2 + k))
    return pairs


def send(x, perm):
    return lax.ppermute(x, AXES, perm)


def row_bits(geo, core):
    bits = [1 << i for i in range(geo.rows.bit_length() - 1)]
    return bits if core == 0 else bits[::-1]


def row_masks(geo, core):
    masks = [0]
    for bit in row_bits(geo, core):
        masks = masks + [m ^ bit for m in masks]
    return masks


def after(x, *others):
    return lax.optimization_barrier((x, *others))[0]


def double_rows(geo, x, step):
    perm = device_perm(geo, lambda r, z, k: (r ^ row_bits(geo, k)[step], z, k))
    return send(x, perm)


def row_stages(geo, parts, holds, split):
    held = parts
    steps = len(row_bits(geo, 0))
    for step in range(steps):
        held = held[0] if len(held) == 1 else jnp.concatenate(held, axis=0)
        if step < len(holds):
            held = after(held, *holds[step])
        if split and step == steps - 1:
            first, second = held[:, : geo.deep1], held[:, geo.deep1 :]
            return [held, double_rows(geo, first, step), double_rows(geo, second, step)]
        held = [held, double_rows(geo, held, step)]
    return held


def depth_groups(geo, own):
    found = {0: own}
    for i in reversed(range(geo.zs.bit_length() - 1)):
        perm = device_perm(geo, lambda r, z, k: (r, z ^ (1 << i), k))
        found.update({mask ^ (1 << i): send(x, perm) for mask, x in list(found.items())})
    masks = list(range(geo.zs))
    split = [masks[:1], masks[1:-1], masks[-1:]] if geo.zs > 1 else [masks]
    return [(group, [found[m] for m in group]) for group in split if group]


def gather_pieces(geo, w_in, w_out):
    k1 = w_in.reshape(1, geo.deep1, geo.mid)
    k2 = w_out.reshape(geo.deep2, geo.blocks, geo.mid).transpose(1, 0, 2)
    own = jnp.concatenate([k1, k2.reshape(1, geo.deep1, geo.mid)], axis=1)
    groups = depth_groups(geo, own)
    last = groups[-1][1][-1]
    done = []
    for n, (_, parts) in enumerate(groups):
        holds = []
        if n == 1 and len(groups) == 3:
            holds = [[done[0][0]], [last, done[0][1]]]
        if n == 2:
            holds = [[done[1][0]]]
        done.append(row_stages(geo, parts, holds, n == len(groups) - 1))
    return [(masks, arrays) for (masks, _), arrays in zip(groups, done)]


def swap_cores(geo, x):
    return send(x, device_perm(geo, lambda r, z, k: (r, z, 1 - k)))


def chip_table(geo, core, groups):
    row = lax.axis_index("row")
    z = lax.axis_index("col") // 2
    table = []
    for masks, _ in groups:
        depth = z ^ jnp.array(masks)[None, :]
        both = [
            ((row ^ jnp.array(row_masks(geo, k))[:, None]) * geo.zs + depth).reshape(-1)
            for k in (0, 1)
        ]
        table += [jnp.where(core == 0, *both), jnp.where(core == 0, *both[::-1])]
    return jnp.concatenate([jnp.asarray([core]), *table]).astype(jnp.int32)


def place_rows(target, base, offset, columns, rows):
    skew = offset % 16
    at = pl.multiple_of(base + (offset - skew), 16)
    if skew:
        rows = jnp.concatenate([target[pl.ds(at, 16), columns][:skew], rows], axis=0)
    target[pl.ds(at, rows.shape[0]), columns] = rows


def place_first(geo, chip, of_core, rows, k1s):
    base = pl.multiple_of(chip * (2 * geo.deep1), 16)
    place_rows(k1s, base, of_core * geo.deep1, slice(0, geo.mid), rows)


def place_second(geo, chip, of_core, rows, k2s):
    base = pl.multiple_of((chip // 2) * (4 * geo.deep2), 16)
    for odd in range(2):

        @pl.when(chip % 2 == odd)
        def _():
            for b in range(geo.blocks):
                columns = slice(b * geo.mid, (b + 1) * geo.mid)
                block = rows[b * geo.deep2 : (b + 1) * geo.deep2]
                offset = (2 * odd + of_core) * geo.deep2
                place_rows(k2s, base, offset, columns, block)


def place_array(geo, table, start, source, ref, k1s, k2s):
    core = table[0]

    @pl.loop(0, ref.shape[0])
    def _(n):
        chip = table[start + n]
        for of_core in range(2):

            @pl.when(core == (source ^ of_core))
            def _():
                if k1s is not None:
                    place_first(geo, chip, of_core, ref[n, : geo.deep1], k1s)
                if k2s is not None:
                    place_second(geo, chip, of_core, ref[n, ref.shape[1] - geo.deep1 :], k2s)


def weights_calls(geo, table, groups, x):
    start = 1
    weights, ext = [], None

    def pieces(starts, arrays, waits):
        theirs = [swap_cores(geo, after(y, *w) if w else y) for y, w in zip(arrays, waits)]
        return [
            (at + source * many, source, y)
            for source, ys in enumerate((arrays, theirs))
            for at, y in zip(starts, ys)
        ]

    held, first, second = groups[-1][1]
    for masks, arrays in groups[:-1]:
        many = geo.rows * len(masks)
        starts = [start, start + arrays[0].shape[0]]
        waits = [[], [*weights[:1], held]] if weights else [[], []]
        weights = early_call(geo, table, pieces(starts, arrays, waits), weights)
        start += 2 * many
    many = geo.rows * len(groups[-1][0])
    next_ = start + held.shape[0]
    wholes = pieces([start], [held], [[]])
    firsts = pieces([next_], [first], [weights[:1]])
    ext, *weights = first_call(geo, table, x, weights, (wholes, firsts))
    return ext, weights, pieces([next_], [second], [[ext]])


def weights_shapes(geo):
    taps = TAPS * TAPS
    return [
        jax.ShapeDtypeStruct((taps * geo.chan, geo.mid), jnp.bfloat16),
        jax.ShapeDtypeStruct((taps * geo.mid, geo.chan), jnp.bfloat16),
    ]


def smem():
    return pl.BlockSpec(memory_space=pltpu.SMEM)


def parameters():
    return pltpu.CompilerParams(vmem_limit_bytes=VMEM_LIMIT)


def early_call(geo, table, pieces, weights):
    def kernel(table, *refs):
        k1s, k2s = refs[-2:]
        for (start, source, _), ref in zip(pieces, refs):
            place_array(geo, table, start, source, ref, k1s, k2s)

    arrays = [x for _, _, x in pieces]
    outs = weights_shapes(geo)
    return pl.pallas_call(
        kernel,
        out_shape=outs,
        in_specs=[smem()] + [whole(x) for x in (*arrays, *weights)],
        out_specs=[whole(o) for o in outs],
        input_output_aliases={1 + len(arrays) + n: n for n in range(len(weights))},
        compiler_params=parameters(),
        cost_estimate=pl.CostEstimate(flops=0, bytes_accessed=0, transcendentals=0),
    )(table, *arrays, *weights)


def partial_convolution(geo, kind, weights, tile, ext, acc):
    mid, chan, wide, high = geo.mid, geo.chan, geo.wide, geo.high
    taps = TAPS * TAPS
    shape = (geo.batch, high, wide, mid)
    lane = lax.broadcasted_iota(jnp.int32, (geo.batch, geo.ext, wide, mid), 2)
    acc[...] = jnp.zeros_like(acc)
    for t in range(0, taps, 2):
        many = min(2, taps - t)
        if kind == 0:
            rhs = [weights[(t + n) * chan : (t + n + 1) * chan, :] for n in range(many)]
            rhs = rhs[0] if many == 1 else jnp.concatenate(rhs, axis=1)
            y = jnp.dot(tile[...], rhs, preferred_element_type=jnp.float32)
        else:
            rhs = weights[t * mid : (t + many) * mid, :]
            y = lax.dot_general(
                tile[...], rhs, (((1,), (1,)), ((), ())), preferred_element_type=jnp.float32
            )
        for n in range(many):
            a, e = divmod(t + n, TAPS)
            if kind == 0:
                a, e = TAPS - 1 - a, TAPS - 1 - e
            acc[e, :, a : a + high] += y[:, n * mid : (n + 1) * mid].reshape(shape)
    to_left = pltpu.roll(acc[0], wide - 1, 2)
    to_right = pltpu.roll(acc[2], 1, 2)
    zero = jnp.zeros_like(to_left)
    main = (
        acc[1]
        + jnp.where(lane == wide - 1, zero, to_left)
        + jnp.where(lane == 0, zero, to_right)
    )
    side = jnp.where(lane == wide - 1, to_left, zero) + jnp.where(lane == 0, to_right, zero)
    ext[pl.ds(0, geo.plane), :] = main.reshape(geo.plane, mid)
    ext[pl.ds(geo.plane, geo.plane), :] = side.reshape(geo.plane, mid)


def column(geo, ext, part, j):
    return ext[pl.ds(part * geo.plane + j, geo.lines, stride=geo.wide), :]


def first_call(geo, table, x, weights, pieces=None):
    ext = jax.ShapeDtypeStruct((2 * geo.plane, geo.mid), jnp.float32)
    wholes, firsts = pieces if pieces else ([], [])
    arrays = [x for _, _, x in wholes + firsts]
    count = len(arrays)

    def kernel(table, x, *refs):
        tile, acc, sem = refs[-3:]
        load = pltpu.make_async_copy(x, tile, sem)
        load.start()
        if pieces:
            ext, k1s, k2s = refs[-6:-3]
            for (start, source, _), ref in zip(wholes, refs):
                place_array(geo, table, start, source, ref, k1s, k2s)
            for (start, source, _), ref in zip(firsts, refs[len(wholes) :]):
                place_array(geo, table, start, source, ref, k1s, None)
        else:
            k1s, ext = refs[0], refs[-4]
        load.wait()
        partial_convolution(geo, 0, k1s, tile, ext, acc)

    args = [table, x, *arrays, *weights]
    outs = [ext] + (weights_shapes(geo) if pieces else [])
    return pl.pallas_call(
        kernel,
        out_shape=outs,
        in_specs=[smem(), far(x)] + [whole(a) for a in args[2:]],
        out_specs=[whole(o) for o in outs],
        scratch_shapes=[
            pltpu.VMEM(x.shape, x.dtype),
            pltpu.VMEM((TAPS, geo.batch, geo.ext, geo.wide, geo.mid), jnp.float32),
            pltpu.SemaphoreType.DMA,
        ],
        input_output_aliases={2 + count + n: 1 + n for n in range(len(weights))} if pieces else {},
        compiler_params=parameters(),
        cost_estimate=pl.CostEstimate(flops=0, bytes_accessed=0, transcendentals=0),
    )(*args)


def back_call(geo, table, cot, ext_pre, k2, pieces=None):
    ext = jax.ShapeDtypeStruct((2 * geo.plane, geo.mid), jnp.float32)
    edge = jax.ShapeDtypeStruct((2, 2, geo.lines, geo.mid), jnp.bfloat16)
    pieces = pieces or []
    arrays = [x for _, _, x in pieces]
    count = len(arrays)

    def kernel(table, cot, ext_pre, *refs):
        k2_in = refs[count]
        ext, inner, outer = refs[count + 1 : count + 4]
        tile, acc, sem = refs[-3:]
        load = pltpu.make_async_copy(cot, tile, sem)
        load.start()
        k2s = refs[-4] if count else k2_in
        for (start, source, _), ref in zip(pieces, refs):
            place_array(geo, table, start, source, ref, None, k2s)
        load.wait()
        partial_convolution(geo, 1, k2s, tile, ext, acc)
        left, right = ((1, geo.wide - 1), (0, 0)), ((0, geo.wide - 1), (1, 0))
        core = table[0]
        for out, is_right in ((inner, core == 0), (outer, core != 0)):
            for kind, plane in enumerate((ext_pre, ext)):
                for n in range(2):
                    value = jnp.where(
                        is_right, column(geo, plane, *right[n]), column(geo, plane, *left[n])
                    )
                    out[kind, n] = value.astype(jnp.bfloat16)

    args = [table, cot, ext_pre, *arrays, k2]
    outs = [ext, edge, edge] + (weights_shapes(geo)[1:] if count else [])
    return pl.pallas_call(
        kernel,
        out_shape=outs,
        in_specs=[smem(), far(cot)] + [whole(a) for a in args[2:]],
        out_specs=[whole(o) for o in outs],
        scratch_shapes=[
            pltpu.VMEM(cot.shape, cot.dtype),
            pltpu.VMEM((TAPS, geo.batch, geo.ext, geo.wide, geo.mid), jnp.float32),
            pltpu.SemaphoreType.DMA,
        ],
        input_output_aliases={3 + count: 3} if count else {},
        compiler_params=parameters(),
        cost_estimate=pl.CostEstimate(
            flops=2 * geo.pixels * TAPS * TAPS * geo.chan * geo.mid,
            bytes_accessed=2 * TAPS * TAPS * geo.chan * geo.mid,
            transcendentals=0,
        ),
    )(*args)[:3]


def beside(geo, inner, outer):
    swap = device_perm(geo, lambda r, z, k: (r, z, 1 - k))
    pairs = []
    for row in range(geo.rows):
        for col in range(1, geo.cols - 1, 2):
            a, b = row * geo.cols + col, row * geo.cols + col + 1
            pairs += [(a, b), (b, a)]
    return send(inner, swap), send(outer, pairs)


def join_call(geo, place, ext_pre, ext_back, inner, outer):
    full = jax.ShapeDtypeStruct((4 * geo.plane, geo.mid), jnp.float32)
    strip = jax.ShapeDtypeStruct((2, 2, geo.batch, 2 * geo.wide, geo.mid), jnp.bfloat16)

    def kernel(place, ext_pre, ext_back, inner, outer, full, near_strip, next_strip):
        core = place[0]
        even = place[1] % 2 == 0
        wide = geo.wide
        for kind, ext in enumerate((ext_pre, ext_back)):
            base = kind * 2 * geo.plane
            full[pl.ds(base, 2 * geo.plane), :] = ext[...]

            def add(part, j, value):
                at = pl.ds(base + part * geo.plane + j, geo.lines, stride=wide)
                full[at, :] = full[at, :] + value

            near = [inner[kind, n].astype(jnp.float32) for n in range(2)]
            next_ = [outer[kind, n].astype(jnp.float32) for n in range(2)]
            left = [jnp.where(core == 0, b, a) for a, b in zip(near, next_)]
            right = [jnp.where(core == 0, a, b) for a, b in zip(near, next_)]
            add(1, wide - 1, left[0])
            add(0, 0, left[1])
            add(0, wide - 1, right[0])
            add(1, 0, right[1])
            for part in range(2):
                for b in range(geo.batch):
                    top = base + part * geo.plane + b * geo.ext * wide
                    for out, low in ((near_strip, even), (next_strip, jnp.logical_not(even))):
                        line = pl.multiple_of(top + jnp.where(low, geo.high * wide, 0), 8)
                        two = full[pl.ds(line, 2 * wide), :]
                        out[kind, part, b] = two.astype(jnp.bfloat16)

    args = [place, ext_pre, ext_back, inner, outer]
    return pl.pallas_call(
        kernel,
        out_shape=[full, strip, strip],
        in_specs=[smem()] + [whole(a) for a in args[1:]],
        out_specs=[whole(o) for o in (full, strip, strip)],
        compiler_params=parameters(),
    )(*args)


def gradient(geo, place, full, lines, shifted):
    mid, wide = geo.mid, geo.wide
    f32 = jnp.float32
    first, count = lines
    shape = (geo.batch, count, wide, mid)
    line = lax.broadcasted_iota(jnp.int32, shape, 1) + first
    lane = lax.broadcasted_iota(jnp.int32, shape, 2)
    row, col = place[1], place[2]
    inside = jnp.logical_and(
        jnp.logical_or(line > 0, row > 0),
        jnp.logical_or(line < geo.ext - 1, row < geo.rows - 1),
    )
    beside = jnp.logical_or(
        jnp.logical_and(lane == wide - 1, col > 0),
        jnp.logical_and(lane == 0, col < geo.cols - 1),
    )
    grads = []
    for part, keep in enumerate((inside, jnp.logical_and(inside, beside))):
        pre, back = full(0, part), full(1, part)
        s = jax.nn.sigmoid(pre)
        grad = back * (s * (1.0 + pre * (1.0 - s)))
        grad = jnp.where(keep, grad, jnp.zeros_like(grad))
        grads.append(grad.astype(jnp.bfloat16).astype(f32))
    main, side = grads
    left = jnp.where(
        lane == wide - 1, pltpu.roll(side, wide - 1, 2), pltpu.roll(main, wide - 1, 2)
    )
    right = jnp.where(lane == 0, pltpu.roll(side, 1, 2), pltpu.roll(main, 1, 2))
    for e, value in enumerate((left, main, right)):
        shifted[e, :, first : first + count] = value


def windows(geo, shifted, spans, lhs):
    for t in range(TAPS * TAPS):
        a, e = divmod(t, TAPS)
        parts = []
        for first, count in spans:
            at = first + TAPS - 1 - a
            parts.append(shifted[e, :, at : at + count])
        window = parts[0] if len(parts) == 1 else jnp.concatenate(parts, axis=1)
        window = window.reshape(-1, geo.mid).astype(jnp.bfloat16)
        lhs[:, t * geo.mid : (t + 1) * geo.mid] = window


def convolve_back(geo, lhs, k1s, cot, spans, out, tiles, sems):
    width = 2 * geo.mid
    at = [sum(many for _, many in spans[:n]) for n in range(len(spans))]
    loads, stores = [], []
    for n, (start, many) in enumerate(spans):
        here, there = pl.ds(at[n], many), pl.ds(start, many)
        loads.append(
            pltpu.make_async_copy(cot.at[:, there], tiles.at[:, here], sems.at[0, n])
        )
        stores.append(
            pltpu.make_async_copy(tiles.at[:, here], out.at[:, there], sems.at[1, n])
        )
    for load in loads:
        load.start()
    yield
    for load in loads:
        load.wait()
    for n in range(geo.chan // width):
        columns = slice(n * width, (n + 1) * width)
        rhs = jnp.concatenate(
            [
                k1s[t * geo.chan + n * width : t * geo.chan + (n + 1) * width, :]
                for t in range(TAPS * TAPS)
            ],
            axis=1,
        )
        y = lax.dot_general(
            lhs[...], rhs, (((1,), (1,)), ((), ())), preferred_element_type=jnp.float32
        )
        y = y.reshape(geo.batch, -1, width)
        tiles[:, :, columns] = (tiles[:, :, columns].astype(jnp.float32) + y).astype(jnp.bfloat16)
    for store in stores:
        store.start()
    for store in stores:
        store.wait()
    yield


def inner_kernel(geo, place, k1s, ext, cot, out, shifted, lhs, tiles, sems):
    wide, mid, high = geo.wide, geo.mid, geo.high
    steps = convolve_back(
        geo, lhs, k1s, cot, [(2 * wide, (high - 4) * wide)], out, tiles, sems
    )
    next(steps)
    count = geo.ext - 4

    def full(kind, part):
        base = (kind * 2 + part) * geo.plane
        plane = ext[pl.ds(base, geo.plane), :].reshape(geo.batch, geo.ext, wide, mid)
        return plane[:, 2 : 2 + count]

    gradient(geo, place, full, (2, count), shifted)
    windows(geo, shifted, [(2, high - 4)], lhs)
    next(steps)


def outer_kernel(geo, place, k1s, ext, near_strip, next_strip, cot, given, out, shifted, lhs, tiles, sems):
    wide, mid, high = geo.wide, geo.mid, geo.high
    two = (geo.batch, 2, wide, mid)
    steps = convolve_back(
        geo, lhs, k1s, cot, [(0, 2 * wide), ((high - 2) * wide, 2 * wide)], out, tiles, sems
    )
    next(steps)
    even = place[1] % 2 == 0
    for first in (0, geo.ext - 4):
        near = jnp.logical_xor(even, first == 0)

        def full(kind, part):
            base = (kind * 2 + part) * geo.plane
            plane = ext[pl.ds(base, geo.plane), :].reshape(geo.batch, geo.ext, wide, mid)
            plane = plane[:, first : first + 4]
            got = jnp.where(
                near,
                near_strip[kind, part].astype(jnp.float32),
                next_strip[kind, part].astype(jnp.float32),
            ).reshape(two)
            none = jnp.zeros_like(got)
            return plane + jnp.concatenate([none, got] if first else [got, none], axis=1)

        gradient(geo, place, full, (first, 4), shifted)
    windows(geo, shifted, [(0, 2), (high - 2, 2)], lhs)
    next(steps)


def second_calls(geo, place, k1, ext, near_strip, next_strip, cot):
    taps = TAPS * TAPS
    image = (geo.batch, geo.high * geo.wide, geo.chan)
    out = jax.ShapeDtypeStruct(image, jnp.bfloat16)
    cot = cot.reshape(image)

    def call(kernel, args, rows, given):
        pixels = rows * geo.wide
        return pl.pallas_call(
            lambda *refs: kernel(geo, *refs),
            out_shape=out,
            in_specs=[smem()] + [whole(a) for a in args[1:]] + [far(a) for a in (cot, *given)],
            out_specs=far(out),
            scratch_shapes=[
                pltpu.VMEM((TAPS, geo.batch, geo.ext, geo.wide, geo.mid), jnp.float32),
                pltpu.VMEM((geo.batch * pixels, taps * geo.mid), jnp.bfloat16),
                pltpu.VMEM((geo.batch, pixels, geo.chan), jnp.bfloat16),
                pltpu.SemaphoreType.DMA((2, 2)),
            ],
            input_output_aliases={len(args) + 1: 0} if given else {},
            compiler_params=pltpu.CompilerParams(vmem_limit_bytes=VMEM_LIMIT),
            cost_estimate=pl.CostEstimate(
                flops=2 * geo.batch * pixels * taps * geo.chan * geo.mid,
                bytes_accessed=2 * taps * geo.chan * geo.mid,
                transcendentals=geo.plane * geo.mid,
            ),
        )(*args, cot, *given)

    inner = call(inner_kernel, [place, k1, ext], geo.high - 4, [])
    return call(outer_kernel, [place, k1, ext, near_strip, next_strip], 4, [inner])


def along_rows(geo, near_strip, next_strip):
    pair = [(i, i ^ 1) for i in range(geo.rows) if i ^ 1 < geo.rows]
    between = [p for i in range(1, geo.rows - 1, 2) for p in ((i, i + 1), (i + 1, i))]
    return lax.ppermute(near_strip, "row", pair), lax.ppermute(next_strip, "row", between)


def shards(inputs, cotangent, w_in, w_out):
    geo = Geometry(inputs, w_in)
    row, col = lax.axis_index("row"), lax.axis_index("col")
    core = col % 2
    x = inputs.reshape(geo.pixels, geo.chan)
    cot = cotangent.reshape(geo.pixels, geo.chan)
    place = jnp.stack([core, row, col]).astype(jnp.int32)
    if geo.pieces_fit():
        groups = gather_pieces(geo, w_in, w_out)
        table = chip_table(geo, core, groups)
        ext_pre, (k1, k2), pieces = weights_calls(geo, table, groups, x)
        ext_back, inner, outer = back_call(geo, table, cot, ext_pre, k2, pieces)
    else:
        k1 = lax.all_gather(w_in, AXES, axis=0, tiled=True).reshape(-1, geo.mid)
        k2 = lax.all_gather(w_out, AXES, axis=0, tiled=True).reshape(-1, geo.chan)
        (ext_pre,) = first_call(geo, place, x, [k1])
        ext_back, inner, outer = back_call(geo, place, cot, ext_pre, k2)
    inner, outer = beside(geo, inner, outer)
    full, *strips = join_call(geo, place, ext_pre, ext_back, inner, outer)
    out = second_calls(geo, place, k1, full, *along_rows(geo, *strips), cot)
    return out.reshape(inputs.shape)


def solution(mesh):
    return jax.shard_map(
        shards,
        mesh=mesh,
        in_specs=(
            P(None, "row", "col", None),
            P(None, "row", "col", None),
            P(("row", "col")),
            P(("row", "col")),
        ),
        out_specs=P(None, "row", "col", None),
        check_vma=False,
    )
```

time: 159 us -> 72.3 us (0.45)
  blocking collectives: 34.3 us -> 0 us
  matrix products: 17.3 us -> 0 us
  waiting for transfers between devices: 45.5 us -> 29.4 us
  Pallas kernels: 0 us -> 14.8 us
  between operations: 13.7 us -> 0.24 us
  starting transfers between devices: 36.4 us -> 24.1 us
  local copies, waits for them, and re-layouts: 9.43 us -> 1.33 us
    all_gather x2 -> x0, waiting for transfers between devices: 38.9 us -> none  [the longest x1 38.1 us: shards(): lax.all_gather(part_out, 'row', axis=0, tiled=True)]
    all_gather x2 -> x0, blocking collectives: 34.3 us -> none  [the longest x1 17.6 us: shards(): lax.all_gather(w_in, 'col', axis=0, tiled=True)]
    ppermute x12 -> x21, waiting for transfers between devices: 6.54 us -> 29.4 us  [the longest x19 29.4 us: send(): return lax.ppermute(x, AXES, perm)]
    conv_general_dilated x3 -> x0, matrix products: 17.3 us -> none  [convolve(): lax.conv_general_dilated(padded, kernel, (1, 1), 'VALID', dimension_numbe...]
    pallas_call x0 -> x7, Pallas kernels: none -> 14.8 us  [the longest x2 5.89 us: call(): pl.pallas_call(lambda *refs: kernel(geo, *refs), out_shape=out, in_specs=...]
    ppermute x12 -> x21, starting transfers between devices: 36.4 us -> 24.1 us  [the longest x19 19.7 us: send(): return lax.ppermute(x, AXES, perm)]
    reshape x1 -> x2, local copies, waits for them, and re-layouts: 6.59 us -> 0.97 us  [the longest x1 0.95 us: gather_pieces(): k2 = w_out.reshape(geo.deep2, geo.blocks, geo.mid).transpose(1, 0, 2)]
    unnamed x16 -> x9, local copies, waits for them, and re-layouts: 2.45 us -> 0.03 us
  transfers between devices with their start and end apart: 14 -> 21, of which waited for: 5 -> 11; matrix products, arithmetic and copies ran while one was open for 11% -> 2% of each run, Pallas kernels for 0% -> 12%
where the time goes in v2:
time: 72.3 us; the launch traced here: 72 us
  waiting for transfers between devices  29.4 us (41%)
  starting transfers between devices  24.1 us (33%)
  Pallas kernels  14.8 us (20%)
  other arithmetic  2.08 us (3%)
  local copies, waits for them, and re-layouts  1.33 us (2%)
    ppermute x19, waiting for transfers between devices, send(): return lax.ppermute(x, AXES, perm)  29.4 us
    ppermute x19, starting transfers between devices, send(): return lax.ppermute(x, AXES, perm)  19.7 us
    pallas_call x2, Pallas kernels, call(): pl.pallas_call(lambda *refs: kernel(geo, *refs), out_shape=out, in_specs=...  5.89 us
    ppermute x1, starting transfers between devices, along_rows(): lax.ppermute(next_strip, 'row', between)  4.37 us
    pallas_call x1, Pallas kernels, first_call(): pl.pallas_call(kernel, out_shape=outs, in_specs=[smem(), far(x)] + [whole...  2.87 us
    pallas_call x1, Pallas kernels, back_call(): pl.pallas_call(kernel, out_shape=outs, in_specs=[smem(), far(cot)] + [who...  2.79 us
    pallas_call x2, Pallas kernels, early_call(): pl.pallas_call(kernel, out_shape=outs, in_specs=[smem()] + [whole(x) for...  2.53 us
  transfers between devices with their start and end apart: 21, of which 11 were waited for; matrix products, arithmetic and copies ran while one was open for 2% of the time, Pallas kernels for 12%

profile of v2, /device:TPU:3, one launch (start us, length us, event | category | flops | bytes accessed | tf_op | source)
XLA Modules:
  0.0 72.0 jit_solution(15935773441981562531)
XLA Ops:
  0.0 1.0 %reshape.64 = bf16[36,10,128]{2,1,0:T(8,128)(2,1)S(1)} reshape(bf16[46080]{0:T(1024)(128)(2,1)} %param.16) | data formatting | bytes 184320 | tf_op jit(solution)/shard_map/reshape | solution.py:113
  1.9 1.3 %collective-permute-start.3 = (bf16[1,720,128]{2,1,0:T(8,128)(2,1)S(1)}, bf16[1,720,128]{2,1,0:T(8,128)(2,1)S(1)}, u32[]{:S(2)}, u32[]{:S(2)}) collective-permute-start(bf16[1,720,128]{2,1,0:T(8,128)(2,1)S(1)} %pad_maximum_fusion.3), channel_id=1, source_target_pairs={{0,8},{1,17},{2,10},{3,19},{4,12},{5,21},{6,14},{7,23},{8,0},{9,25... | collective-permute-start | bytes 552968 | tf_op jit(solution)/shard_map/ppermute | solution.py:63
  3.2 2.3 %collective-permute-start = (bf16[1,720,128]{2,1,0:T(8,128)(2,1)S(1)}, bf16[1,720,128]{2,1,0:T(8,128)(2,1)S(1)}, u32[]{:S(2)}, u32[]{:S(2)}) collective-permute-start(bf16[1,720,128]{2,1,0:T(8,128)(2,1)S(1)} %pad_maximum_fusion.3), channel_id=1, source_target_pairs={{0,4},{1,5},{2,6},{3,7},{4,0},{5,1},{6,2},{7,3},{8,12},{9,13},{10,... | collective-permute-start | bytes 552968 | tf_op jit(solution)/shard_map/ppermute | solution.py:63
  5.5 1.3 %collective-permute-start.2 = (bf16[1,720,128]{2,1,0:T(8,128)(2,1)S(1)}, bf16[1,720,128]{2,1,0:T(8,128)(2,1)S(1)}, u32[]{:S(2)}, u32[]{:S(2)}) collective-permute-start(bf16[1,720,128]{2,1,0:T(8,128)(2,1)S(1)} %pad_maximum_fusion.3), channel_id=1, source_target_pairs={{0,2},{1,3},{2,0},{3,1},{4,6},{5,7},{6,4},{7,5},{8,10},{9,11},{10,... | collective-permute-start | bytes 552968 | tf_op jit(solution)/shard_map/ppermute | solution.py:63
  7.8 6.9 %collective-permute-done = bf16[1,720,128]{2,1,0:T(8,128)(2,1)S(1)} collective-permute-done((bf16[1,720,128]{2,1,0:T(8,128)(2,1)S(1)}, bf16[1,720,128]{2,1,0:T(8,128)(2,1)S(1)}, u32[]{:S(2)}, u32[]{:S(2)}) %collective-permute-start) | collective-permute-done | bytes 184352 | tf_op jit(solution)/shard_map/ppermute | solution.py:63
  14.9 1.2 %collective-permute-start.1 = (bf16[1,720,128]{2,1,0:T(8,128)(2,1)S(1)}, bf16[1,720,128]{2,1,0:T(8,128)(2,1)S(1)}, u32[]{:S(2)}, u32[]{:S(2)}) collective-permute-start(bf16[1,720,128]{2,1,0:T(8,128)(2,1)S(1)} %collective-permute-done), channel_id=1, source_target_pairs={{0,2},{1,3},{2,0},{3,1},{4,6},{5,7},{6,4},{7,5},{8,10},{9,11},{10,... | collective-permute-start | bytes 552968 | tf_op jit(solution)/shard_map/ppermute | solution.py:63
  16.1 7.5 %collective-permute-done.4 = bf16[2,720,128]{2,1,0:T(8,128)(2,1)S(1)} collective-permute-done((bf16[2,720,128]{2,1,0:T(8,128)(2,1)S(1)}, bf16[2,720,128]{2,1,0:T(8,128)(2,1)S(1)}, u32[]{:S(2)}, u32[]{:S(2)}) %collective-permute-start.4) | collective-permute-done | bytes 368672 | tf_op jit(solution)/shard_map/ppermute | solution.py:63
  24.4 3.3 %collective-permute-start.11 = (bf16[2,720,128]{2,1,0:T(8,128)(2,1)S(1)}, bf16[2,720,128]{2,1,0:T(8,128)(2,1)S(1)}, u32[]{:S(2)}, u32[]{:S(2)}) collective-permute-start(bf16[2,720,128]{2,1,0:T(8,128)(2,1)S(1)} %pad_maximum_fusion.2.refs_0_), channel_id=1, source_target_pairs={{0,1},{1,0},{2,3},{3,2},{4,5},{5,4},{6,7},{7,6},{8,9},{9,8},{10,11... | collective-permute-start | bytes 1105928 | tf_op jit(solution)/shard_map/ppermute | solution.py:63
  28.7 5.7 %collective-permute-done.6 = bf16[1,720,128]{2,1,0:T(8,128)(2,1)S(1)} collective-permute-done((bf16[1,720,128]{2,1,0:T(8,128)(2,1)S(1)}, bf16[1,720,128]{2,1,0:T(8,128)(2,1)S(1)}, u32[]{:S(2)}, u32[]{:S(2)}) %collective-permute-start.6) | collective-permute-done | bytes 184352 | tf_op jit(solution)/shard_map/ppermute | solution.py:63
  34.4 1.0 %shard_map.127 = (bf16[11520,128]{1,0:T(8,128)(2,1)S(1)}, bf16[1152,1280]{1,0:T(8,128)(2,1)S(1)}) custom-call(s32[33]{0:T(128)S(1)} %concatenate.18.table, bf16[2,720,128]{2,1,0:T(8,128)(2,1)S(1)} %pad_maximum_fusion.2.refs_0_, bf16[2,720,128]{2,1,0:T(8,128)(2,1)S(1)} %collective-permute-done.5.refs_1_, ...), custom_call_target="tpu_custom_call" | custom-call | tf_op jit(solution)/shard_map/pallas_call | solution.py:239
  35.5 1.5 %collective-permute-done.9.refs_1_ = bf16[4,720,128]{2,1,0:T(8,128)(2,1)S(1)} collective-permute-done((bf16[4,720,128]{2,1,0:T(8,128)(2,1)S(1)}, bf16[4,720,128]{2,1,0:T(8,128)(2,1)S(1)}, u32[]{:S(2)}, u32[]{:S(2)}) %collective-permute-start.9) | collective-permute-done | bytes 737312 | tf_op jit(solution)/shard_map/ppermute | solution.py:63
  36.9 2.5 %collective-permute-start.13 = (bf16[4,720,128]{2,1,0:T(8,128)(2,1)S(1)}, bf16[4,720,128]{2,1,0:T(8,128)(2,1)S(1)}, u32[]{:S(2)}, u32[]{:S(2)}) collective-permute-start(bf16[4,720,128]{2,1,0:T(8,128)(2,1)S(1)} %collective-permute-done.9.refs_1_), channel_id=1, source_target_pairs={{0,1},{1,0},{2,3},{3,2},{4,5},{5,4},{6,7},{7,6},{8,9},{9,8},{10,11... | collective-permute-start | bytes 2211848 | tf_op jit(solution)/shard_map/ppermute | solution.py:63
  39.6 1.6 %collective-permute-start.7 = (bf16[2,720,128]{2,1,0:T(8,128)(2,1)S(1)}, bf16[2,720,128]{2,1,0:T(8,128)(2,1)S(1)}, u32[]{:S(2)}, u32[]{:S(2)}) collective-permute-start(bf16[2,720,128]{2,1,0:T(8,128)(2,1)S(1)} %constant_dynamic-update-slice_fusion.refs_0_), channel_id=1, source_target_pairs={{0,1},{1,0},{2,3},{3,2},{4,5},{5,4},{6,7},{7,6},{8,9},{9,8},{10,11... | collective-permute-start | bytes 1105928 | tf_op jit(solution)/shard_map/ppermute | solution.py:63
  41.3 1.5 %shard_map.128 = (bf16[11520,128]{1,0:T(8,128)(2,1)S(1)}, bf16[1152,1280]{1,0:T(8,128)(2,1)S(1)}) custom-call(s32[33]{0:T(128)S(1)} %concatenate.18.table, bf16[4,720,128]{2,1,0:T(8,128)(2,1)S(1)} %pad_maximum_fusion.refs_0_, bf16[4,720,128]{2,1,0:T(8,128)(2,1)S(1)} %collective-permute-done.9.refs_1_, ...), custom_call_target="tpu_custom_call", output_to_operand_aliasing={{0}: (5, {}), {1}: (6, {})} | custom-call | tf_op jit(solution)/shard_map/pallas_call | solution.py:239
  42.8 1.4 %collective-permute-done.8.refs_2_ = bf16[2,360,128]{2,1,0:T(8,128)(2,1)S(1)} collective-permute-done((bf16[2,360,128]{2,1,0:T(8,128)(2,1)S(1)}, bf16[2,360,128]{2,1,0:T(8,128)(2,1)S(1)}, u32[]{:S(2)}, u32[]{:S(2)}) %collective-permute-start.8) | collective-permute-done | bytes 184352 | tf_op jit(solution)/shard_map/ppermute | solution.py:63
  45.1 1.0 %collective-permute-done.14.refs_3_ = bf16[2,360,128]{2,1,0:T(8,128)(2,1)S(1)} collective-permute-done((bf16[2,360,128]{2,1,0:T(8,128)(2,1)S(1)}, bf16[2,360,128]{2,1,0:T(8,128)(2,1)S(1)}, u32[]{:S(2)}, u32[]{:S(2)}) %collective-permute-start.14) | collective-permute-done | bytes 184352 | tf_op jit(solution)/shard_map/ppermute | solution.py:63
  46.2 2.9 %shard_map.129 = (f32[1152,128]{1,0:T(8,128)S(1)}, bf16[11520,128]{1,0:T(8,128)(2,1)S(1)}, bf16[1152,1280]{1,0:T(8,128)(2,1)S(1)}) custom-call(s32[33]{0:T(128)S(1)} %concatenate.18.table, bf16[512,1280]{1,0:T(8,128)(2,1)S(1)} %bitcast.12, ...), custom_call_target="tpu_custom_call", output_to_operand_aliasing={{1}: (6, {}), {2}: (7, {})} | custom-call | tf_op jit(solution)/shard_map/pallas_call | solution.py:312
  50.7 1.1 %collective-permute-done.16.refs_1_ = bf16[2,360,128]{2,1,0:T(8,128)(2,1)S(1)} collective-permute-done((bf16[2,360,128]{2,1,0:T(8,128)(2,1)S(1)}, bf16[2,360,128]{2,1,0:T(8,128)(2,1)S(1)}, u32[]{:S(2)}, u32[]{:S(2)}) %collective-permute-start.16) | collective-permute-done | bytes 184352 | tf_op jit(solution)/shard_map/ppermute | solution.py:63
  51.7 2.8 %shard_map.130 = (f32[1152,128]{1,0:T(8,128)S(1)}, bf16[2,2,72,128]{3,2,1,0:T(8,128)(2,1)S(1)}, bf16[2,2,72,128]{3,2,1,0:T(8,128)(2,1)S(1)}, bf16[1152,1280]{1,0:T(8,128)(2,1)S(1)}) custom-call(s32[33]{0:T(128)S(1)} %concatenate.18.table, bf16[512,1280]{1,0:T(8,128)(2,1)S(1)} %bitcast.9, ...), custom_call_target="tpu_custom_call", output_to_operand_aliasing={{3}: (5, {})} | custom-call | flops 1509949440 | bytes 2949120 | tf_op jit(solution)/shard_map/pallas_call | solution.py:358
  54.9 3.1 %collective-permute-start.18 = (bf16[2,2,72,128]{3,2,1,0:T(8,128)(2,1)S(1)}, bf16[2,2,72,128]{3,2,1,0:T(8,128)(2,1)S(1)}, u32[]{:S(2)}, u32[]{:S(2)}) collective-permute-start(bf16[2,2,72,128]{3,2,1,0:T(8,128)(2,1)S(1)} %get-tuple-element.39), channel_id=1, source_target_pairs={{1,2},{2,1},{3,4},{4,3},{5,6},{6,5},{9,10},{10,9},{11,12},{12,11},... | collective-permute-start | bytes 221192 | tf_op jit(solution)/shard_map/ppermute | solution.py:63
  58.1 2.8 %collective-permute-done.18.outer = bf16[2,2,72,128]{3,2,1,0:T(8,128)(2,1)S(1)} collective-permute-done((bf16[2,2,72,128]{3,2,1,0:T(8,128)(2,1)S(1)}, bf16[2,2,72,128]{3,2,1,0:T(8,128)(2,1)S(1)}, u32[]{:S(2)}, u32[]{:S(2)}) %collective-permute-start.18) | collective-permute-done | bytes 73760 | tf_op jit(solution)/shard_map/ppermute | solution.py:63
  61.7 4.4 %collective-permute-start.20 = (bf16[2,2,4,16,128]{4,3,2,1,0:T(8,128)(2,1)S(1)}, bf16[2,2,4,16,128]{4,3,2,1,0:T(8,128)(2,1)S(1)}, u32[]{:S(2)}, u32[]{:S(2)}) collective-permute-start(bf16[2,2,4,16,128]{4,3,2,1,0:T(8,128)(2,1)S(1)} %get-tuple-element.42), channel_id=1, source_target_pairs={{8,16},{16,8},{9,17},{17,9},{10,18},{18,10},{11,19},{19,11},{12,20... | collective-permute-start | bytes 196616 | tf_op jit(solution)/shard_map/ppermute | solution.py:593
  66.1 3.4 %shard_map.132.refs_6_ = bf16[4,128,1280]{2,1,0:T(8,128)(2,1)} custom-call(s32[3]{0:T(128)S(1)} %pad_add_fusion.place.refs_0_, bf16[11520,128]{1,0:T(8,128)(2,1)S(1)} %get-tuple-element.33.refs_1_, f32[2304,128]{1,0:T(8,128)S(1)} %get-tuple-element.40.refs_2_, bf16[4,128,1280]{2,1,0:T(8,128)(2,1)S(1)} %bitcast.10), custom_call_target="tpu_custom_call" | custom-call | flops 1132462080 | bytes 2949120 | tf_op jit(solution)/shard_map/pallas_call | solution.py:566
  69.5 2.5 %shard_map.133 = bf16[4,128,1280]{2,1,0:T(8,128)(2,1)} custom-call(s32[3]{0:T(128)S(1)} %pad_add_fusion.place.refs_0_, bf16[11520,128]{1,0:T(8,128)(2,1)S(1)} %get-tuple-element.33.refs_1_, f32[2304,128]{1,0:T(8,128)S(1)} %get-tuple-element.40.refs_2_, ...), custom_call_target="tpu_custom_call", output_to_operand_aliasing={{}: (6, {})} | custom-call | flops 377487360 | bytes 2949120 | tf_op jit(solution)/shard_map/pallas_call | solution.py:566
  (50 shorter events, 7.9 us)
Async XLA Ops:
  0.0 24.4 %copy-start.3 = (s32[2]{0:T(128)S(1)}, s32[2]{0:T(128)}, u32[]{:S(2)}) copy-start(s32[2]{0:T(128)} %constant.47.clone) | copy-start | bytes 28
  0.0 24.4 %copy-start.2 = (s32[4]{0:T(128)S(1)}, s32[4]{0:T(128)}, u32[]{:S(2)}) copy-start(s32[4]{0:T(128)} %constant.46.clone) | copy-start | bytes 52
  1.9 4.9 %collective-permute-start.3 = (bf16[1,720,128]{2,1,0:T(8,128)(2,1)S(1)}, bf16[1,720,128]{2,1,0:T(8,128)(2,1)S(1)}, u32[]{:S(2)}, u32[]{:S(2)}) collective-permute-start(bf16[1,720,128]{2,1,0:T(8,128)(2,1)S(1)} %pad_maximum_fusion.3), channel_id=1, source_target_pairs={{0,8},{1,17},{2,10},{3,19},{4,12},{5,21},{6,14},{7,23},{8,0},{9,25... | collective-permute-start | bytes 552968 | tf_op jit(solution)/shard_map/ppermute | solution.py:63
  3.2 11.5 %collective-permute-start = (bf16[1,720,128]{2,1,0:T(8,128)(2,1)S(1)}, bf16[1,720,128]{2,1,0:T(8,128)(2,1)S(1)}, u32[]{:S(2)}, u32[]{:S(2)}) collective-permute-start(bf16[1,720,128]{2,1,0:T(8,128)(2,1)S(1)} %pad_maximum_fusion.3), channel_id=1, source_target_pairs={{0,4},{1,5},{2,6},{3,7},{4,0},{5,1},{6,2},{7,3},{8,12},{9,13},{10,... | collective-permute-start | bytes 552968 | tf_op jit(solution)/shard_map/ppermute | solution.py:63
  5.5 9.1 %collective-permute-start.2 = (bf16[1,720,128]{2,1,0:T(8,128)(2,1)S(1)}, bf16[1,720,128]{2,1,0:T(8,128)(2,1)S(1)}, u32[]{:S(2)}, u32[]{:S(2)}) collective-permute-start(bf16[1,720,128]{2,1,0:T(8,128)(2,1)S(1)} %pad_maximum_fusion.3), channel_id=1, source_target_pairs={{0,2},{1,3},{2,0},{3,1},{4,6},{5,7},{6,4},{7,5},{8,10},{9,11},{10,... | collective-permute-start | bytes 552968 | tf_op jit(solution)/shard_map/ppermute | solution.py:63
  14.7 8.9 %collective-permute-start.4 = (bf16[2,720,128]{2,1,0:T(8,128)(2,1)S(1)}, bf16[2,720,128]{2,1,0:T(8,128)(2,1)S(1)}, u32[]{:S(2)}, u32[]{:S(2)}) collective-permute-start(bf16[2,720,128]{2,1,0:T(8,128)(2,1)S(1)} %pad_maximum_fusion.1), channel_id=1, source_target_pairs={{0,8},{1,17},{2,10},{3,19},{4,12},{5,21},{6,14},{7,23},{8,0},{9,25... | collective-permute-start | bytes 1105928 | tf_op jit(solution)/shard_map/ppermute | solution.py:63
  14.8 9.5 %collective-permute-start.5 = (bf16[2,720,128]{2,1,0:T(8,128)(2,1)S(1)}, bf16[2,720,128]{2,1,0:T(8,128)(2,1)S(1)}, u32[]{:S(2)}, u32[]{:S(2)}) collective-permute-start(bf16[2,720,128]{2,1,0:T(8,128)(2,1)S(1)} %pad_maximum_fusion.2.refs_0_), channel_id=1, source_target_pairs={{0,16},{1,9},{2,18},{3,11},{4,20},{5,13},{6,22},{7,15},{8,24},{9,1... | collective-permute-start | bytes 1105928 | tf_op jit(solution)/shard_map/ppermute | solution.py:63
  14.9 8.8 %collective-permute-start.1 = (bf16[1,720,128]{2,1,0:T(8,128)(2,1)S(1)}, bf16[1,720,128]{2,1,0:T(8,128)(2,1)S(1)}, u32[]{:S(2)}, u32[]{:S(2)}) collective-permute-start(bf16[1,720,128]{2,1,0:T(8,128)(2,1)S(1)} %collective-permute-done), channel_id=1, source_target_pairs={{0,2},{1,3},{2,0},{3,1},{4,6},{5,7},{6,4},{7,5},{8,10},{9,11},{10,... | collective-permute-start | bytes 552968 | tf_op jit(solution)/shard_map/ppermute | solution.py:63
  24.3 12.6 %collective-permute-start.9 = (bf16[4,720,128]{2,1,0:T(8,128)(2,1)S(1)}, bf16[4,720,128]{2,1,0:T(8,128)(2,1)S(1)}, u32[]{:S(2)}, u32[]{:S(2)}) collective-permute-start(bf16[4,720,128]{2,1,0:T(8,128)(2,1)S(1)} %pad_maximum_fusion.refs_0_), channel_id=1, source_target_pairs={{0,16},{1,9},{2,18},{3,11},{4,20},{5,13},{6,22},{7,15},{8,24},{9,1... | collective-permute-start | bytes 2211848 | tf_op jit(solution)/shard_map/ppermute | solution.py:63
  24.4 10.0 %collective-permute-start.11 = (bf16[2,720,128]{2,1,0:T(8,128)(2,1)S(1)}, bf16[2,720,128]{2,1,0:T(8,128)(2,1)S(1)}, u32[]{:S(2)}, u32[]{:S(2)}) collective-permute-start(bf16[2,720,128]{2,1,0:T(8,128)(2,1)S(1)} %pad_maximum_fusion.2.refs_0_), channel_id=1, source_target_pairs={{0,1},{1,0},{2,3},{3,2},{4,5},{5,4},{6,7},{7,6},{8,9},{9,8},{10,11... | collective-permute-start | bytes 1105928 | tf_op jit(solution)/shard_map/ppermute | solution.py:63
  27.7 6.7 %collective-permute-start.6 = (bf16[1,720,128]{2,1,0:T(8,128)(2,1)S(1)}, bf16[1,720,128]{2,1,0:T(8,128)(2,1)S(1)}, u32[]{:S(2)}, u32[]{:S(2)}) collective-permute-start(bf16[1,720,128]{2,1,0:T(8,128)(2,1)S(1)} %collective-permute-done.1), channel_id=1, source_target_pairs={{0,8},{1,17},{2,10},{3,19},{4,12},{5,21},{6,14},{7,23},{8,0},{9,25... | collective-permute-start | bytes 552968 | tf_op jit(solution)/shard_map/ppermute | solution.py:63
  27.9 6.6 %collective-permute-start.12 = (bf16[2,720,128]{2,1,0:T(8,128)(2,1)S(1)}, bf16[2,720,128]{2,1,0:T(8,128)(2,1)S(1)}, u32[]{:S(2)}, u32[]{:S(2)}) collective-permute-start(bf16[2,720,128]{2,1,0:T(8,128)(2,1)S(1)} %collective-permute-done.5.refs_1_), channel_id=1, source_target_pairs={{0,1},{1,0},{2,3},{3,2},{4,5},{5,4},{6,7},{7,6},{8,9},{9,8},{10,11... | collective-permute-start | bytes 1105928 | tf_op jit(solution)/shard_map/ppermute | solution.py:63
  28.5 12.7 %collective-permute-start.10 = (bf16[4,720,128]{2,1,0:T(8,128)(2,1)S(1)}, bf16[4,720,128]{2,1,0:T(8,128)(2,1)S(1)}, u32[]{:S(2)}, u32[]{:S(2)}) collective-permute-start(bf16[4,720,128]{2,1,0:T(8,128)(2,1)S(1)} %pad_maximum_fusion.refs_0_), channel_id=1, source_target_pairs={{0,1},{1,0},{2,3},{3,2},{4,5},{5,4},{6,7},{7,6},{8,9},{9,8},{10,11... | collective-permute-start | bytes 2211848 | tf_op jit(solution)/shard_map/ppermute | solution.py:63
  36.9 4.4 %collective-permute-start.13 = (bf16[4,720,128]{2,1,0:T(8,128)(2,1)S(1)}, bf16[4,720,128]{2,1,0:T(8,128)(2,1)S(1)}, u32[]{:S(2)}, u32[]{:S(2)}) collective-permute-start(bf16[4,720,128]{2,1,0:T(8,128)(2,1)S(1)} %collective-permute-done.9.refs_1_), channel_id=1, source_target_pairs={{0,1},{1,0},{2,3},{3,2},{4,5},{5,4},{6,7},{7,6},{8,9},{9,8},{10,11... | collective-permute-start | bytes 2211848 | tf_op jit(solution)/shard_map/ppermute | solution.py:63
  39.5 4.7 %collective-permute-start.8 = (bf16[2,360,128]{2,1,0:T(8,128)(2,1)S(1)}, bf16[2,360,128]{2,1,0:T(8,128)(2,1)S(1)}, u32[]{:S(2)}, u32[]{:S(2)}) collective-permute-start(bf16[2,360,128]{2,1,0:T(8,128)(2,1)S(1)} %get-tuple-element.44), channel_id=1, source_target_pairs={{0,16},{1,9},{2,18},{3,11},{4,20},{5,13},{6,22},{7,15},{8,24},{9,1... | collective-permute-start | bytes 552968 | tf_op jit(solution)/shard_map/ppermute | solution.py:63
  39.6 5.5 %collective-permute-start.7 = (bf16[2,720,128]{2,1,0:T(8,128)(2,1)S(1)}, bf16[2,720,128]{2,1,0:T(8,128)(2,1)S(1)}, u32[]{:S(2)}, u32[]{:S(2)}) collective-permute-start(bf16[2,720,128]{2,1,0:T(8,128)(2,1)S(1)} %constant_dynamic-update-slice_fusion.refs_0_), channel_id=1, source_target_pairs={{0,1},{1,0},{2,3},{3,2},{4,5},{5,4},{6,7},{7,6},{8,9},{9,8},{10,11... | collective-permute-start | bytes 1105928 | tf_op jit(solution)/shard_map/ppermute | solution.py:63
  44.3 1.9 %collective-permute-start.14 = (bf16[2,360,128]{2,1,0:T(8,128)(2,1)S(1)}, bf16[2,360,128]{2,1,0:T(8,128)(2,1)S(1)}, u32[]{:S(2)}, u32[]{:S(2)}) collective-permute-start(bf16[2,360,128]{2,1,0:T(8,128)(2,1)S(1)} %collective-permute-done.8.refs_2_), channel_id=1, source_target_pairs={{0,1},{1,0},{2,3},{3,2},{4,5},{5,4},{6,7},{7,6},{8,9},{9,8},{10,11... | collective-permute-start | bytes 552968 | tf_op jit(solution)/shard_map/ppermute | solution.py:63
  45.1 4.7 %collective-permute-start.15 = (bf16[2,360,128]{2,1,0:T(8,128)(2,1)S(1)}, bf16[2,360,128]{2,1,0:T(8,128)(2,1)S(1)}, u32[]{:S(2)}, u32[]{:S(2)}) collective-permute-start(bf16[2,360,128]{2,1,0:T(8,128)(2,1)S(1)} %get-tuple-element.43), channel_id=1, source_target_pairs={{0,16},{1,9},{2,18},{3,11},{4,20},{5,13},{6,22},{7,15},{8,24},{9,1... | collective-permute-start | bytes 552968 | tf_op jit(solution)/shard_map/ppermute | solution.py:63
  46.2 5.5 %copy-start = (bf16[4,16,8,1280]{3,2,1,0:T(8,128)(2,1)S(1)}, bf16[4,16,8,1280]{3,2,1,0:T(8,128)(2,1)}, u32[]{:S(2)}) copy-start(bf16[4,16,8,1280]{3,2,1,0:T(8,128)(2,1)} %param.14) | copy-start | bytes 3932164
  49.8 1.9 %collective-permute-start.16 = (bf16[2,360,128]{2,1,0:T(8,128)(2,1)S(1)}, bf16[2,360,128]{2,1,0:T(8,128)(2,1)S(1)}, u32[]{:S(2)}, u32[]{:S(2)}) collective-permute-start(bf16[2,360,128]{2,1,0:T(8,128)(2,1)S(1)} %collective-permute-done.15.refs_0_), channel_id=1, source_target_pairs={{0,1},{1,0},{2,3},{3,2},{4,5},{5,4},{6,7},{7,6},{8,9},{9,8},{10,11... | collective-permute-start | bytes 552968 | tf_op jit(solution)/shard_map/ppermute | solution.py:63
  54.5 3.6 %collective-permute-start.17 = (bf16[2,2,72,128]{3,2,1,0:T(8,128)(2,1)S(1)}, bf16[2,2,72,128]{3,2,1,0:T(8,128)(2,1)S(1)}, u32[]{:S(2)}, u32[]{:S(2)}) collective-permute-start(bf16[2,2,72,128]{3,2,1,0:T(8,128)(2,1)S(1)} %get-tuple-element.38), channel_id=1, source_target_pairs={{0,1},{1,0},{2,3},{3,2},{4,5},{5,4},{6,7},{7,6},{8,9},{9,8},{10,11... | collective-permute-start | bytes 221192 | tf_op jit(solution)/shard_map/ppermute | solution.py:63
  54.9 6.0 %collective-permute-start.18 = (bf16[2,2,72,128]{3,2,1,0:T(8,128)(2,1)S(1)}, bf16[2,2,72,128]{3,2,1,0:T(8,128)(2,1)S(1)}, u32[]{:S(2)}, u32[]{:S(2)}) collective-permute-start(bf16[2,2,72,128]{3,2,1,0:T(8,128)(2,1)S(1)} %get-tuple-element.39), channel_id=1, source_target_pairs={{1,2},{2,1},{3,4},{4,3},{5,6},{6,5},{9,10},{10,9},{11,12},{12,11},... | collective-permute-start | bytes 221192 | tf_op jit(solution)/shard_map/ppermute | solution.py:63
  61.7 7.8 %collective-permute-start.19 = (bf16[2,2,4,16,128]{4,3,2,1,0:T(8,128)(2,1)S(1)}, bf16[2,2,4,16,128]{4,3,2,1,0:T(8,128)(2,1)S(1)}, u32[]{:S(2)}, u32[]{:S(2)}) collective-permute-start(bf16[2,2,4,16,128]{4,3,2,1,0:T(8,128)(2,1)S(1)} %get-tuple-element.41), channel_id=1, source_target_pairs={{0,8},{8,0},{16,24},{24,16},{1,9},{9,1},{17,25},{25,17},{2,10},{10... | collective-permute-start | bytes 196616 | tf_op jit(solution)/shard_map/ppermute | solution.py:593
  61.7 7.8 %collective-permute-start.20 = (bf16[2,2,4,16,128]{4,3,2,1,0:T(8,128)(2,1)S(1)}, bf16[2,2,4,16,128]{4,3,2,1,0:T(8,128)(2,1)S(1)}, u32[]{:S(2)}, u32[]{:S(2)}) collective-permute-start(bf16[2,2,4,16,128]{4,3,2,1,0:T(8,128)(2,1)S(1)} %get-tuple-element.42), channel_id=1, source_target_pairs={{8,16},{16,8},{9,17},{17,9},{10,18},{18,10},{11,19},{19,11},{12,20... | collective-permute-start | bytes 196616 | tf_op jit(solution)/shard_map/ppermute | solution.py:593
  (1 other events, 4.9 us)

commit v3 on v2

--- a/solution.py
+++ b/solution.py
@@ -8,6 +8,17 @@
 AXES = ("row", "col")
 VMEM_LIMIT = 16 * 1024 * 1024
 TAPS = 3
+PLAN = {
+    "far_half": True,
+    "modes": {"c": "cat", "d": "sep", "o": "cat"},
+    "holds": {},
+    "early": ("o", "c", "d"),
+    "pin": True,
+    "late": 1,
+    "late_c": 1,
+    "table": "d2",
+    "costs": (0, 0),
+}
 
 
 def is_power(n):
@@ -84,57 +95,89 @@
     return send(x, perm)
 
 
-def row_stages(geo, parts, holds, split):
-    held = parts
+def depth_groups(geo):
+    masks = list(range(geo.zs))
+    cut = max(1, geo.zs // 2 if PLAN["far_half"] else geo.zs - 1)
+    groups = {"o": masks[:1], "c": masks[1:cut], "d": masks[cut:]}
+    return {name: group for name, group in groups.items() if group}
+
+
+def own_part(geo, w_in, w_out):
+    def kernel(first, second, out):
+        out[0, : geo.deep1] = first[...]
+        target = lax.broadcasted_iota(jnp.int32, (geo.deep1, 1), 0)
+        block = sum((target >= b * geo.deep2).astype(jnp.int32) for b in range(1, geo.blocks))
+        wanted = (target - geo.deep2 * block) * geo.blocks + block
+        source = lax.broadcasted_iota(jnp.int32, (geo.deep1, geo.deep1), 1)
+        pick = (source == wanted).astype(jnp.bfloat16)
+        rows = jnp.dot(pick, second[...], preferred_element_type=jnp.float32)
+        out[0, geo.deep1 :] = rows.astype(jnp.bfloat16)
+
+    out = jax.ShapeDtypeStruct((1, 2 * geo.deep1, geo.mid), jnp.bfloat16)
+    args = [w.reshape(geo.deep1, geo.mid) for w in (w_in, w_out)]
+    return pl.pallas_call(
+        kernel,
+        out_shape=out,
+        in_specs=[whole(a) for a in args],
+        out_specs=whole(out),
+        compiler_params=parameters(),
+    )(*args)
+
+
+def gather_pieces(geo, w_in, w_out):
+    own = own_part(geo, w_in, w_out)
     steps = len(row_bits(geo, 0))
-    for step in range(steps):
-        held = held[0] if len(held) == 1 else jnp.concatenate(held, axis=0)
-        if step < len(holds):
-            held = after(held, *holds[step])
-        if split and step == steps - 1:
-            first, second = held[:, : geo.deep1], held[:, geo.deep1 :]
-            return [held, double_rows(geo, first, step), double_rows(geo, second, step)]
-        held = [held, double_rows(geo, held, step)]
-    return held
-
-
-def depth_groups(geo, own):
-    found = {0: own}
-    for i in reversed(range(geo.zs.bit_length() - 1)):
-        perm = device_perm(geo, lambda r, z, k: (r, z ^ (1 << i), k))
-        found.update({mask ^ (1 << i): send(x, perm) for mask, x in list(found.items())})
-    masks = list(range(geo.zs))
-    split = [masks[:1], masks[1:-1], masks[-1:]] if geo.zs > 1 else [masks]
-    return [(group, [found[m] for m in group]) for group in split if group]
-
-
-def gather_pieces(geo, w_in, w_out):
-    k1 = w_in.reshape(1, geo.deep1, geo.mid)
-    k2 = w_out.reshape(geo.deep2, geo.blocks, geo.mid).transpose(1, 0, 2)
-    own = jnp.concatenate([k1, k2.reshape(1, geo.deep1, geo.mid)], axis=1)
-    groups = depth_groups(geo, own)
-    last = groups[-1][1][-1]
-    done = []
-    for n, (_, parts) in enumerate(groups):
-        holds = []
-        if n == 1 and len(groups) == 3:
-            holds = [[done[0][0]], [last, done[0][1]]]
-        if n == 2:
-            holds = [[done[1][0]]]
-        done.append(row_stages(geo, parts, holds, n == len(groups) - 1))
-    return [(masks, arrays) for (masks, _), arrays in zip(groups, done)]
+    found = {"z0": own}
+
+    def ready(name, x):
+        held = [found[other] for other in PLAN["holds"].get(name, ()) if other in found]
+        return after(x, *held) if held else x
+
+    def along_z(mask):
+        bit = mask & -mask
+        perm = device_perm(geo, lambda r, z, k: (r, z ^ bit, k))
+        name = f"z{mask}"
+        found[name] = send(ready(name, found[f"z{mask ^ bit}"]), perm)
+
+    def along_rows_of(name, x):
+        parts, count = [x], 0
+        for step in range(steps):
+            if PLAN["modes"][name] == "cat":
+                parts = [parts[0] if step == 0 else jnp.concatenate(parts, axis=0)]
+            new = []
+            for part in parts:
+                key = f"{name}{count}"
+                found[key] = double_rows(geo, ready(key, part), step)
+                new.append(found[key])
+                count += 1
+            parts = parts + new
+        return parts
+
+    groups = depth_groups(geo)
+    if geo.zs > 1:
+        along_z(geo.zs // 2)
+    done = {"o": along_rows_of("o", own)}
+    for mask in sorted(range(1, geo.zs), key=lambda m: (m.bit_count(), m)):
+        if mask != geo.zs // 2:
+            along_z(mask)
+    for name in groups:
+        if name != "o":
+            parts = [found[f"z{mask}"] for mask in groups[name]]
+            x = parts[0] if len(parts) == 1 else jnp.concatenate(parts, axis=0)
+            done[name] = along_rows_of(name, x)
+    return done, found
 
 
 def swap_cores(geo, x):
     return send(x, device_perm(geo, lambda r, z, k: (r, z, 1 - k)))
 
 
-def chip_table(geo, core, groups):
+def chip_table(geo, core):
     row = lax.axis_index("row")
     z = lax.axis_index("col") // 2
     table = []
-    for masks, _ in groups:
-        depth = z ^ jnp.array(masks)[None, :]
+    for group in depth_groups(geo).values():
+        depth = z ^ jnp.array(group)[None, :]
         both = [
             ((row ^ jnp.array(row_masks(geo, k))[:, None]) * geo.zs + depth).reshape(-1)
             for k in (0, 1)
@@ -185,31 +228,47 @@
                     place_second(geo, chip, of_core, ref[n, ref.shape[1] - geo.deep1 :], k2s)
 
 
-def weights_calls(geo, table, groups, x):
+def weights_calls(geo, table, groups, found, tiles):
     start = 1
-    weights, ext = [], None
-
-    def pieces(starts, arrays, waits):
-        theirs = [swap_cores(geo, after(y, *w) if w else y) for y, w in zip(arrays, waits)]
-        return [
-            (at + source * many, source, y)
-            for source, ys in enumerate((arrays, theirs))
-            for at, y in zip(starts, ys)
+    entries = {}
+    last = list(groups)[-1]
+    for name, arrays in groups.items():
+        total = sum(y.shape[0] for y in arrays)
+        at = start
+        entries[name] = []
+        for y in arrays:
+            entries[name].append((at, total, y))
+            at += y.shape[0]
+        start += 2 * total
+
+    def both(some, wait):
+        theirs = [
+            swap_cores(geo, after(y, wait) if wait is not None and n == len(some) - 1 else y)
+            for n, (_, _, y) in enumerate(some)
         ]
-
-    held, first, second = groups[-1][1]
-    for masks, arrays in groups[:-1]:
-        many = geo.rows * len(masks)
-        starts = [start, start + arrays[0].shape[0]]
-        waits = [[], [*weights[:1], held]] if weights else [[], []]
-        weights = early_call(geo, table, pieces(starts, arrays, waits), weights)
-        start += 2 * many
-    many = geo.rows * len(groups[-1][0])
-    next_ = start + held.shape[0]
-    wholes = pieces([start], [held], [[]])
-    firsts = pieces([next_], [first], [weights[:1]])
-    ext, *weights = first_call(geo, table, x, weights, (wholes, firsts))
-    return ext, weights, pieces([next_], [second], [[ext]])
+        return [(at, 0, y) for at, _, y in some] + [
+            (at + total, 1, y) for (at, total, _), y in zip(some, theirs)
+        ]
+
+    final = groups[last][-1]
+    late = entries[last][-PLAN["late"] :]
+    entries[last] = entries[last][: -PLAN["late"]]
+    before = []
+    if PLAN["late_c"] and len(groups) == 3:
+        before = entries["c"][-1:]
+        entries["c"] = entries["c"][:-1]
+    weights = []
+    for names in PLAN["early"]:
+        pieces = []
+        is_last = names == PLAN["early"][-1]
+        loads = tiles if is_last else ()
+        here = after(table, found[PLAN["table"]]) if is_last and PLAN["table"] in found else table
+        for name in names:
+            if entries.get(name):
+                pieces += both(entries[name], weights[0] if weights and PLAN["pin"] else None)
+        if pieces:
+            weights = early_call(geo, here, pieces, weights[:2], loads)
+    return weights[:2], weights[2:], both(before, final) + both(late, None)
 
 
 def weights_shapes(geo):
@@ -228,23 +287,39 @@
     return pltpu.CompilerParams(vmem_limit_bytes=VMEM_LIMIT)
 
 
-def early_call(geo, table, pieces, weights):
+def early_call(geo, table, pieces, weights, tiles=()):
+    arrays = [x for _, _, x in pieces]
+    count = len(arrays) + len(weights)
+
     def kernel(table, *refs):
-        k1s, k2s = refs[-2:]
+        sem = refs[-1]
+        outs = refs[count + len(tiles) : -1]
+        loads = [
+            pltpu.make_async_copy(refs[count + n], outs[2 + n], sem.at[n])
+            for n in range(len(tiles))
+        ]
+        for load in loads:
+            load.start()
         for (start, source, _), ref in zip(pieces, refs):
-            place_array(geo, table, start, source, ref, k1s, k2s)
-
-    arrays = [x for _, _, x in pieces]
-    outs = weights_shapes(geo)
+            place_array(geo, table, start, source, ref, *outs[:2])
+        for load in loads:
+            load.wait()
+
+    outs = weights_shapes(geo) + [jax.ShapeDtypeStruct(t.shape, t.dtype) for t in tiles]
     return pl.pallas_call(
         kernel,
         out_shape=outs,
-        in_specs=[smem()] + [whole(x) for x in (*arrays, *weights)],
+        in_specs=[smem()] + [whole(x) for x in (*arrays, *weights)] + [far(t) for t in tiles],
         out_specs=[whole(o) for o in outs],
+        scratch_shapes=[pltpu.SemaphoreType.DMA((2,))],
         input_output_aliases={1 + len(arrays) + n: n for n in range(len(weights))},
         compiler_params=parameters(),
-        cost_estimate=pl.CostEstimate(flops=0, bytes_accessed=0, transcendentals=0),
-    )(table, *arrays, *weights)
+        cost_estimate=pl.CostEstimate(
+            flops=0,
+            bytes_accessed=PLAN["costs"][0] * 8 * TAPS * TAPS * geo.chan * geo.mid,
+            transcendentals=0,
+        ),
+    )(table, *arrays, *weights, *tiles)
 
 
 def partial_convolution(geo, kind, weights, tile, ext, acc):
@@ -286,93 +361,49 @@
     return ext[pl.ds(part * geo.plane + j, geo.lines, stride=geo.wide), :]
 
 
-def first_call(geo, table, x, weights, pieces=None):
-    ext = jax.ShapeDtypeStruct((2 * geo.plane, geo.mid), jnp.float32)
-    wholes, firsts = pieces if pieces else ([], [])
-    arrays = [x for _, _, x in wholes + firsts]
+def partial_call(geo, table, x, cot, weights, pieces=()):
+    ext = jax.ShapeDtypeStruct((4 * geo.plane, geo.mid), jnp.float32)
+    edge = jax.ShapeDtypeStruct((2, 2, geo.lines, geo.mid), jnp.bfloat16)
+    arrays = [y for _, _, y in pieces]
     count = len(arrays)
 
-    def kernel(table, x, *refs):
-        tile, acc, sem = refs[-3:]
-        load = pltpu.make_async_copy(x, tile, sem)
-        load.start()
-        if pieces:
-            ext, k1s, k2s = refs[-6:-3]
-            for (start, source, _), ref in zip(wholes, refs):
-                place_array(geo, table, start, source, ref, k1s, k2s)
-            for (start, source, _), ref in zip(firsts, refs[len(wholes) :]):
-                place_array(geo, table, start, source, ref, k1s, None)
-        else:
-            k1s, ext = refs[0], refs[-4]
-        load.wait()
-        partial_convolution(geo, 0, k1s, tile, ext, acc)
-
-    args = [table, x, *arrays, *weights]
-    outs = [ext] + (weights_shapes(geo) if pieces else [])
-    return pl.pallas_call(
-        kernel,
-        out_shape=outs,
-        in_specs=[smem(), far(x)] + [whole(a) for a in args[2:]],
-        out_specs=[whole(o) for o in outs],
-        scratch_shapes=[
-            pltpu.VMEM(x.shape, x.dtype),
-            pltpu.VMEM((TAPS, geo.batch, geo.ext, geo.wide, geo.mid), jnp.float32),
-            pltpu.SemaphoreType.DMA,
-        ],
-        input_output_aliases={2 + count + n: 1 + n for n in range(len(weights))} if pieces else {},
-        compiler_params=parameters(),
-        cost_estimate=pl.CostEstimate(flops=0, bytes_accessed=0, transcendentals=0),
-    )(*args)
-
-
-def back_call(geo, table, cot, ext_pre, k2, pieces=None):
-    ext = jax.ShapeDtypeStruct((2 * geo.plane, geo.mid), jnp.float32)
-    edge = jax.ShapeDtypeStruct((2, 2, geo.lines, geo.mid), jnp.bfloat16)
-    pieces = pieces or []
-    arrays = [x for _, _, x in pieces]
-    count = len(arrays)
-
-    def kernel(table, cot, ext_pre, *refs):
-        k2_in = refs[count]
-        ext, inner, outer = refs[count + 1 : count + 4]
-        tile, acc, sem = refs[-3:]
-        load = pltpu.make_async_copy(cot, tile, sem)
-        load.start()
-        k2s = refs[-4] if count else k2_in
+    def kernel(table, x, cot, *refs):
+        acc = refs[-1]
+        outs = refs[count + len(weights) : -1]
+        exts = [outs[0].at[pl.ds(kind * 2 * geo.plane, 2 * geo.plane)] for kind in range(2)]
+        edges = outs[1:3]
+        placed = outs[3:] if pieces else refs[:2]
         for (start, source, _), ref in zip(pieces, refs):
-            place_array(geo, table, start, source, ref, None, k2s)
-        load.wait()
-        partial_convolution(geo, 1, k2s, tile, ext, acc)
+            place_array(geo, table, start, source, ref, *placed)
+        for kind in range(2):
+            partial_convolution(geo, kind, placed[kind], (x, cot)[kind], exts[kind], acc)
         left, right = ((1, geo.wide - 1), (0, 0)), ((0, geo.wide - 1), (1, 0))
         core = table[0]
-        for out, is_right in ((inner, core == 0), (outer, core != 0)):
-            for kind, plane in enumerate((ext_pre, ext)):
+        for out, is_right in zip(edges, (core == 0, core != 0)):
+            for kind, plane in enumerate(exts):
                 for n in range(2):
                     value = jnp.where(
                         is_right, column(geo, plane, *right[n]), column(geo, plane, *left[n])
                     )
                     out[kind, n] = value.astype(jnp.bfloat16)
 
-    args = [table, cot, ext_pre, *arrays, k2]
-    outs = [ext, edge, edge] + (weights_shapes(geo)[1:] if count else [])
+    args = [table, x, cot, *arrays, *weights]
+    outs = [ext, edge, edge] + (weights_shapes(geo) if pieces else [])
+    alias = {3 + count + n: 3 + n for n in range(len(weights))}
     return pl.pallas_call(
         kernel,
         out_shape=outs,
-        in_specs=[smem(), far(cot)] + [whole(a) for a in args[2:]],
+        in_specs=[smem()] + [whole(a) for a in args[1:]],
         out_specs=[whole(o) for o in outs],
-        scratch_shapes=[
-            pltpu.VMEM(cot.shape, cot.dtype),
-            pltpu.VMEM((TAPS, geo.batch, geo.ext, geo.wide, geo.mid), jnp.float32),
-            pltpu.SemaphoreType.DMA,
-        ],
-        input_output_aliases={3 + count: 3} if count else {},
+        scratch_shapes=[pltpu.VMEM((TAPS, geo.batch, geo.ext, geo.wide, geo.mid), jnp.float32)],
+        input_output_aliases=alias if pieces else {},
         compiler_params=parameters(),
         cost_estimate=pl.CostEstimate(
-            flops=2 * geo.pixels * TAPS * TAPS * geo.chan * geo.mid,
-            bytes_accessed=2 * TAPS * TAPS * geo.chan * geo.mid,
+            flops=PLAN["costs"][1] * 4 * geo.pixels * TAPS * TAPS * geo.chan * geo.mid,
+            bytes_accessed=PLAN["costs"][1] * 4 * TAPS * TAPS * geo.chan * geo.mid,
             transcendentals=0,
         ),
-    )(*args)[:3]
+    )(*args)
 
 
 def beside(geo, inner, outer):
@@ -385,17 +416,16 @@
     return send(inner, swap), send(outer, pairs)
 
 
-def join_call(geo, place, ext_pre, ext_back, inner, outer):
+def join_call(geo, place, ext, inner, outer):
     full = jax.ShapeDtypeStruct((4 * geo.plane, geo.mid), jnp.float32)
     strip = jax.ShapeDtypeStruct((2, 2, geo.batch, 2 * geo.wide, geo.mid), jnp.bfloat16)
 
-    def kernel(place, ext_pre, ext_back, inner, outer, full, near_strip, next_strip):
+    def kernel(place, ext, inner, outer, full, near_strip, next_strip):
         core = place[0]
         even = place[1] % 2 == 0
         wide = geo.wide
-        for kind, ext in enumerate((ext_pre, ext_back)):
+        for kind in range(2):
             base = kind * 2 * geo.plane
-            full[pl.ds(base, 2 * geo.plane), :] = ext[...]
 
             def add(part, j, value):
                 at = pl.ds(base + part * geo.plane + j, geo.lines, stride=wide)
@@ -417,12 +447,13 @@
                         two = full[pl.ds(line, 2 * wide), :]
                         out[kind, part, b] = two.astype(jnp.bfloat16)
 
-    args = [place, ext_pre, ext_back, inner, outer]
+    args = [place, ext, inner, outer]
     return pl.pallas_call(
         kernel,
         out_shape=[full, strip, strip],
         in_specs=[smem()] + [whole(a) for a in args[1:]],
         out_specs=[whole(o) for o in (full, strip, strip)],
+        input_output_aliases={1: 0},
         compiler_params=parameters(),
     )(*args)
 
@@ -473,21 +504,6 @@
 
 def convolve_back(geo, lhs, k1s, cot, spans, out, tiles, sems):
     width = 2 * geo.mid
-    at = [sum(many for _, many in spans[:n]) for n in range(len(spans))]
-    loads, stores = [], []
-    for n, (start, many) in enumerate(spans):
-        here, there = pl.ds(at[n], many), pl.ds(start, many)
-        loads.append(
-            pltpu.make_async_copy(cot.at[:, there], tiles.at[:, here], sems.at[0, n])
-        )
-        stores.append(
-            pltpu.make_async_copy(tiles.at[:, here], out.at[:, there], sems.at[1, n])
-        )
-    for load in loads:
-        load.start()
-    yield
-    for load in loads:
-        load.wait()
     for n in range(geo.chan // width):
         columns = slice(n * width, (n + 1) * width)
         rhs = jnp.concatenate(
@@ -501,20 +517,24 @@
             lhs[...], rhs, (((1,), (1,)), ((), ())), preferred_element_type=jnp.float32
         )
         y = y.reshape(geo.batch, -1, width)
-        tiles[:, :, columns] = (tiles[:, :, columns].astype(jnp.float32) + y).astype(jnp.bfloat16)
-    for store in stores:
-        store.start()
+        at = 0
+        for start, many in spans:
+            base = cot[:, start : start + many, columns].astype(jnp.float32)
+            total = (base + y[:, at : at + many]).astype(jnp.bfloat16)
+            tiles[:, at : at + many, columns] = total
+            at += many
+    at, stores = 0, []
+    for n, (start, many) in enumerate(spans):
+        here, there = pl.ds(at, many), pl.ds(start, many)
+        stores.append(pltpu.make_async_copy(tiles.at[:, here], out.at[:, there], sems.at[n]))
+        stores[-1].start()
+        at += many
     for store in stores:
         store.wait()
-    yield
 
 
 def inner_kernel(geo, place, k1s, ext, cot, out, shifted, lhs, tiles, sems):
     wide, mid, high = geo.wide, geo.mid, geo.high
-    steps = convolve_back(
-        geo, lhs, k1s, cot, [(2 * wide, (high - 4) * wide)], out, tiles, sems
-    )
-    next(steps)
     count = geo.ext - 4
 
     def full(kind, part):
@@ -524,16 +544,12 @@
 
     gradient(geo, place, full, (2, count), shifted)
     windows(geo, shifted, [(2, high - 4)], lhs)
-    next(steps)
+    convolve_back(geo, lhs, k1s, cot, [(2 * wide, (high - 4) * wide)], out, tiles, sems)
 
 
 def outer_kernel(geo, place, k1s, ext, near_strip, next_strip, cot, given, out, shifted, lhs, tiles, sems):
     wide, mid, high = geo.wide, geo.mid, geo.high
     two = (geo.batch, 2, wide, mid)
-    steps = convolve_back(
-        geo, lhs, k1s, cot, [(0, 2 * wide), ((high - 2) * wide, 2 * wide)], out, tiles, sems
-    )
-    next(steps)
     even = place[1] % 2 == 0
     for first in (0, geo.ext - 4):
         near = jnp.logical_xor(even, first == 0)
@@ -552,7 +568,8 @@
 
         gradient(geo, place, full, (first, 4), shifted)
     windows(geo, shifted, [(0, 2), (high - 2, 2)], lhs)
-    next(steps)
+    spans = [(0, 2 * wide), ((high - 2) * wide, 2 * wide)]
+    convolve_back(geo, lhs, k1s, cot, spans, out, tiles, sems)
 
 
 def second_calls(geo, place, k1, ext, near_strip, next_strip, cot):
@@ -566,13 +583,13 @@
         return pl.pallas_call(
             lambda *refs: kernel(geo, *refs),
             out_shape=out,
-            in_specs=[smem()] + [whole(a) for a in args[1:]] + [far(a) for a in (cot, *given)],
+            in_specs=[smem()] + [whole(a) for a in (*args[1:], cot)] + [far(g) for g in given],
             out_specs=far(out),
             scratch_shapes=[
                 pltpu.VMEM((TAPS, geo.batch, geo.ext, geo.wide, geo.mid), jnp.float32),
                 pltpu.VMEM((geo.batch * pixels, taps * geo.mid), jnp.bfloat16),
                 pltpu.VMEM((geo.batch, pixels, geo.chan), jnp.bfloat16),
-                pltpu.SemaphoreType.DMA((2, 2)),
+                pltpu.SemaphoreType.DMA((2,)),
             ],
             input_output_aliases={len(args) + 1: 0} if given else {},
             compiler_params=pltpu.CompilerParams(vmem_limit_bytes=VMEM_LIMIT),
@@ -601,17 +618,16 @@
     cot = cotangent.reshape(geo.pixels, geo.chan)
     place = jnp.stack([core, row, col]).astype(jnp.int32)
     if geo.pieces_fit():
-        groups = gather_pieces(geo, w_in, w_out)
-        table = chip_table(geo, core, groups)
-        ext_pre, (k1, k2), pieces = weights_calls(geo, table, groups, x)
-        ext_back, inner, outer = back_call(geo, table, cot, ext_pre, k2, pieces)
+        groups, found = gather_pieces(geo, w_in, w_out)
+        table = chip_table(geo, core)
+        weights, (x, cot), pieces = weights_calls(geo, table, groups, found, (x, cot))
+        ext, inner, outer, k1, _ = partial_call(geo, table, x, cot, weights, pieces)
     else:
         k1 = lax.all_gather(w_in, AXES, axis=0, tiled=True).reshape(-1, geo.mid)
         k2 = lax.all_gather(w_out, AXES, axis=0, tiled=True).reshape(-1, geo.chan)
-        (ext_pre,) = first_call(geo, place, x, [k1])
-        ext_back, inner, outer = back_call(geo, place, cot, ext_pre, k2)
+        ext, inner, outer = partial_call(geo, place, x, cot, [k1, k2])
     inner, outer = beside(geo, inner, outer)
-    full, *strips = join_call(geo, place, ext_pre, ext_back, inner, outer)
+    full, *strips = join_call(geo, place, ext, inner, outer)
     out = second_calls(geo, place, k1, full, *along_rows(geo, *strips), cot)
     return out.reshape(inputs.shape)
 

time: 72.3 us -> 63.6 us (0.88)
  waiting for transfers between devices: 29.4 us -> 18.8 us
  starting transfers between devices: 24.1 us -> 26.4 us
  local copies, waits for them, and re-layouts: 1.33 us -> 2.12 us
    ppermute x19 -> x20, waiting for transfers between devices: 29.4 us -> 18.8 us  [send(): return lax.ppermute(x, AXES, perm)]
    ppermute x19 -> x20, starting transfers between devices: 19.7 us -> 22 us  [send(): return lax.ppermute(x, AXES, perm)]
    concatenate x4 -> x1, other arithmetic: 1.92 us -> 0.04 us  [along_rows_of(): parts = [parts[0] if step == 0 else jnp.concatenate(parts, axis=0)]]
    unnamed x9 -> x10, local copies, waits for them, and re-layouts: 0.03 us -> 1.82 us
    reshape x2 -> x0, local copies, waits for them, and re-layouts: 0.97 us -> none  [the longest x1 0.95 us: gather_pieces(): k2 = w_out.reshape(geo.deep2, geo.blocks, geo.mid).transpose(1, 0, 2)]
    pallas_call x2 -> x3, Pallas kernels: 2.53 us -> 3.3 us  [early_call(): pl.pallas_call(kernel, out_shape=outs, in_specs=[smem()] + [whole(x) for...]
    pallas_call x2, Pallas kernels: 5.66 us -> 4.91 us  [the longest x1 4.66 us: partial_call(): pl.pallas_call(kernel, out_shape=outs, in_specs=[smem()] + [whole(a) for...]
  transfers between devices with their start and end apart: 21 -> 22, of which waited for: 11 -> 9; matrix products, arithmetic and copies ran while one was open for 2% -> 3% of each run, Pallas kernels for 12% -> 10%
where the time goes in v3:
time: 63.6 us; the launch traced here: 63.4 us
  starting transfers between devices  26.4 us (42%)
  waiting for transfers between devices  18.8 us (30%)
  Pallas kernels  14.3 us (22%)
  local copies, waits for them, and re-layouts  2.12 us (3%)
  other arithmetic  1.51 us (2%)
    ppermute x20, starting transfers between devices, send(): return lax.ppermute(x, AXES, perm)  22 us
    ppermute x20, waiting for transfers between devices, send(): return lax.ppermute(x, AXES, perm)  18.8 us
    pallas_call x2, Pallas kernels, call(): pl.pallas_call(lambda *refs: kernel(geo, *refs), out_shape=out, in_specs=...  5.42 us
    pallas_call x1, Pallas kernels, partial_call(): pl.pallas_call(kernel, out_shape=outs, in_specs=[smem()] + [whole(a) for...  4.66 us
    ppermute x1, starting transfers between devices, along_rows(): lax.ppermute(next_strip, 'row', between)  4.07 us
    pallas_call x3, Pallas kernels, early_call(): pl.pallas_call(kernel, out_shape=outs, in_specs=[smem()] + [whole(x) for...  3.3 us
    unnamed x10, local copies, waits for them, and re-layouts  1.82 us
  transfers between devices with their start and end apart: 22, of which 9 were waited for; matrix products, arithmetic and copies ran while one was open for 3% of the time, Pallas kernels for 10%

profile of v3, /device:TPU:3, one launch (start us, length us, event | category | flops | bytes accessed | tf_op | source)
XLA Modules:
  0.0 63.4 jit_solution(585252574568267952)
XLA Ops:
  2.0 2.4 %collective-permute-start = (bf16[1,720,128]{2,1,0:T(8,128)(2,1)S(1)}, bf16[1,720,128]{2,1,0:T(8,128)(2,1)S(1)}, u32[]{:S(2)}, u32[]{:S(2)}) collective-permute-start(bf16[1,720,128]{2,1,0:T(8,128)(2,1)S(1)} %shard_map.127), channel_id=1, source_target_pairs={{0,4},{1,5},{2,6},{3,7},{4,0},{5,1},{6,2},{7,3},{8,12},{9,13},{10,... | collective-permute-start | bytes 552968 | tf_op jit(solution)/shard_map/ppermute | solution.py:74
  4.4 1.3 %collective-permute-start.7 = (bf16[1,720,128]{2,1,0:T(8,128)(2,1)S(1)}, bf16[1,720,128]{2,1,0:T(8,128)(2,1)S(1)}, u32[]{:S(2)}, u32[]{:S(2)}) collective-permute-start(bf16[1,720,128]{2,1,0:T(8,128)(2,1)S(1)} %shard_map.127), channel_id=1, source_target_pairs={{0,2},{1,3},{2,0},{3,1},{4,6},{5,7},{6,4},{7,5},{8,10},{9,11},{10,... | collective-permute-start | bytes 552968 | tf_op jit(solution)/shard_map/ppermute | solution.py:74
  5.7 1.2 %collective-permute-start.9 = (bf16[1,720,128]{2,1,0:T(8,128)(2,1)S(1)}, bf16[1,720,128]{2,1,0:T(8,128)(2,1)S(1)}, u32[]{:S(2)}, u32[]{:S(2)}) collective-permute-start(bf16[1,720,128]{2,1,0:T(8,128)(2,1)S(1)} %shard_map.127), channel_id=1, source_target_pairs={{0,8},{1,17},{2,10},{3,19},{4,12},{5,21},{6,14},{7,23},{8,0},{9,25... | collective-permute-start | bytes 552968 | tf_op jit(solution)/shard_map/ppermute | solution.py:74
  7.6 2.8 %collective-permute-done.9 = bf16[1,720,128]{2,1,0:T(8,128)(2,1)S(1)} collective-permute-done((bf16[1,720,128]{2,1,0:T(8,128)(2,1)S(1)}, bf16[1,720,128]{2,1,0:T(8,128)(2,1)S(1)}, u32[]{:S(2)}, u32[]{:S(2)}) %collective-permute-start.9) | collective-permute-done | bytes 184352 | tf_op jit(solution)/shard_map/ppermute | solution.py:74
  10.7 1.7 %collective-permute-done = bf16[1,720,128]{2,1,0:T(8,128)(2,1)S(1)} collective-permute-done((bf16[1,720,128]{2,1,0:T(8,128)(2,1)S(1)}, bf16[1,720,128]{2,1,0:T(8,128)(2,1)S(1)}, u32[]{:S(2)}, u32[]{:S(2)}) %collective-permute-start) | collective-permute-done | bytes 184352 | tf_op jit(solution)/shard_map/ppermute | solution.py:74
  12.5 1.4 %collective-permute-start.1 = (bf16[1,720,128]{2,1,0:T(8,128)(2,1)S(1)}, bf16[1,720,128]{2,1,0:T(8,128)(2,1)S(1)}, u32[]{:S(2)}, u32[]{:S(2)}) collective-permute-start(bf16[1,720,128]{2,1,0:T(8,128)(2,1)S(1)} %collective-permute-done), channel_id=1, source_target_pairs={{0,2},{1,3},{2,0},{3,1},{4,6},{5,7},{6,4},{7,5},{8,10},{9,11},{10,... | collective-permute-start | bytes 552968 | tf_op jit(solution)/shard_map/ppermute | solution.py:74
  15.3 1.2 %collective-permute-start.8 = (bf16[1,720,128]{2,1,0:T(8,128)(2,1)S(1)}, bf16[1,720,128]{2,1,0:T(8,128)(2,1)S(1)}, u32[]{:S(2)}, u32[]{:S(2)}) collective-permute-start(bf16[1,720,128]{2,1,0:T(8,128)(2,1)S(1)} %collective-permute-done.7), channel_id=1, source_target_pairs={{0,8},{1,17},{2,10},{3,19},{4,12},{5,21},{6,14},{7,23},{8,0},{9,25... | collective-permute-start | bytes 552968 | tf_op jit(solution)/shard_map/ppermute | solution.py:74
  17.4 1.3 %collective-permute-start.2 = (bf16[2,720,128]{2,1,0:T(8,128)(2,1)S(1)}, bf16[2,720,128]{2,1,0:T(8,128)(2,1)S(1)}, u32[]{:S(2)}, u32[]{:S(2)}) collective-permute-start(bf16[2,720,128]{2,1,0:T(8,128)(2,1)S(1)} %constant_dynamic-update-slice_fusion.refs_0_), channel_id=1, source_target_pairs={{0,8},{1,17},{2,10},{3,19},{4,12},{5,21},{6,14},{7,23},{8,0},{9,25... | collective-permute-start | bytes 1105928 | tf_op jit(solution)/shard_map/ppermute | solution.py:74
  18.8 2.9 %collective-permute-start.12 = (bf16[2,720,128]{2,1,0:T(8,128)(2,1)S(1)}, bf16[2,720,128]{2,1,0:T(8,128)(2,1)S(1)}, u32[]{:S(2)}, u32[]{:S(2)}) collective-permute-start(bf16[2,720,128]{2,1,0:T(8,128)(2,1)S(1)} %collective-permute-done.10.refs_1_), channel_id=1, source_target_pairs={{0,1},{1,0},{2,3},{3,2},{4,5},{5,4},{6,7},{7,6},{8,9},{9,8},{10,11... | collective-permute-start | bytes 1105928 | tf_op jit(solution)/shard_map/ppermute | solution.py:74
  23.0 1.0 %shard_map.128 = (bf16[11520,128]{1,0:T(8,128)(2,1)S(1)}, bf16[1152,1280]{1,0:T(8,128)(2,1)S(1)}) custom-call(s32[33]{0:T(128)S(1)} %concatenate.12.table, bf16[2,720,128]{2,1,0:T(8,128)(2,1)S(1)} %pad_maximum_fusion.refs_0_, bf16[2,720,128]{2,1,0:T(8,128)(2,1)S(1)} %collective-permute-done.10.refs_1_, ...), custom_call_target="tpu_custom_call" | custom-call | tf_op jit(solution)/shard_map/pallas_call | solution.py:309
  24.7 1.2 %collective-permute-start.15 = (bf16[2,720,128]{2,1,0:T(8,128)(2,1)S(1)}, bf16[2,720,128]{2,1,0:T(8,128)(2,1)S(1)}, u32[]{:S(2)}, u32[]{:S(2)}) collective-permute-start(bf16[2,720,128]{2,1,0:T(8,128)(2,1)S(1)} %constant_dynamic-update-slice_fusion.2.refs_0_), channel_id=1, source_target_pairs={{0,16},{1,9},{2,18},{3,11},{4,20},{5,13},{6,22},{7,15},{8,24},{9,1... | collective-permute-start | bytes 1105928 | tf_op jit(solution)/shard_map/ppermute | solution.py:74
  26.2 2.6 %collective-permute-start.5 = (bf16[2,720,128]{2,1,0:T(8,128)(2,1)S(1)}, bf16[2,720,128]{2,1,0:T(8,128)(2,1)S(1)}, u32[]{:S(2)}, u32[]{:S(2)}) collective-permute-start(bf16[2,720,128]{2,1,0:T(8,128)(2,1)S(1)} %constant_dynamic-update-slice_fusion.refs_0_), channel_id=1, source_target_pairs={{0,1},{1,0},{2,3},{3,2},{4,5},{5,4},{6,7},{7,6},{8,9},{9,8},{10,11... | collective-permute-start | bytes 1105928 | tf_op jit(solution)/shard_map/ppermute | solution.py:74
  29.6 1.5 %collective-permute-done.4.refs_2_ = bf16[2,720,128]{2,1,0:T(8,128)(2,1)S(1)} collective-permute-done((bf16[2,720,128]{2,1,0:T(8,128)(2,1)S(1)}, bf16[2,720,128]{2,1,0:T(8,128)(2,1)S(1)}, u32[]{:S(2)}, u32[]{:S(2)}) %collective-permute-start.4) | collective-permute-done | bytes 368672 | tf_op jit(solution)/shard_map/ppermute | solution.py:74
  31.1 1.0 %collective-permute-start.14 = (bf16[2,720,128]{2,1,0:T(8,128)(2,1)S(1)}, bf16[2,720,128]{2,1,0:T(8,128)(2,1)S(1)}, u32[]{:S(2)}, u32[]{:S(2)}) collective-permute-start(bf16[2,720,128]{2,1,0:T(8,128)(2,1)S(1)} %collective-permute-done.4.refs_2_), channel_id=1, source_target_pairs={{0,1},{1,0},{2,3},{3,2},{4,5},{5,4},{6,7},{7,6},{8,9},{9,8},{10,11... | collective-permute-start | bytes 1105928 | tf_op jit(solution)/shard_map/ppermute | solution.py:74
  32.1 3.0 %collective-permute-done.15.refs_0_ = bf16[2,720,128]{2,1,0:T(8,128)(2,1)S(1)} collective-permute-done((bf16[2,720,128]{2,1,0:T(8,128)(2,1)S(1)}, bf16[2,720,128]{2,1,0:T(8,128)(2,1)S(1)}, u32[]{:S(2)}, u32[]{:S(2)}) %collective-permute-start.15) | collective-permute-done | bytes 368672 | tf_op jit(solution)/shard_map/ppermute | solution.py:74
  35.1 3.9 %collective-permute-done.3.refs_2_ = bf16[2,720,128]{2,1,0:T(8,128)(2,1)S(1)} collective-permute-done((bf16[2,720,128]{2,1,0:T(8,128)(2,1)S(1)}, bf16[2,720,128]{2,1,0:T(8,128)(2,1)S(1)}, u32[]{:S(2)}, u32[]{:S(2)}) %collective-permute-start.3) | collective-permute-done | bytes 368672 | tf_op jit(solution)/shard_map/ppermute | solution.py:74
  39.0 1.0 %collective-permute-start.16 = (bf16[2,720,128]{2,1,0:T(8,128)(2,1)S(1)}, bf16[2,720,128]{2,1,0:T(8,128)(2,1)S(1)}, u32[]{:S(2)}, u32[]{:S(2)}) collective-permute-start(bf16[2,720,128]{2,1,0:T(8,128)(2,1)S(1)} %collective-permute-done.15.refs_0_), channel_id=1, source_target_pairs={{0,1},{1,0},{2,3},{3,2},{4,5},{5,4},{6,7},{7,6},{8,9},{9,8},{10,11... | collective-permute-start | bytes 1105928 | tf_op jit(solution)/shard_map/ppermute | solution.py:74
  40.1 1.5 %shard_map.130 = (bf16[11520,128]{1,0:T(8,128)(2,1)S(1)}, bf16[1152,1280]{1,0:T(8,128)(2,1)S(1)}, bf16[512,1280]{1,0:T(8,128)(2,1)S(1)}, bf16[512,1280]{1,0:T(8,128)(2,1)S(1)}) custom-call(s32[33]{0:T(128)S(1)} %concatenate.12.table, ...), custom_call_target="tpu_custom_call", output_to_operand_aliasing={{0}: (7, {}), {1}: (8, {})} | custom-call | tf_op jit(solution)/shard_map/pallas_call | solution.py:309
  41.9 4.7 %shard_map.131 = (f32[2304,128]{1,0:T(8,128)S(1)}, bf16[2,2,72,128]{3,2,1,0:T(8,128)(2,1)S(1)}, bf16[2,2,72,128]{3,2,1,0:T(8,128)(2,1)S(1)}, bf16[11520,128]{1,0:T(8,128)(2,1)S(1)}, bf16[1152,1280]{1,0:T(8,128)(2,1)S(1)}) custom-call(s32[33]{0:T(128)S(1)} %concatenate.12.table, ...), custom_call_target="tpu_custom_call", output_to_operand_aliasing={{3}: (7, {}), {4}: (8, {})} | custom-call | tf_op jit(solution)/shard_map/pallas_call | solution.py:393
  47.0 2.0 %collective-permute-start.19 = (bf16[2,2,72,128]{3,2,1,0:T(8,128)(2,1)S(1)}, bf16[2,2,72,128]{3,2,1,0:T(8,128)(2,1)S(1)}, u32[]{:S(2)}, u32[]{:S(2)}) collective-permute-start(bf16[2,2,72,128]{3,2,1,0:T(8,128)(2,1)S(1)} %get-tuple-element.39), channel_id=1, source_target_pairs={{1,2},{2,1},{3,4},{4,3},{5,6},{6,5},{9,10},{10,9},{11,12},{12,11},... | collective-permute-start | bytes 221192 | tf_op jit(solution)/shard_map/ppermute | solution.py:74
  49.0 3.8 %collective-permute-done.19.outer = bf16[2,2,72,128]{3,2,1,0:T(8,128)(2,1)S(1)} collective-permute-done((bf16[2,2,72,128]{3,2,1,0:T(8,128)(2,1)S(1)}, bf16[2,2,72,128]{3,2,1,0:T(8,128)(2,1)S(1)}, u32[]{:S(2)}, u32[]{:S(2)}) %collective-permute-start.19) | collective-permute-done | bytes 73760 | tf_op jit(solution)/shard_map/ppermute | solution.py:74
  53.8 4.1 %collective-permute-start.21 = (bf16[2,2,4,16,128]{4,3,2,1,0:T(8,128)(2,1)S(1)}, bf16[2,2,4,16,128]{4,3,2,1,0:T(8,128)(2,1)S(1)}, u32[]{:S(2)}, u32[]{:S(2)}) collective-permute-start(bf16[2,2,4,16,128]{4,3,2,1,0:T(8,128)(2,1)S(1)} %get-tuple-element.42), channel_id=1, source_target_pairs={{8,16},{16,8},{9,17},{17,9},{10,18},{18,10},{11,19},{19,11},{12,20... | collective-permute-start | bytes 196616 | tf_op jit(solution)/shard_map/ppermute | solution.py:610
  57.9 3.1 %shard_map.133.refs_6_ = bf16[4,128,1280]{2,1,0:T(8,128)(2,1)} custom-call(s32[3]{0:T(128)S(1)} %pad_add_fusion.place.refs_0_, bf16[11520,128]{1,0:T(8,128)(2,1)S(1)} %get-tuple-element.36.refs_1_, f32[2304,128]{1,0:T(8,128)S(1)} %get-tuple-element.40.refs_2_, bf16[4,128,1280]{2,1,0:T(8,128)(2,1)S(1)} %bitcast.9), custom_call_target="tpu_custom_call" | custom-call | flops 1132462080 | bytes 2949120 | tf_op jit(solution)/shard_map/pallas_call | solution.py:583
  61.1 2.3 %shard_map.134 = bf16[4,128,1280]{2,1,0:T(8,128)(2,1)} custom-call(s32[3]{0:T(128)S(1)} %pad_add_fusion.place.refs_0_, bf16[11520,128]{1,0:T(8,128)(2,1)S(1)} %get-tuple-element.36.refs_1_, f32[2304,128]{1,0:T(8,128)S(1)} %get-tuple-element.40.refs_2_, ...), custom_call_target="tpu_custom_call", output_to_operand_aliasing={{}: (6, {})} | custom-call | flops 377487360 | bytes 2949120 | tf_op jit(solution)/shard_map/pallas_call | solution.py:583
  (48 shorter events, 10.2 us)
Async XLA Ops:
  2.0 10.4 %collective-permute-start = (bf16[1,720,128]{2,1,0:T(8,128)(2,1)S(1)}, bf16[1,720,128]{2,1,0:T(8,128)(2,1)S(1)}, u32[]{:S(2)}, u32[]{:S(2)}) collective-permute-start(bf16[1,720,128]{2,1,0:T(8,128)(2,1)S(1)} %shard_map.127), channel_id=1, source_target_pairs={{0,4},{1,5},{2,6},{3,7},{4,0},{5,1},{6,2},{7,3},{8,12},{9,13},{10,... | collective-permute-start | bytes 552968 | tf_op jit(solution)/shard_map/ppermute | solution.py:74
  4.4 10.9 %collective-permute-start.7 = (bf16[1,720,128]{2,1,0:T(8,128)(2,1)S(1)}, bf16[1,720,128]{2,1,0:T(8,128)(2,1)S(1)}, u32[]{:S(2)}, u32[]{:S(2)}) collective-permute-start(bf16[1,720,128]{2,1,0:T(8,128)(2,1)S(1)} %shard_map.127), channel_id=1, source_target_pairs={{0,2},{1,3},{2,0},{3,1},{4,6},{5,7},{6,4},{7,5},{8,10},{9,11},{10,... | collective-permute-start | bytes 552968 | tf_op jit(solution)/shard_map/ppermute | solution.py:74
  5.7 4.7 %collective-permute-start.9 = (bf16[1,720,128]{2,1,0:T(8,128)(2,1)S(1)}, bf16[1,720,128]{2,1,0:T(8,128)(2,1)S(1)}, u32[]{:S(2)}, u32[]{:S(2)}) collective-permute-start(bf16[1,720,128]{2,1,0:T(8,128)(2,1)S(1)} %shard_map.127), channel_id=1, source_target_pairs={{0,8},{1,17},{2,10},{3,19},{4,12},{5,21},{6,14},{7,23},{8,0},{9,25... | collective-permute-start | bytes 552968 | tf_op jit(solution)/shard_map/ppermute | solution.py:74
  10.4 8.3 %collective-permute-start.10 = (bf16[2,720,128]{2,1,0:T(8,128)(2,1)S(1)}, bf16[2,720,128]{2,1,0:T(8,128)(2,1)S(1)}, u32[]{:S(2)}, u32[]{:S(2)}) collective-permute-start(bf16[2,720,128]{2,1,0:T(8,128)(2,1)S(1)} %pad_maximum_fusion.refs_0_), channel_id=1, source_target_pairs={{0,16},{1,9},{2,18},{3,11},{4,20},{5,13},{6,22},{7,15},{8,24},{9,1... | collective-permute-start | bytes 1105928 | tf_op jit(solution)/shard_map/ppermute | solution.py:74
  12.5 4.9 %collective-permute-start.1 = (bf16[1,720,128]{2,1,0:T(8,128)(2,1)S(1)}, bf16[1,720,128]{2,1,0:T(8,128)(2,1)S(1)}, u32[]{:S(2)}, u32[]{:S(2)}) collective-permute-start(bf16[1,720,128]{2,1,0:T(8,128)(2,1)S(1)} %collective-permute-done), channel_id=1, source_target_pairs={{0,2},{1,3},{2,0},{3,1},{4,6},{5,7},{6,4},{7,5},{8,10},{9,11},{10,... | collective-permute-start | bytes 552968 | tf_op jit(solution)/shard_map/ppermute | solution.py:74
  14.6 7.5 %collective-permute-start.11 = (bf16[2,720,128]{2,1,0:T(8,128)(2,1)S(1)}, bf16[2,720,128]{2,1,0:T(8,128)(2,1)S(1)}, u32[]{:S(2)}, u32[]{:S(2)}) collective-permute-start(bf16[2,720,128]{2,1,0:T(8,128)(2,1)S(1)} %pad_maximum_fusion.refs_0_), channel_id=1, source_target_pairs={{0,1},{1,0},{2,3},{3,2},{4,5},{5,4},{6,7},{7,6},{8,9},{9,8},{10,11... | collective-permute-start | bytes 1105928 | tf_op jit(solution)/shard_map/ppermute | solution.py:74
  15.3 6.7 %collective-permute-start.8 = (bf16[1,720,128]{2,1,0:T(8,128)(2,1)S(1)}, bf16[1,720,128]{2,1,0:T(8,128)(2,1)S(1)}, u32[]{:S(2)}, u32[]{:S(2)}) collective-permute-start(bf16[1,720,128]{2,1,0:T(8,128)(2,1)S(1)} %collective-permute-done.7), channel_id=1, source_target_pairs={{0,8},{1,17},{2,10},{3,19},{4,12},{5,21},{6,14},{7,23},{8,0},{9,25... | collective-permute-start | bytes 552968 | tf_op jit(solution)/shard_map/ppermute | solution.py:74
  17.4 8.5 %collective-permute-start.2 = (bf16[2,720,128]{2,1,0:T(8,128)(2,1)S(1)}, bf16[2,720,128]{2,1,0:T(8,128)(2,1)S(1)}, u32[]{:S(2)}, u32[]{:S(2)}) collective-permute-start(bf16[2,720,128]{2,1,0:T(8,128)(2,1)S(1)} %constant_dynamic-update-slice_fusion.refs_0_), channel_id=1, source_target_pairs={{0,8},{1,17},{2,10},{3,19},{4,12},{5,21},{6,14},{7,23},{8,0},{9,25... | collective-permute-start | bytes 1105928 | tf_op jit(solution)/shard_map/ppermute | solution.py:74
  18.8 4.3 %collective-permute-start.12 = (bf16[2,720,128]{2,1,0:T(8,128)(2,1)S(1)}, bf16[2,720,128]{2,1,0:T(8,128)(2,1)S(1)}, u32[]{:S(2)}, u32[]{:S(2)}) collective-permute-start(bf16[2,720,128]{2,1,0:T(8,128)(2,1)S(1)} %collective-permute-done.10.refs_1_), channel_id=1, source_target_pairs={{0,1},{1,0},{2,3},{3,2},{4,5},{5,4},{6,7},{7,6},{8,9},{9,8},{10,11... | collective-permute-start | bytes 1105928 | tf_op jit(solution)/shard_map/ppermute | solution.py:74
  24.0 4.7 %collective-permute-start.13 = (bf16[2,720,128]{2,1,0:T(8,128)(2,1)S(1)}, bf16[2,720,128]{2,1,0:T(8,128)(2,1)S(1)}, u32[]{:S(2)}, u32[]{:S(2)}) collective-permute-start(bf16[2,720,128]{2,1,0:T(8,128)(2,1)S(1)} %constant_dynamic-update-slice_fusion.2.refs_0_), channel_id=1, source_target_pairs={{0,1},{1,0},{2,3},{3,2},{4,5},{5,4},{6,7},{7,6},{8,9},{9,8},{10,11... | collective-permute-start | bytes 1105928 | tf_op jit(solution)/shard_map/ppermute | solution.py:74
  24.5 6.7 %collective-permute-start.4 = (bf16[2,720,128]{2,1,0:T(8,128)(2,1)S(1)}, bf16[2,720,128]{2,1,0:T(8,128)(2,1)S(1)}, u32[]{:S(2)}, u32[]{:S(2)}) collective-permute-start(bf16[2,720,128]{2,1,0:T(8,128)(2,1)S(1)} %constant_dynamic-update-slice_fusion.refs_0_), channel_id=1, source_target_pairs={{0,16},{1,9},{2,18},{3,11},{4,20},{5,13},{6,22},{7,15},{8,24},{9,1... | collective-permute-start | bytes 1105928 | tf_op jit(solution)/shard_map/ppermute | solution.py:74
  24.7 10.4 %collective-permute-start.15 = (bf16[2,720,128]{2,1,0:T(8,128)(2,1)S(1)}, bf16[2,720,128]{2,1,0:T(8,128)(2,1)S(1)}, u32[]{:S(2)}, u32[]{:S(2)}) collective-permute-start(bf16[2,720,128]{2,1,0:T(8,128)(2,1)S(1)} %constant_dynamic-update-slice_fusion.2.refs_0_), channel_id=1, source_target_pairs={{0,16},{1,9},{2,18},{3,11},{4,20},{5,13},{6,22},{7,15},{8,24},{9,1... | collective-permute-start | bytes 1105928 | tf_op jit(solution)/shard_map/ppermute | solution.py:74
  26.0 13.1 %collective-permute-start.3 = (bf16[2,720,128]{2,1,0:T(8,128)(2,1)S(1)}, bf16[2,720,128]{2,1,0:T(8,128)(2,1)S(1)}, u32[]{:S(2)}, u32[]{:S(2)}) collective-permute-start(bf16[2,720,128]{2,1,0:T(8,128)(2,1)S(1)} %collective-permute-done.2.refs_1_), channel_id=1, source_target_pairs={{0,16},{1,9},{2,18},{3,11},{4,20},{5,13},{6,22},{7,15},{8,24},{9,1... | collective-permute-start | bytes 1105928 | tf_op jit(solution)/shard_map/ppermute | solution.py:74
  26.2 13.8 %collective-permute-start.5 = (bf16[2,720,128]{2,1,0:T(8,128)(2,1)S(1)}, bf16[2,720,128]{2,1,0:T(8,128)(2,1)S(1)}, u32[]{:S(2)}, u32[]{:S(2)}) collective-permute-start(bf16[2,720,128]{2,1,0:T(8,128)(2,1)S(1)} %constant_dynamic-update-slice_fusion.refs_0_), channel_id=1, source_target_pairs={{0,1},{1,0},{2,3},{3,2},{4,5},{5,4},{6,7},{7,6},{8,9},{9,8},{10,11... | collective-permute-start | bytes 1105928 | tf_op jit(solution)/shard_map/ppermute | solution.py:74
  28.8 11.3 %collective-permute-start.6 = (bf16[2,720,128]{2,1,0:T(8,128)(2,1)S(1)}, bf16[2,720,128]{2,1,0:T(8,128)(2,1)S(1)}, u32[]{:S(2)}, u32[]{:S(2)}) collective-permute-start(bf16[2,720,128]{2,1,0:T(8,128)(2,1)S(1)} %collective-permute-done.2.refs_1_), channel_id=1, source_target_pairs={{0,1},{1,0},{2,3},{3,2},{4,5},{5,4},{6,7},{7,6},{8,9},{9,8},{10,11... | collective-permute-start | bytes 1105928 | tf_op jit(solution)/shard_map/ppermute | solution.py:74
  28.8 11.3 %copy-start = (bf16[4,16,8,1280]{3,2,1,0:T(8,128)(2,1)S(1)}, bf16[4,16,8,1280]{3,2,1,0:T(8,128)(2,1)}, u32[]{:S(2)}) copy-start(bf16[4,16,8,1280]{3,2,1,0:T(8,128)(2,1)} %param.13) | copy-start | bytes 3932164
  28.8 11.3 %copy-start.1 = (bf16[4,16,8,1280]{3,2,1,0:T(8,128)(2,1)S(1)}, bf16[4,16,8,1280]{3,2,1,0:T(8,128)(2,1)}, u32[]{:S(2)}) copy-start(bf16[4,16,8,1280]{3,2,1,0:T(8,128)(2,1)} %param.14) | copy-start | bytes 3932164
  31.1 8.9 %collective-permute-start.14 = (bf16[2,720,128]{2,1,0:T(8,128)(2,1)S(1)}, bf16[2,720,128]{2,1,0:T(8,128)(2,1)S(1)}, u32[]{:S(2)}, u32[]{:S(2)}) collective-permute-start(bf16[2,720,128]{2,1,0:T(8,128)(2,1)S(1)} %collective-permute-done.4.refs_2_), channel_id=1, source_target_pairs={{0,1},{1,0},{2,3},{3,2},{4,5},{5,4},{6,7},{7,6},{8,9},{9,8},{10,11... | collective-permute-start | bytes 1105928 | tf_op jit(solution)/shard_map/ppermute | solution.py:74
  39.0 2.5 %collective-permute-start.16 = (bf16[2,720,128]{2,1,0:T(8,128)(2,1)S(1)}, bf16[2,720,128]{2,1,0:T(8,128)(2,1)S(1)}, u32[]{:S(2)}, u32[]{:S(2)}) collective-permute-start(bf16[2,720,128]{2,1,0:T(8,128)(2,1)S(1)} %collective-permute-done.15.refs_0_), channel_id=1, source_target_pairs={{0,1},{1,0},{2,3},{3,2},{4,5},{5,4},{6,7},{7,6},{8,9},{9,8},{10,11... | collective-permute-start | bytes 1105928 | tf_op jit(solution)/shard_map/ppermute | solution.py:74
  40.0 1.8 %collective-permute-start.17 = (bf16[2,720,128]{2,1,0:T(8,128)(2,1)S(1)}, bf16[2,720,128]{2,1,0:T(8,128)(2,1)S(1)}, u32[]{:S(2)}, u32[]{:S(2)}) collective-permute-start(bf16[2,720,128]{2,1,0:T(8,128)(2,1)S(1)} %collective-permute-done.3.refs_2_), channel_id=1, source_target_pairs={{0,1},{1,0},{2,3},{3,2},{4,5},{5,4},{6,7},{7,6},{8,9},{9,8},{10,11... | collective-permute-start | bytes 1105928 | tf_op jit(solution)/shard_map/ppermute | solution.py:74
  46.5 2.5 %collective-permute-start.18 = (bf16[2,2,72,128]{3,2,1,0:T(8,128)(2,1)S(1)}, bf16[2,2,72,128]{3,2,1,0:T(8,128)(2,1)S(1)}, u32[]{:S(2)}, u32[]{:S(2)}) collective-permute-start(bf16[2,2,72,128]{3,2,1,0:T(8,128)(2,1)S(1)} %get-tuple-element.38), channel_id=1, source_target_pairs={{0,1},{1,0},{2,3},{3,2},{4,5},{5,4},{6,7},{7,6},{8,9},{9,8},{10,11... | collective-permute-start | bytes 221192 | tf_op jit(solution)/shard_map/ppermute | solution.py:74
  47.0 5.9 %collective-permute-start.19 = (bf16[2,2,72,128]{3,2,1,0:T(8,128)(2,1)S(1)}, bf16[2,2,72,128]{3,2,1,0:T(8,128)(2,1)S(1)}, u32[]{:S(2)}, u32[]{:S(2)}) collective-permute-start(bf16[2,2,72,128]{3,2,1,0:T(8,128)(2,1)S(1)} %get-tuple-element.39), channel_id=1, source_target_pairs={{1,2},{2,1},{3,4},{4,3},{5,6},{6,5},{9,10},{10,9},{11,12},{12,11},... | collective-permute-start | bytes 221192 | tf_op jit(solution)/shard_map/ppermute | solution.py:74
  53.5 7.5 %collective-permute-start.20 = (bf16[2,2,4,16,128]{4,3,2,1,0:T(8,128)(2,1)S(1)}, bf16[2,2,4,16,128]{4,3,2,1,0:T(8,128)(2,1)S(1)}, u32[]{:S(2)}, u32[]{:S(2)}) collective-permute-start(bf16[2,2,4,16,128]{4,3,2,1,0:T(8,128)(2,1)S(1)} %get-tuple-element.41), channel_id=1, source_target_pairs={{0,8},{8,0},{16,24},{24,16},{1,9},{9,1},{17,25},{25,17},{2,10},{10... | collective-permute-start | bytes 196616 | tf_op jit(solution)/shard_map/ppermute | solution.py:610
  53.8 7.2 %collective-permute-start.21 = (bf16[2,2,4,16,128]{4,3,2,1,0:T(8,128)(2,1)S(1)}, bf16[2,2,4,16,128]{4,3,2,1,0:T(8,128)(2,1)S(1)}, u32[]{:S(2)}, u32[]{:S(2)}) collective-permute-start(bf16[2,2,4,16,128]{4,3,2,1,0:T(8,128)(2,1)S(1)} %get-tuple-element.42), channel_id=1, source_target_pairs={{8,16},{16,8},{9,17},{17,9},{10,18},{18,10},{11,19},{19,11},{12,20... | collective-permute-start | bytes 196616 | tf_op jit(solution)/shard_map/ppermute | solution.py:610
  (2 other events, 1.8 us)

commit v4 on v3

--- a/solution.py
+++ b/solution.py
@@ -11,11 +11,13 @@
 PLAN = {
     "far_half": True,
     "modes": {"c": "cat", "d": "sep", "o": "cat"},
-    "holds": {},
+    "holds": {"z3": ("z2",)},
     "early": ("o", "c", "d"),
     "pin": True,
     "late": 1,
-    "late_c": 1,
+    "late_c": 0,
+    "cut": 1,
+    "wait_c": "d2",
     "table": "d2",
     "costs": (0, 0),
 }
@@ -145,10 +147,15 @@
             if PLAN["modes"][name] == "cat":
                 parts = [parts[0] if step == 0 else jnp.concatenate(parts, axis=0)]
             new = []
-            for part in parts:
+            for n, part in enumerate(parts):
                 key = f"{name}{count}"
-                found[key] = double_rows(geo, ready(key, part), step)
-                new.append(found[key])
+                part = ready(key, part)
+                if name == "d" and step == steps - 1 and n == len(parts) - 1:
+                    found[key] = double_rows(geo, part[:, : geo.deep1], step)
+                    new += [found[key], double_rows(geo, part[:, geo.deep1 :], step)]
+                else:
+                    found[key] = double_rows(geo, part, step)
+                    new.append(found[key])
                 count += 1
             parts = parts + new
         return parts
@@ -231,17 +238,19 @@
 def weights_calls(geo, table, groups, found, tiles):
     start = 1
     entries = {}
-    last = list(groups)[-1]
-    for name, arrays in groups.items():
+    *_, name = groups
+    *groups[name], second = groups[name]
+    first = groups[name][-1]
+    for group, arrays in groups.items():
         total = sum(y.shape[0] for y in arrays)
         at = start
-        entries[name] = []
+        entries[group] = []
         for y in arrays:
-            entries[name].append((at, total, y))
+            entries[group].append((at, total, y))
             at += y.shape[0]
         start += 2 * total
 
-    def both(some, wait):
+    def both(some, wait=None):
         theirs = [
             swap_cores(geo, after(y, wait) if wait is not None and n == len(some) - 1 else y)
             for n, (_, _, y) in enumerate(some)
@@ -250,25 +259,25 @@
             (at + total, 1, y) for (at, total, _), y in zip(some, theirs)
         ]
 
-    final = groups[last][-1]
-    late = entries[last][-PLAN["late"] :]
-    entries[last] = entries[last][: -PLAN["late"]]
+    at, total, _ = entries[name].pop()
     before = []
     if PLAN["late_c"] and len(groups) == 3:
-        before = entries["c"][-1:]
-        entries["c"] = entries["c"][:-1]
+        before = [entries["c"].pop()]
     weights = []
     for names in PLAN["early"]:
         pieces = []
         is_last = names == PLAN["early"][-1]
         loads = tiles if is_last else ()
         here = after(table, found[PLAN["table"]]) if is_last and PLAN["table"] in found else table
-        for name in names:
-            if entries.get(name):
-                pieces += both(entries[name], weights[0] if weights and PLAN["pin"] else None)
+        for group in names:
+            if entries.get(group):
+                pieces += both(entries[group], weights[0] if weights and PLAN["pin"] else None)
         if pieces:
             weights = early_call(geo, here, pieces, weights[:2], loads)
-    return weights[:2], weights[2:], both(before, final) + both(late, None)
+    firsts = both(before, found.get(PLAN["wait_c"]))
+    for n in range(0, first.shape[0], PLAN["cut"]):
+        firsts += both([(at + n, total, first[n : n + PLAN["cut"]])])
+    return weights[:2], weights[2:], firsts, lambda ext: both([(at, total, second)], ext)
 
 
 def weights_shapes(geo):
@@ -361,35 +370,24 @@
     return ext[pl.ds(part * geo.plane + j, geo.lines, stride=geo.wide), :]
 
 
-def partial_call(geo, table, x, cot, weights, pieces=()):
-    ext = jax.ShapeDtypeStruct((4 * geo.plane, geo.mid), jnp.float32)
-    edge = jax.ShapeDtypeStruct((2, 2, geo.lines, geo.mid), jnp.bfloat16)
+def first_call(geo, table, x, weights, pieces=()):
+    ext = jax.ShapeDtypeStruct((2 * geo.plane, geo.mid), jnp.float32)
     arrays = [y for _, _, y in pieces]
-    count = len(arrays)
-
-    def kernel(table, x, cot, *refs):
+
+    def kernel(table, x, *refs):
         acc = refs[-1]
-        outs = refs[count + len(weights) : -1]
-        exts = [outs[0].at[pl.ds(kind * 2 * geo.plane, 2 * geo.plane)] for kind in range(2)]
-        edges = outs[1:3]
-        placed = outs[3:] if pieces else refs[:2]
-        for (start, source, _), ref in zip(pieces, refs):
-            place_array(geo, table, start, source, ref, *placed)
-        for kind in range(2):
-            partial_convolution(geo, kind, placed[kind], (x, cot)[kind], exts[kind], acc)
-        left, right = ((1, geo.wide - 1), (0, 0)), ((0, geo.wide - 1), (1, 0))
-        core = table[0]
-        for out, is_right in zip(edges, (core == 0, core != 0)):
-            for kind, plane in enumerate(exts):
-                for n in range(2):
-                    value = jnp.where(
-                        is_right, column(geo, plane, *right[n]), column(geo, plane, *left[n])
-                    )
-                    out[kind, n] = value.astype(jnp.bfloat16)
-
-    args = [table, x, cot, *arrays, *weights]
-    outs = [ext, edge, edge] + (weights_shapes(geo) if pieces else [])
-    alias = {3 + count + n: 3 + n for n in range(len(weights))}
+        if pieces:
+            ext, k1s, k2s = refs[-4:-1]
+            for (start, source, _), ref in zip(pieces, refs):
+                both = ref.shape[1] > geo.deep1
+                place_array(geo, table, start, source, ref, k1s, k2s if both else None)
+        else:
+            k1s, ext = refs[0], refs[-2]
+        partial_convolution(geo, 0, k1s, x, ext, acc)
+
+    args = [table, x, *arrays, *weights]
+    outs = [ext] + (weights_shapes(geo) if pieces else [])
+    alias = {2 + len(arrays) + n: 1 + n for n in range(len(weights))}
     return pl.pallas_call(
         kernel,
         out_shape=outs,
@@ -399,11 +397,51 @@
         input_output_aliases=alias if pieces else {},
         compiler_params=parameters(),
         cost_estimate=pl.CostEstimate(
-            flops=PLAN["costs"][1] * 4 * geo.pixels * TAPS * TAPS * geo.chan * geo.mid,
-            bytes_accessed=PLAN["costs"][1] * 4 * TAPS * TAPS * geo.chan * geo.mid,
+            flops=PLAN["costs"][1] * 2 * geo.pixels * TAPS * TAPS * geo.chan * geo.mid,
+            bytes_accessed=PLAN["costs"][1] * 2 * TAPS * TAPS * geo.chan * geo.mid,
             transcendentals=0,
         ),
     )(*args)
+
+
+def back_call(geo, table, cot, ext_pre, k2, pieces=()):
+    ext = jax.ShapeDtypeStruct((2 * geo.plane, geo.mid), jnp.float32)
+    edge = jax.ShapeDtypeStruct((2, 2, geo.lines, geo.mid), jnp.bfloat16)
+    arrays = [x for _, _, x in pieces]
+    count = len(arrays)
+
+    def kernel(table, cot, ext_pre, *refs):
+        ext, inner, outer = refs[count + 1 : count + 4]
+        k2s = refs[-2] if count else refs[0]
+        for (start, source, _), ref in zip(pieces, refs):
+            place_array(geo, table, start, source, ref, None, k2s)
+        partial_convolution(geo, 1, k2s, cot, ext, refs[-1])
+        left, right = ((1, geo.wide - 1), (0, 0)), ((0, geo.wide - 1), (1, 0))
+        core = table[0]
+        for out, is_right in ((inner, core == 0), (outer, core != 0)):
+            for kind, plane in enumerate((ext_pre, ext)):
+                for n in range(2):
+                    value = jnp.where(
+                        is_right, column(geo, plane, *right[n]), column(geo, plane, *left[n])
+                    )
+                    out[kind, n] = value.astype(jnp.bfloat16)
+
+    outs = [ext, edge, edge] + (weights_shapes(geo)[1:] if count else [])
+    args = [table, cot, ext_pre, *arrays, k2]
+    return pl.pallas_call(
+        kernel,
+        out_shape=outs,
+        in_specs=[smem()] + [whole(a) for a in args[1:]],
+        out_specs=[whole(o) for o in outs],
+        scratch_shapes=[pltpu.VMEM((TAPS, geo.batch, geo.ext, geo.wide, geo.mid), jnp.float32)],
+        input_output_aliases={3 + count: 3} if count else {},
+        compiler_params=parameters(),
+        cost_estimate=pl.CostEstimate(
+            flops=2 * geo.pixels * TAPS * TAPS * geo.chan * geo.mid,
+            bytes_accessed=2 * TAPS * TAPS * geo.chan * geo.mid,
+            transcendentals=0,
+        ),
+    )(*args)[:3]
 
 
 def beside(geo, inner, outer):
@@ -416,19 +454,18 @@
     return send(inner, swap), send(outer, pairs)
 
 
-def join_call(geo, place, ext, inner, outer):
-    full = jax.ShapeDtypeStruct((4 * geo.plane, geo.mid), jnp.float32)
+def join_call(geo, place, ext_pre, ext_back, inner, outer):
+    full = jax.ShapeDtypeStruct((2 * geo.plane, geo.mid), jnp.float32)
     strip = jax.ShapeDtypeStruct((2, 2, geo.batch, 2 * geo.wide, geo.mid), jnp.bfloat16)
 
-    def kernel(place, ext, inner, outer, full, near_strip, next_strip):
+    def kernel(place, _, __, inner, outer, pre, back, near_strip, next_strip):
         core = place[0]
         even = place[1] % 2 == 0
         wide = geo.wide
-        for kind in range(2):
-            base = kind * 2 * geo.plane
+        for kind, full in enumerate((pre, back)):
 
             def add(part, j, value):
-                at = pl.ds(base + part * geo.plane + j, geo.lines, stride=wide)
+                at = pl.ds(part * geo.plane + j, geo.lines, stride=wide)
                 full[at, :] = full[at, :] + value
 
             near = [inner[kind, n].astype(jnp.float32) for n in range(2)]
@@ -441,19 +478,19 @@
             add(1, 0, right[1])
             for part in range(2):
                 for b in range(geo.batch):
-                    top = base + part * geo.plane + b * geo.ext * wide
+                    top = part * geo.plane + b * geo.ext * wide
                     for out, low in ((near_strip, even), (next_strip, jnp.logical_not(even))):
                         line = pl.multiple_of(top + jnp.where(low, geo.high * wide, 0), 8)
                         two = full[pl.ds(line, 2 * wide), :]
                         out[kind, part, b] = two.astype(jnp.bfloat16)
 
-    args = [place, ext, inner, outer]
+    args = [place, ext_pre, ext_back, inner, outer]
     return pl.pallas_call(
         kernel,
-        out_shape=[full, strip, strip],
+        out_shape=[full, full, strip, strip],
         in_specs=[smem()] + [whole(a) for a in args[1:]],
-        out_specs=[whole(o) for o in (full, strip, strip)],
-        input_output_aliases={1: 0},
+        out_specs=[whole(o) for o in (full, full, strip, strip)],
+        input_output_aliases={1: 0, 2: 1},
         compiler_params=parameters(),
     )(*args)
 
@@ -533,13 +570,13 @@
         store.wait()
 
 
-def inner_kernel(geo, place, k1s, ext, cot, out, shifted, lhs, tiles, sems):
+def inner_kernel(geo, place, k1s, pre, back, cot, out, shifted, lhs, tiles, sems):
     wide, mid, high = geo.wide, geo.mid, geo.high
+    exts = (pre, back)
     count = geo.ext - 4
 
     def full(kind, part):
-        base = (kind * 2 + part) * geo.plane
-        plane = ext[pl.ds(base, geo.plane), :].reshape(geo.batch, geo.ext, wide, mid)
+        plane = exts[kind][pl.ds(part * geo.plane, geo.plane), :].reshape(geo.batch, geo.ext, wide, mid)
         return plane[:, 2 : 2 + count]
 
     gradient(geo, place, full, (2, count), shifted)
@@ -547,16 +584,16 @@
     convolve_back(geo, lhs, k1s, cot, [(2 * wide, (high - 4) * wide)], out, tiles, sems)
 
 
-def outer_kernel(geo, place, k1s, ext, near_strip, next_strip, cot, given, out, shifted, lhs, tiles, sems):
+def outer_kernel(geo, place, k1s, pre, back, near_strip, next_strip, cot, given, out, shifted, lhs, tiles, sems):
     wide, mid, high = geo.wide, geo.mid, geo.high
+    exts = (pre, back)
     two = (geo.batch, 2, wide, mid)
     even = place[1] % 2 == 0
     for first in (0, geo.ext - 4):
         near = jnp.logical_xor(even, first == 0)
 
         def full(kind, part):
-            base = (kind * 2 + part) * geo.plane
-            plane = ext[pl.ds(base, geo.plane), :].reshape(geo.batch, geo.ext, wide, mid)
+            plane = exts[kind][pl.ds(part * geo.plane, geo.plane), :].reshape(geo.batch, geo.ext, wide, mid)
             plane = plane[:, first : first + 4]
             got = jnp.where(
                 near,
@@ -572,7 +609,7 @@
     convolve_back(geo, lhs, k1s, cot, spans, out, tiles, sems)
 
 
-def second_calls(geo, place, k1, ext, near_strip, next_strip, cot):
+def second_calls(geo, place, k1, pre, back, near_strip, next_strip, cot):
     taps = TAPS * TAPS
     image = (geo.batch, geo.high * geo.wide, geo.chan)
     out = jax.ShapeDtypeStruct(image, jnp.bfloat16)
@@ -600,8 +637,8 @@
             ),
         )(*args, cot, *given)
 
-    inner = call(inner_kernel, [place, k1, ext], geo.high - 4, [])
-    return call(outer_kernel, [place, k1, ext, near_strip, next_strip], 4, [inner])
+    inner = call(inner_kernel, [place, k1, pre, back], geo.high - 4, [])
+    return call(outer_kernel, [place, k1, pre, back, near_strip, next_strip], 4, [inner])
 
 
 def along_rows(geo, near_strip, next_strip):
@@ -620,15 +657,17 @@
     if geo.pieces_fit():
         groups, found = gather_pieces(geo, w_in, w_out)
         table = chip_table(geo, core)
-        weights, (x, cot), pieces = weights_calls(geo, table, groups, found, (x, cot))
-        ext, inner, outer, k1, _ = partial_call(geo, table, x, cot, weights, pieces)
+        weights, (x, cot), firsts, seconds = weights_calls(geo, table, groups, found, (x, cot))
+        ext_pre, k1, k2 = first_call(geo, table, x, weights, firsts)
+        ext_back, inner, outer = back_call(geo, table, cot, ext_pre, k2, seconds(ext_pre))
     else:
         k1 = lax.all_gather(w_in, AXES, axis=0, tiled=True).reshape(-1, geo.mid)
         k2 = lax.all_gather(w_out, AXES, axis=0, tiled=True).reshape(-1, geo.chan)
-        ext, inner, outer = partial_call(geo, place, x, cot, [k1, k2])
+        (ext_pre,) = first_call(geo, place, x, [k1])
+        ext_back, inner, outer = back_call(geo, place, cot, ext_pre, k2)
     inner, outer = beside(geo, inner, outer)
-    full, *strips = join_call(geo, place, ext, inner, outer)
-    out = second_calls(geo, place, k1, full, *along_rows(geo, *strips), cot)
+    pre, back, *strips = join_call(geo, place, ext_pre, ext_back, inner, outer)
+    out = second_calls(geo, place, k1, pre, back, *along_rows(geo, *strips), cot)
     return out.reshape(inputs.shape)
 
 

time: 63.6 us -> 63.5 us (level)
  starting transfers between devices: 26.4 us -> 22.3 us
  waiting for transfers between devices: 18.8 us -> 21.5 us
  Pallas kernels: 14.3 us -> 15.1 us
    ppermute x20 -> x23, starting transfers between devices: 22 us -> 18.8 us  [send(): return lax.ppermute(x, AXES, perm)]
    ppermute x20 -> x23, waiting for transfers between devices: 18.8 us -> 21.4 us  [send(): return lax.ppermute(x, AXES, perm)]
    ppermute x1, starting transfers between devices: 4.07 us -> 3.25 us  [along_rows(): lax.ppermute(next_strip, 'row', between)]
    pallas_call x2 -> x3, Pallas kernels: 5.32 us -> 5.86 us  [the longest x1 2.7 us: back_call(): pl.pallas_call(kernel, out_shape=outs, in_specs=[smem()] + [whole(a) for...]
  transfers between devices with their start and end apart: 22 -> 25, of which waited for: 9 -> 8; matrix products, arithmetic and copies ran while one was open for 3% -> 3% of each run, Pallas kernels for 10% -> 15%
where the time goes in v4:
time: 63.5 us; the launch traced here: 62.7 us
  starting transfers between devices  22.3 us (35%)
  waiting for transfers between devices  21.5 us (34%)
  Pallas kernels  15.1 us (24%)
  local copies, waits for them, and re-layouts  2.16 us (3%)
  other arithmetic  1.51 us (2%)
    ppermute x23, waiting for transfers between devices, send(): return lax.ppermute(x, AXES, perm)  21.4 us
    ppermute x23, starting transfers between devices, send(): return lax.ppermute(x, AXES, perm)  18.8 us
    pallas_call x2, Pallas kernels, call(): pl.pallas_call(lambda *refs: kernel(geo, *refs), out_shape=out, in_specs=...  5.42 us
    pallas_call x3, Pallas kernels, early_call(): pl.pallas_call(kernel, out_shape=outs, in_specs=[smem()] + [whole(x) for...  3.55 us
    ppermute x1, starting transfers between devices, along_rows(): lax.ppermute(next_strip, 'row', between)  3.25 us
    pallas_call x1, Pallas kernels, back_call(): pl.pallas_call(kernel, out_shape=outs, in_specs=[smem()] + [whole(a) for...  2.7 us
    pallas_call x1, Pallas kernels, first_call(): pl.pallas_call(kernel, out_shape=outs, in_specs=[smem()] + [whole(a) for...  2.51 us
    unnamed x10, local copies, waits for them, and re-layouts  1.82 us
  transfers between devices with their start and end apart: 25, of which 8 were waited for; matrix products, arithmetic and copies ran while one was open for 3% of the time, Pallas kernels for 15%

profile of v4, /device:TPU:3, one launch (start us, length us, event | category | flops | bytes accessed | tf_op | source)
XLA Modules:
  0.0 62.7 jit_solution(17771574001646260915)
XLA Ops:
  2.0 2.4 %collective-permute-start = (bf16[1,720,128]{2,1,0:T(8,128)(2,1)S(1)}, bf16[1,720,128]{2,1,0:T(8,128)(2,1)S(1)}, u32[]{:S(2)}, u32[]{:S(2)}) collective-permute-start(bf16[1,720,128]{2,1,0:T(8,128)(2,1)S(1)} %shard_map.127), channel_id=1, source_target_pairs={{0,4},{1,5},{2,6},{3,7},{4,0},{5,1},{6,2},{7,3},{8,12},{9,13},{10,... | collective-permute-start | bytes 552968 | tf_op jit(solution)/shard_map/ppermute | solution.py:76
  4.4 1.3 %collective-permute-start.7 = (bf16[1,720,128]{2,1,0:T(8,128)(2,1)S(1)}, bf16[1,720,128]{2,1,0:T(8,128)(2,1)S(1)}, u32[]{:S(2)}, u32[]{:S(2)}) collective-permute-start(bf16[1,720,128]{2,1,0:T(8,128)(2,1)S(1)} %shard_map.127), channel_id=1, source_target_pairs={{0,2},{1,3},{2,0},{3,1},{4,6},{5,7},{6,4},{7,5},{8,10},{9,11},{10,... | collective-permute-start | bytes 552968 | tf_op jit(solution)/shard_map/ppermute | solution.py:76
  5.7 1.2 %collective-permute-start.11 = (bf16[1,720,128]{2,1,0:T(8,128)(2,1)S(1)}, bf16[1,720,128]{2,1,0:T(8,128)(2,1)S(1)}, u32[]{:S(2)}, u32[]{:S(2)}) collective-permute-start(bf16[1,720,128]{2,1,0:T(8,128)(2,1)S(1)} %shard_map.127), channel_id=1, source_target_pairs={{0,8},{1,17},{2,10},{3,19},{4,12},{5,21},{6,14},{7,23},{8,0},{9,25... | collective-permute-start | bytes 552968 | tf_op jit(solution)/shard_map/ppermute | solution.py:76
  7.6 2.8 %collective-permute-done.11 = bf16[1,720,128]{2,1,0:T(8,128)(2,1)S(1)} collective-permute-done((bf16[1,720,128]{2,1,0:T(8,128)(2,1)S(1)}, bf16[1,720,128]{2,1,0:T(8,128)(2,1)S(1)}, u32[]{:S(2)}, u32[]{:S(2)}) %collective-permute-start.11) | collective-permute-done | bytes 184352 | tf_op jit(solution)/shard_map/ppermute | solution.py:76
  10.7 3.4 %collective-permute-start.13 = (bf16[2,720,128]{2,1,0:T(8,128)(2,1)S(1)}, bf16[2,720,128]{2,1,0:T(8,128)(2,1)S(1)}, u32[]{:S(2)}, u32[]{:S(2)}) collective-permute-start(bf16[2,720,128]{2,1,0:T(8,128)(2,1)S(1)} %pad_maximum_fusion.refs_0_), channel_id=1, source_target_pairs={{0,1},{1,0},{2,3},{3,2},{4,5},{5,4},{6,7},{7,6},{8,9},{9,8},{10,11... | collective-permute-start | bytes 1105928 | tf_op jit(solution)/shard_map/ppermute | solution.py:76
  14.3 0.9 %collective-permute-start.8 = (bf16[1,720,128]{2,1,0:T(8,128)(2,1)S(1)}, bf16[1,720,128]{2,1,0:T(8,128)(2,1)S(1)}, u32[]{:S(2)}, u32[]{:S(2)}) collective-permute-start(bf16[1,720,128]{2,1,0:T(8,128)(2,1)S(1)} %collective-permute-done.7), channel_id=1, source_target_pairs={{0,8},{1,17},{2,10},{3,19},{4,12},{5,21},{6,14},{7,23},{8,0},{9,25... | collective-permute-start | bytes 552968 | tf_op jit(solution)/shard_map/ppermute | solution.py:76
  15.3 5.1 %collective-permute-done.1 = bf16[1,720,128]{2,1,0:T(8,128)(2,1)S(1)} collective-permute-done((bf16[1,720,128]{2,1,0:T(8,128)(2,1)S(1)}, bf16[1,720,128]{2,1,0:T(8,128)(2,1)S(1)}, u32[]{:S(2)}, u32[]{:S(2)}) %collective-permute-start.1) | collective-permute-done | bytes 184352 | tf_op jit(solution)/shard_map/ppermute | solution.py:76
  21.5 0.9 %collective-permute-start.14 = (bf16[2,720,128]{2,1,0:T(8,128)(2,1)S(1)}, bf16[2,720,128]{2,1,0:T(8,128)(2,1)S(1)}, u32[]{:S(2)}, u32[]{:S(2)}) collective-permute-start(bf16[2,720,128]{2,1,0:T(8,128)(2,1)S(1)} %collective-permute-done.12.refs_1_), channel_id=1, source_target_pairs={{0,1},{1,0},{2,3},{3,2},{4,5},{5,4},{6,7},{7,6},{8,9},{9,8},{10,11... | collective-permute-start | bytes 1105928 | tf_op jit(solution)/shard_map/ppermute | solution.py:76
  23.4 1.2 %collective-permute-start.4 = (bf16[2,720,128]{2,1,0:T(8,128)(2,1)S(1)}, bf16[2,720,128]{2,1,0:T(8,128)(2,1)S(1)}, u32[]{:S(2)}, u32[]{:S(2)}) collective-permute-start(bf16[2,720,128]{2,1,0:T(8,128)(2,1)S(1)} %constant_dynamic-update-slice_fusion.refs_0_), channel_id=1, source_target_pairs={{0,16},{1,9},{2,18},{3,11},{4,20},{5,13},{6,22},{7,15},{8,24},{9,1... | collective-permute-start | bytes 1105928 | tf_op jit(solution)/shard_map/ppermute | solution.py:76
  24.9 1.0 %shard_map.128 = (bf16[11520,128]{1,0:T(8,128)(2,1)S(1)}, bf16[1152,1280]{1,0:T(8,128)(2,1)S(1)}) custom-call(s32[33]{0:T(128)S(1)} %concatenate.12.table, bf16[2,720,128]{2,1,0:T(8,128)(2,1)S(1)} %pad_maximum_fusion.refs_0_, bf16[2,720,128]{2,1,0:T(8,128)(2,1)S(1)} %collective-permute-done.12.refs_1_, ...), custom_call_target="tpu_custom_call" | custom-call | tf_op jit(solution)/shard_map/pallas_call | solution.py:318
  26.0 5.3 %collective-permute-done.9.refs_1_ = bf16[2,720,128]{2,1,0:T(8,128)(2,1)S(1)} collective-permute-done((bf16[2,720,128]{2,1,0:T(8,128)(2,1)S(1)}, bf16[2,720,128]{2,1,0:T(8,128)(2,1)S(1)}, u32[]{:S(2)}, u32[]{:S(2)}) %collective-permute-start.9) | collective-permute-done | bytes 368672 | tf_op jit(solution)/shard_map/ppermute | solution.py:76
  31.8 1.6 %collective-permute-start.5 = (bf16[2,720,128]{2,1,0:T(8,128)(2,1)S(1)}, bf16[2,720,128]{2,1,0:T(8,128)(2,1)S(1)}, u32[]{:S(2)}, u32[]{:S(2)}) collective-permute-start(bf16[2,720,128]{2,1,0:T(8,128)(2,1)S(1)} %constant_dynamic-update-slice_fusion.refs_0_), channel_id=1, source_target_pairs={{0,1},{1,0},{2,3},{3,2},{4,5},{5,4},{6,7},{7,6},{8,9},{9,8},{10,11... | collective-permute-start | bytes 1105928 | tf_op jit(solution)/shard_map/ppermute | solution.py:76
  33.5 1.0 %shard_map.129 = (bf16[11520,128]{1,0:T(8,128)(2,1)S(1)}, bf16[1152,1280]{1,0:T(8,128)(2,1)S(1)}) custom-call(s32[33]{0:T(128)S(1)} %concatenate.12.table, bf16[2,720,128]{2,1,0:T(8,128)(2,1)S(1)} %constant_dynamic-update-slice_fusion.2.refs_0_, ...), custom_call_target="tpu_custom_call", output_to_operand_aliasing={{0}: (5, {}), {1}: (6, {})} | custom-call | tf_op jit(solution)/shard_map/pallas_call | solution.py:318
  34.5 0.9 %collective-permute-done.4.refs_2_ = bf16[2,720,128]{2,1,0:T(8,128)(2,1)S(1)} collective-permute-done((bf16[2,720,128]{2,1,0:T(8,128)(2,1)S(1)}, bf16[2,720,128]{2,1,0:T(8,128)(2,1)S(1)}, u32[]{:S(2)}, u32[]{:S(2)}) %collective-permute-start.4) | collective-permute-done | bytes 368672 | tf_op jit(solution)/shard_map/ppermute | solution.py:76
  35.7 2.0 %collective-permute-done.3 = bf16[2,360,128]{2,1,0:T(8,128)(2,1)S(1)} collective-permute-done((bf16[2,360,128]{2,1,0:T(8,128)(2,1)S(1)}, bf16[2,360,128]{2,1,0:T(8,128)(2,1)S(1)}, u32[]{:S(2)}, u32[]{:S(2)}) %collective-permute-start.3) | collective-permute-done | bytes 184352 | tf_op jit(solution)/shard_map/ppermute | solution.py:76
  38.5 1.5 %shard_map.130 = (bf16[11520,128]{1,0:T(8,128)(2,1)S(1)}, bf16[1152,1280]{1,0:T(8,128)(2,1)S(1)}, bf16[512,1280]{1,0:T(8,128)(2,1)S(1)}, bf16[512,1280]{1,0:T(8,128)(2,1)S(1)}) custom-call(s32[33]{0:T(128)S(1)} %concatenate.12.table, ...), custom_call_target="tpu_custom_call", output_to_operand_aliasing={{0}: (7, {}), {1}: (8, {})} | custom-call | tf_op jit(solution)/shard_map/pallas_call | solution.py:318
  40.0 2.5 %shard_map.131 = (f32[1152,128]{1,0:T(8,128)S(1)}, bf16[11520,128]{1,0:T(8,128)(2,1)S(1)}, bf16[1152,1280]{1,0:T(8,128)(2,1)S(1)}) custom-call(s32[33]{0:T(128)S(1)} %concatenate.12.table, bf16[512,1280]{1,0:T(8,128)(2,1)S(1)} %get-tuple-element.36.x, ...), custom_call_target="tpu_custom_call", output_to_operand_aliasing={{1}: (6, {}), {2}: (7, {})} | custom-call | tf_op jit(solution)/shard_map/pallas_call | solution.py:391
  43.0 1.1 %collective-permute-done.20.refs_1_ = bf16[2,360,128]{2,1,0:T(8,128)(2,1)S(1)} collective-permute-done((bf16[2,360,128]{2,1,0:T(8,128)(2,1)S(1)}, bf16[2,360,128]{2,1,0:T(8,128)(2,1)S(1)}, u32[]{:S(2)}, u32[]{:S(2)}) %collective-permute-start.20) | collective-permute-done | bytes 184352 | tf_op jit(solution)/shard_map/ppermute | solution.py:76
  44.0 2.7 %shard_map.132 = (f32[1152,128]{1,0:T(8,128)S(1)}, bf16[2,2,72,128]{3,2,1,0:T(8,128)(2,1)S(1)}, bf16[2,2,72,128]{3,2,1,0:T(8,128)(2,1)S(1)}, bf16[1152,1280]{1,0:T(8,128)(2,1)S(1)}) custom-call(s32[33]{0:T(128)S(1)} %concatenate.12.table, bf16[512,1280]{1,0:T(8,128)(2,1)S(1)} %get-tuple-element.41.cot, ...), custom_call_target="tpu_custom_call", output_to_operand_aliasing={{3}: (5, {})} | custom-call | flops 1509949440 | bytes 2949120 | tf_op jit(solution)/shard_map/pallas_call | solution.py:431
  47.2 2.1 %collective-permute-start.22 = (bf16[2,2,72,128]{3,2,1,0:T(8,128)(2,1)S(1)}, bf16[2,2,72,128]{3,2,1,0:T(8,128)(2,1)S(1)}, u32[]{:S(2)}, u32[]{:S(2)}) collective-permute-start(bf16[2,2,72,128]{3,2,1,0:T(8,128)(2,1)S(1)} %get-tuple-element.46), channel_id=1, source_target_pairs={{1,2},{2,1},{3,4},{4,3},{5,6},{6,5},{9,10},{10,9},{11,12},{12,11},... | collective-permute-start | bytes 221192 | tf_op jit(solution)/shard_map/ppermute | solution.py:76
  49.4 3.6 %collective-permute-done.22.outer = bf16[2,2,72,128]{3,2,1,0:T(8,128)(2,1)S(1)} collective-permute-done((bf16[2,2,72,128]{3,2,1,0:T(8,128)(2,1)S(1)}, bf16[2,2,72,128]{3,2,1,0:T(8,128)(2,1)S(1)}, u32[]{:S(2)}, u32[]{:S(2)}) %collective-permute-start.22) | collective-permute-done | bytes 73760 | tf_op jit(solution)/shard_map/ppermute | solution.py:76
  54.0 3.3 %collective-permute-start.24 = (bf16[2,2,4,16,128]{4,3,2,1,0:T(8,128)(2,1)S(1)}, bf16[2,2,4,16,128]{4,3,2,1,0:T(8,128)(2,1)S(1)}, u32[]{:S(2)}, u32[]{:S(2)}) collective-permute-start(bf16[2,2,4,16,128]{4,3,2,1,0:T(8,128)(2,1)S(1)} %get-tuple-element.50), channel_id=1, source_target_pairs={{8,16},{16,8},{9,17},{17,9},{10,18},{18,10},{11,19},{19,11},{12,20... | collective-permute-start | bytes 196616 | tf_op jit(solution)/shard_map/ppermute | solution.py:647
  57.3 3.1 %shard_map.134.refs_7_ = bf16[4,128,1280]{2,1,0:T(8,128)(2,1)} custom-call(s32[3]{0:T(128)S(1)} %pad_add_fusion.place.refs_0_, bf16[11520,128]{1,0:T(8,128)(2,1)S(1)} %get-tuple-element.39.refs_1_, f32[1152,128]{1,0:T(8,128)S(1)} %get-tuple-element.47.refs_2_, f32[1152,128]{1,0:T(8,128)S(1)} %get-tuple-element.48.refs_3_, bf16[4,128,1280]{2,1,0:T(8,128)(2,1)S(1)} %bitcast.9), custom_call_target="tpu_custom_call" | custom-call | flops 1132462080 | bytes 2949120 | tf_op jit(solution)/shard_map/pallas_call | solution.py:620
  60.4 2.3 %shard_map.135 = bf16[4,128,1280]{2,1,0:T(8,128)(2,1)} custom-call(s32[3]{0:T(128)S(1)} %pad_add_fusion.place.refs_0_, bf16[11520,128]{1,0:T(8,128)(2,1)S(1)} %get-tuple-element.39.refs_1_, f32[1152,128]{1,0:T(8,128)S(1)} %get-tuple-element.47.refs_2_, f32[1152,128]{1,0:T(8,128)S(1)} %get-tuple-element.48.refs_3_, ...), custom_call_target="tpu_custom_call", output_to_operand_aliasing={{}: (7, {})} | custom-call | flops 377487360 | bytes 2949120 | tf_op jit(solution)/shard_map/pallas_call | solution.py:620
  (57 shorter events, 9.1 us)
Async XLA Ops:
  2.0 12.1 %collective-permute-start = (bf16[1,720,128]{2,1,0:T(8,128)(2,1)S(1)}, bf16[1,720,128]{2,1,0:T(8,128)(2,1)S(1)}, u32[]{:S(2)}, u32[]{:S(2)}) collective-permute-start(bf16[1,720,128]{2,1,0:T(8,128)(2,1)S(1)} %shard_map.127), channel_id=1, source_target_pairs={{0,4},{1,5},{2,6},{3,7},{4,0},{5,1},{6,2},{7,3},{8,12},{9,13},{10,... | collective-permute-start | bytes 552968 | tf_op jit(solution)/shard_map/ppermute | solution.py:76
  4.4 9.9 %collective-permute-start.7 = (bf16[1,720,128]{2,1,0:T(8,128)(2,1)S(1)}, bf16[1,720,128]{2,1,0:T(8,128)(2,1)S(1)}, u32[]{:S(2)}, u32[]{:S(2)}) collective-permute-start(bf16[1,720,128]{2,1,0:T(8,128)(2,1)S(1)} %shard_map.127), channel_id=1, source_target_pairs={{0,2},{1,3},{2,0},{3,1},{4,6},{5,7},{6,4},{7,5},{8,10},{9,11},{10,... | collective-permute-start | bytes 552968 | tf_op jit(solution)/shard_map/ppermute | solution.py:76
  5.7 4.7 %collective-permute-start.11 = (bf16[1,720,128]{2,1,0:T(8,128)(2,1)S(1)}, bf16[1,720,128]{2,1,0:T(8,128)(2,1)S(1)}, u32[]{:S(2)}, u32[]{:S(2)}) collective-permute-start(bf16[1,720,128]{2,1,0:T(8,128)(2,1)S(1)} %shard_map.127), channel_id=1, source_target_pairs={{0,8},{1,17},{2,10},{3,19},{4,12},{5,21},{6,14},{7,23},{8,0},{9,25... | collective-permute-start | bytes 552968 | tf_op jit(solution)/shard_map/ppermute | solution.py:76
  10.4 11.0 %collective-permute-start.12 = (bf16[2,720,128]{2,1,0:T(8,128)(2,1)S(1)}, bf16[2,720,128]{2,1,0:T(8,128)(2,1)S(1)}, u32[]{:S(2)}, u32[]{:S(2)}) collective-permute-start(bf16[2,720,128]{2,1,0:T(8,128)(2,1)S(1)} %pad_maximum_fusion.refs_0_), channel_id=1, source_target_pairs={{0,16},{1,9},{2,18},{3,11},{4,20},{5,13},{6,22},{7,15},{8,24},{9,1... | collective-permute-start | bytes 1105928 | tf_op jit(solution)/shard_map/ppermute | solution.py:76
  10.7 13.9 %collective-permute-start.13 = (bf16[2,720,128]{2,1,0:T(8,128)(2,1)S(1)}, bf16[2,720,128]{2,1,0:T(8,128)(2,1)S(1)}, u32[]{:S(2)}, u32[]{:S(2)}) collective-permute-start(bf16[2,720,128]{2,1,0:T(8,128)(2,1)S(1)} %pad_maximum_fusion.refs_0_), channel_id=1, source_target_pairs={{0,1},{1,0},{2,3},{3,2},{4,5},{5,4},{6,7},{7,6},{8,9},{9,8},{10,11... | collective-permute-start | bytes 1105928 | tf_op jit(solution)/shard_map/ppermute | solution.py:76
  14.1 6.3 %collective-permute-start.1 = (bf16[1,720,128]{2,1,0:T(8,128)(2,1)S(1)}, bf16[1,720,128]{2,1,0:T(8,128)(2,1)S(1)}, u32[]{:S(2)}, u32[]{:S(2)}) collective-permute-start(bf16[1,720,128]{2,1,0:T(8,128)(2,1)S(1)} %collective-permute-done), channel_id=1, source_target_pairs={{0,2},{1,3},{2,0},{3,1},{4,6},{5,7},{6,4},{7,5},{8,10},{9,11},{10,... | collective-permute-start | bytes 552968 | tf_op jit(solution)/shard_map/ppermute | solution.py:76
  14.3 6.8 %collective-permute-start.8 = (bf16[1,720,128]{2,1,0:T(8,128)(2,1)S(1)}, bf16[1,720,128]{2,1,0:T(8,128)(2,1)S(1)}, u32[]{:S(2)}, u32[]{:S(2)}) collective-permute-start(bf16[1,720,128]{2,1,0:T(8,128)(2,1)S(1)} %collective-permute-done.7), channel_id=1, source_target_pairs={{0,8},{1,17},{2,10},{3,19},{4,12},{5,21},{6,14},{7,23},{8,0},{9,25... | collective-permute-start | bytes 552968 | tf_op jit(solution)/shard_map/ppermute | solution.py:76
  20.4 11.1 %collective-permute-start.2 = (bf16[2,720,128]{2,1,0:T(8,128)(2,1)S(1)}, bf16[2,720,128]{2,1,0:T(8,128)(2,1)S(1)}, u32[]{:S(2)}, u32[]{:S(2)}) collective-permute-start(bf16[2,720,128]{2,1,0:T(8,128)(2,1)S(1)} %constant_dynamic-update-slice_fusion.refs_0_), channel_id=1, source_target_pairs={{0,8},{1,17},{2,10},{3,19},{4,12},{5,21},{6,14},{7,23},{8,0},{9,25... | collective-permute-start | bytes 1105928 | tf_op jit(solution)/shard_map/ppermute | solution.py:76
  21.1 10.2 %collective-permute-start.9 = (bf16[2,720,128]{2,1,0:T(8,128)(2,1)S(1)}, bf16[2,720,128]{2,1,0:T(8,128)(2,1)S(1)}, u32[]{:S(2)}, u32[]{:S(2)}) collective-permute-start(bf16[2,720,128]{2,1,0:T(8,128)(2,1)S(1)} %constant_dynamic-update-slice_fusion.2.refs_0_), channel_id=1, source_target_pairs={{0,16},{1,9},{2,18},{3,11},{4,20},{5,13},{6,22},{7,15},{8,24},{9,1... | collective-permute-start | bytes 1105928 | tf_op jit(solution)/shard_map/ppermute | solution.py:76
  21.5 3.4 %collective-permute-start.14 = (bf16[2,720,128]{2,1,0:T(8,128)(2,1)S(1)}, bf16[2,720,128]{2,1,0:T(8,128)(2,1)S(1)}, u32[]{:S(2)}, u32[]{:S(2)}) collective-permute-start(bf16[2,720,128]{2,1,0:T(8,128)(2,1)S(1)} %collective-permute-done.12.refs_1_), channel_id=1, source_target_pairs={{0,1},{1,0},{2,3},{3,2},{4,5},{5,4},{6,7},{7,6},{8,9},{9,8},{10,11... | collective-permute-start | bytes 1105928 | tf_op jit(solution)/shard_map/ppermute | solution.py:76
  23.4 12.1 %collective-permute-start.4 = (bf16[2,720,128]{2,1,0:T(8,128)(2,1)S(1)}, bf16[2,720,128]{2,1,0:T(8,128)(2,1)S(1)}, u32[]{:S(2)}, u32[]{:S(2)}) collective-permute-start(bf16[2,720,128]{2,1,0:T(8,128)(2,1)S(1)} %constant_dynamic-update-slice_fusion.refs_0_), channel_id=1, source_target_pairs={{0,16},{1,9},{2,18},{3,11},{4,20},{5,13},{6,22},{7,15},{8,24},{9,1... | collective-permute-start | bytes 1105928 | tf_op jit(solution)/shard_map/ppermute | solution.py:76
  24.6 8.8 %collective-permute-start.10 = (bf16[2,720,128]{2,1,0:T(8,128)(2,1)S(1)}, bf16[2,720,128]{2,1,0:T(8,128)(2,1)S(1)}, u32[]{:S(2)}, u32[]{:S(2)}) collective-permute-start(bf16[2,720,128]{2,1,0:T(8,128)(2,1)S(1)} %constant_dynamic-update-slice_fusion.2.refs_0_), channel_id=1, source_target_pairs={{0,1},{1,0},{2,3},{3,2},{4,5},{5,4},{6,7},{7,6},{8,9},{9,8},{10,11... | collective-permute-start | bytes 1105928 | tf_op jit(solution)/shard_map/ppermute | solution.py:76
  31.3 2.1 %collective-permute-start.15 = (bf16[2,720,128]{2,1,0:T(8,128)(2,1)S(1)}, bf16[2,720,128]{2,1,0:T(8,128)(2,1)S(1)}, u32[]{:S(2)}, u32[]{:S(2)}) collective-permute-start(bf16[2,720,128]{2,1,0:T(8,128)(2,1)S(1)} %collective-permute-done.9.refs_1_), channel_id=1, source_target_pairs={{0,1},{1,0},{2,3},{3,2},{4,5},{5,4},{6,7},{7,6},{8,9},{9,8},{10,11... | collective-permute-start | bytes 1105928 | tf_op jit(solution)/shard_map/ppermute | solution.py:76
  31.5 6.2 %collective-permute-start.3 = (bf16[2,360,128]{2,1,0:T(8,128)(2,1)S(1)}, bf16[2,360,128]{2,1,0:T(8,128)(2,1)S(1)}, u32[]{:S(2)}, u32[]{:S(2)}) collective-permute-start(bf16[2,360,128]{2,1,0:T(8,128)(2,1)S(1)} %get-tuple-element.52), channel_id=1, source_target_pairs={{0,16},{1,9},{2,18},{3,11},{4,20},{5,13},{6,22},{7,15},{8,24},{9,1... | collective-permute-start | bytes 552968 | tf_op jit(solution)/shard_map/ppermute | solution.py:76
  31.8 6.5 %collective-permute-start.5 = (bf16[2,720,128]{2,1,0:T(8,128)(2,1)S(1)}, bf16[2,720,128]{2,1,0:T(8,128)(2,1)S(1)}, u32[]{:S(2)}, u32[]{:S(2)}) collective-permute-start(bf16[2,720,128]{2,1,0:T(8,128)(2,1)S(1)} %constant_dynamic-update-slice_fusion.refs_0_), channel_id=1, source_target_pairs={{0,1},{1,0},{2,3},{3,2},{4,5},{5,4},{6,7},{7,6},{8,9},{9,8},{10,11... | collective-permute-start | bytes 1105928 | tf_op jit(solution)/shard_map/ppermute | solution.py:76
  33.4 5.0 %collective-permute-start.6 = (bf16[2,720,128]{2,1,0:T(8,128)(2,1)S(1)}, bf16[2,720,128]{2,1,0:T(8,128)(2,1)S(1)}, u32[]{:S(2)}, u32[]{:S(2)}) collective-permute-start(bf16[2,720,128]{2,1,0:T(8,128)(2,1)S(1)} %collective-permute-done.2.refs_1_), channel_id=1, source_target_pairs={{0,1},{1,0},{2,3},{3,2},{4,5},{5,4},{6,7},{7,6},{8,9},{9,8},{10,11... | collective-permute-start | bytes 1105928 | tf_op jit(solution)/shard_map/ppermute | solution.py:76
  35.4 3.0 %collective-permute-start.16 = (bf16[2,720,128]{2,1,0:T(8,128)(2,1)S(1)}, bf16[2,720,128]{2,1,0:T(8,128)(2,1)S(1)}, u32[]{:S(2)}, u32[]{:S(2)}) collective-permute-start(bf16[2,720,128]{2,1,0:T(8,128)(2,1)S(1)} %collective-permute-done.4.refs_2_), channel_id=1, source_target_pairs={{0,1},{1,0},{2,3},{3,2},{4,5},{5,4},{6,7},{7,6},{8,9},{9,8},{10,11... | collective-permute-start | bytes 1105928 | tf_op jit(solution)/shard_map/ppermute | solution.py:76
  35.4 7.0 %collective-permute-start.19 = (bf16[2,360,128]{2,1,0:T(8,128)(2,1)S(1)}, bf16[2,360,128]{2,1,0:T(8,128)(2,1)S(1)}, u32[]{:S(2)}, u32[]{:S(2)}) collective-permute-start(bf16[2,360,128]{2,1,0:T(8,128)(2,1)S(1)} %get-tuple-element.51), channel_id=1, source_target_pairs={{0,16},{1,9},{2,18},{3,11},{4,20},{5,13},{6,22},{7,15},{8,24},{9,1... | collective-permute-start | bytes 552968 | tf_op jit(solution)/shard_map/ppermute | solution.py:76
  37.7 2.2 %collective-permute-start.17 = (bf16[1,360,128]{2,1,0:T(8,128)(2,1)S(1)}, bf16[1,360,128]{2,1,0:T(8,128)(2,1)S(1)}, u32[]{:S(2)}, u32[]{:S(2)}) collective-permute-start(bf16[1,360,128]{2,1,0:T(8,128)(2,1)S(1)} %get-tuple-element.54.refs_0_), channel_id=1, source_target_pairs={{0,1},{1,0},{2,3},{3,2},{4,5},{5,4},{6,7},{7,6},{8,9},{9,8},{10,11... | collective-permute-start | bytes 276488 | tf_op jit(solution)/shard_map/ppermute | solution.py:76
  38.4 1.6 %collective-permute-start.18 = (bf16[1,360,128]{2,1,0:T(8,128)(2,1)S(1)}, bf16[1,360,128]{2,1,0:T(8,128)(2,1)S(1)}, u32[]{:S(2)}, u32[]{:S(2)}) collective-permute-start(bf16[1,360,128]{2,1,0:T(8,128)(2,1)S(1)} %get-tuple-element.53.refs_2_), channel_id=1, source_target_pairs={{0,1},{1,0},{2,3},{3,2},{4,5},{5,4},{6,7},{7,6},{8,9},{9,8},{10,11... | collective-permute-start | bytes 276488 | tf_op jit(solution)/shard_map/ppermute | solution.py:76
  46.7 2.7 %collective-permute-start.21 = (bf16[2,2,72,128]{3,2,1,0:T(8,128)(2,1)S(1)}, bf16[2,2,72,128]{3,2,1,0:T(8,128)(2,1)S(1)}, u32[]{:S(2)}, u32[]{:S(2)}) collective-permute-start(bf16[2,2,72,128]{3,2,1,0:T(8,128)(2,1)S(1)} %get-tuple-element.45), channel_id=1, source_target_pairs={{0,1},{1,0},{2,3},{3,2},{4,5},{5,4},{6,7},{7,6},{8,9},{9,8},{10,11... | collective-permute-start | bytes 221192 | tf_op jit(solution)/shard_map/ppermute | solution.py:76
  47.2 5.9 %collective-permute-start.22 = (bf16[2,2,72,128]{3,2,1,0:T(8,128)(2,1)S(1)}, bf16[2,2,72,128]{3,2,1,0:T(8,128)(2,1)S(1)}, u32[]{:S(2)}, u32[]{:S(2)}) collective-permute-start(bf16[2,2,72,128]{3,2,1,0:T(8,128)(2,1)S(1)} %get-tuple-element.46), channel_id=1, source_target_pairs={{1,2},{2,1},{3,4},{4,3},{5,6},{6,5},{9,10},{10,9},{11,12},{12,11},... | collective-permute-start | bytes 221192 | tf_op jit(solution)/shard_map/ppermute | solution.py:76
  53.7 6.7 %collective-permute-start.23 = (bf16[2,2,4,16,128]{4,3,2,1,0:T(8,128)(2,1)S(1)}, bf16[2,2,4,16,128]{4,3,2,1,0:T(8,128)(2,1)S(1)}, u32[]{:S(2)}, u32[]{:S(2)}) collective-permute-start(bf16[2,2,4,16,128]{4,3,2,1,0:T(8,128)(2,1)S(1)} %get-tuple-element.49), channel_id=1, source_target_pairs={{0,8},{8,0},{16,24},{24,16},{1,9},{9,1},{17,25},{25,17},{2,10},{10... | collective-permute-start | bytes 196616 | tf_op jit(solution)/shard_map/ppermute | solution.py:647
  54.0 6.4 %collective-permute-start.24 = (bf16[2,2,4,16,128]{4,3,2,1,0:T(8,128)(2,1)S(1)}, bf16[2,2,4,16,128]{4,3,2,1,0:T(8,128)(2,1)S(1)}, u32[]{:S(2)}, u32[]{:S(2)}) collective-permute-start(bf16[2,2,4,16,128]{4,3,2,1,0:T(8,128)(2,1)S(1)} %get-tuple-element.50), channel_id=1, source_target_pairs={{8,16},{16,8},{9,17},{17,9},{10,18},{18,10},{11,19},{19,11},{12,20... | collective-permute-start | bytes 196616 | tf_op jit(solution)/shard_map/ppermute | solution.py:647
  (5 other events, 13.3 us)
